TPU v7x, 32 devices: a whole 2x2x4 slice. The times are simulated.
32 devices in a mesh: grp: 2 (over core), exp: 4 (over y, x), shd: 4 (over z).
Axes of the slice: x: 2, y: 2, z: 4, core: 2. Of those that a mesh axis runs over, the one named last changes fastest.
Arguments:
- tokens_in: bfloat16 [32, 1024, 768], P(('grp', 'exp', 'shd')), may hold values from -6 to 6
- cotangent: bfloat16 [32, 1024, 768], P(('grp', 'exp', 'shd')), may hold values from -6 to 6
- block_ids: int32 [32, 1024], P(('grp', 'exp', 'shd')), may hold values from 0 to 7, never falling along the last dimension, each value on 1 to 256 neighbouring positions
- expert_ids: int32 [32, 1024, 2], P(('grp', 'exp', 'shd')), may hold values from 0 to 3, all different within a row; in each aligned block of 1024 rows (0 to 1023, 1024 to 2047, ..., all dimensions but the last counted through in order) at most 640 rows name the same one
- scales: float32 [2, 768], P(None, ('exp', 'shd')), may hold values from 0.5 to 1.5
- moment_scales: float32 [2, 768], P(None, ('exp', 'shd')), may hold values from -128 to 128
- square_scales: float32 [2, 768], P(None, ('exp', 'shd')), may hold values from 1736.704 to 6881.28
- attend: float32 [3, 768, 768], P(None, ('exp', 'shd')), may hold values from -0.21875 to 0.21875
- moment_attend: float32 [3, 768, 768], P(None, ('exp', 'shd')), may hold values from -64 to 64
- square_attend: float32 [3, 768, 768], P(None, ('exp', 'shd')), may hold values from 425.984 to 1736.704
- output: float32 [768, 768], P(('exp', 'shd')), may hold values from -1.75 to 1.75
- moment_output: float32 [768, 768], P(('exp', 'shd')), may hold values from -7 to 7
- square_output: float32 [768, 768], P(('exp', 'shd')), may hold values from 6.22592 to 24.90368
- router: float32 [768, 4], P(('exp', 'shd')), may hold values from -0.21875 to 0.21875
- moment_router: float32 [768, 4], P(('exp', 'shd')), may hold values from -320 to 320
- square_router: float32 [768, 4], P(('exp', 'shd')), may hold values from 13337.887 to 52848.23
- widener: float32 [2, 768, 2048], P(None, ('exp', 'shd')), may hold values from -0.21875 to 0.21875
- moment_widener: float32 [2, 768, 2048], P(None, ('exp', 'shd')), may hold values from -64 to 64
- square_widener: float32 [2, 768, 2048], P(None, ('exp', 'shd')), may hold values from 425.984 to 1736.704
- reducer: float32 [2048, 768], P(('exp', 'shd')), may hold values from -0.125 to 0.125
- moment_reducer: float32 [2048, 768], P(('exp', 'shd')), may hold values from -64 to 64
- square_reducer: float32 [2048, 768], P(('exp', 'shd')), may hold values from 425.984 to 1736.704
- experts: float32 [4, 2, 768, 2048], P('exp', None, 'shd'), may hold values from -0.21875 to 0.21875
- moment_experts: float32 [4, 2, 768, 2048], P('exp', None, 'shd'), may hold values from -24 to 24
- square_experts: float32 [4, 2, 768, 2048], P('exp', None, 'shd'), may hold values from 68.8128 to 278.528
- narrower: float32 [4, 2048, 768], P('exp', 'shd'), may hold values from -0.125 to 0.125
- moment_narrower: float32 [4, 2048, 768], P('exp', 'shd'), may hold values from -16 to 16
- square_narrower: float32 [4, 2048, 768], P('exp', 'shd'), may hold values from 39.3216 to 157.2864
Outputs:
- block_out: bfloat16 [32, 1024, 768], P(('grp', 'exp', 'shd'))
- input_grad: float32 [32, 1024, 768], P(('grp', 'exp', 'shd'))
- weight_scales: float32 [2, 768], P(None, ('exp', 'shd'))
- first_scales: float32 [2, 768], P(None, ('exp', 'shd'))
- second_scales: float32 [2, 768], P(None, ('exp', 'shd'))
- weight_attend: float32 [3, 768, 768], P(None, ('exp', 'shd'))
- first_attend: float32 [3, 768, 768], P(None, ('exp', 'shd'))
- second_attend: float32 [3, 768, 768], P(None, ('exp', 'shd'))
- weight_output: float32 [768, 768], P(('exp', 'shd'))
- first_output: float32 [768, 768], P(('exp', 'shd'))
- second_output: float32 [768, 768], P(('exp', 'shd'))
- weight_router: float32 [768, 4], P(('exp', 'shd'))
- first_router: float32 [768, 4], P(('exp', 'shd'))
- second_router: float32 [768, 4], P(('exp', 'shd'))
- weight_widener: float32 [2, 768, 2048], P(None, ('exp', 'shd'))
- first_widener: float32 [2, 768, 2048], P(None, ('exp', 'shd'))
- second_widener: float32 [2, 768, 2048], P(None, ('exp', 'shd'))
- weight_reducer: float32 [2048, 768], P(('exp', 'shd'))
- first_reducer: float32 [2048, 768], P(('exp', 'shd'))
- second_reducer: float32 [2048, 768], P(('exp', 'shd'))
- weight_experts: float32 [4, 2, 768, 2048], P('exp', None, 'shd')
- first_experts: float32 [4, 2, 768, 2048], P('exp', None, 'shd')
- second_experts: float32 [4, 2, 768, 2048], P('exp', None, 'shd')
- weight_narrower: float32 [4, 2048, 768], P('exp', 'shd')
- first_narrower: float32 [4, 2048, 768], P('exp', 'shd')
- second_narrower: float32 [4, 2048, 768], P('exp', 'shd')
Inputs may be any that keep to these rules, and one draw needn't show every extreme that they name: `expert_ids`: each token names 2 different experts; of the 1024 tokens of one sequence no expert is named by more than 640, a bound that some block reaches. `block_ids`: never falls along a sequence; each block holds 1 to 256 tokens.
All inputs are finite; a program needn't handle non-finite values.
Results may differ from a plain program's by a relative error of at most 0.014.
The roundings to bfloat16 on the way count: a program that leaves them out, or rounds other values in their place, can miss the bound.
Values may be sent and summed in bfloat16 or wider, within the bound.
A program may use at most 768 MiB of HBM per device.

v0:
```python
import jax
import jax.numpy as jnp
from jax import lax
from jax.sharding import PartitionSpec as P

HEADS = 12
TOP = 2
CAP = 576


norm_eps = 1e-06
adam_eps = 1e-08
beta_one = 0.9
beta_two = 0.95
first_fix = 1.0 - 0.9**10
second_fix = 1.0 - 0.95**10
learning_rates = (0.3, 0.02, 0.15, 0.02, 0.02, 0.012, 0.02, 0.012)
decay_rates = (0.0, 0.1, 0.1, 0.1, 0.1, 0.1, 0.1, 0.1)
masked_score = -1e30


def silu_parts(values):
    logistic = jax.nn.sigmoid(values)
    return (values * logistic, logistic * (1.0 + values * (1.0 - logistic)))


def product(matrix_one, matrix_two):
    return jnp.dot(matrix_one, matrix_two, preferred_element_type=jnp.float32)


def across_rows(matrix_one, matrix_two):
    return lax.dot_general(
        matrix_one, matrix_two, (((0,), (0,)), ((), ())), preferred_element_type=jnp.float32
    )


def against_rows(matrix_one, matrix_two):
    return lax.dot_general(
        matrix_one, matrix_two, (((1,), (1,)), ((), ())), preferred_element_type=jnp.float32
    )


def rms_scale(values):
    return lax.rsqrt(jnp.mean(values * values, axis=1, keepdims=True) + norm_eps)


def norm_back(incoming, normed, factor, gain_row):
    scaled = incoming * gain_row
    return factor * (scaled - normed * jnp.mean(scaled * normed, axis=1, keepdims=True))


def adam_update(weight, moment, square, gradient, step_rate, shrink_rate):
    moment_next = beta_one * moment + (1.0 - beta_one) * gradient
    square_next = beta_two * square + (1.0 - beta_two) * gradient * gradient
    direction = moment_next / first_fix / (jnp.sqrt(square_next / second_fix) + adam_eps)
    return (weight - step_rate * (direction + shrink_rate * weight), moment_next, square_next)


def slot_tables(choices, experts_all, capacity):
    pair_count = choices.shape[0] * choices.shape[1]
    pair_expert = choices.reshape(pair_count)
    pair_hot = (pair_expert[:, None] == jnp.arange(experts_all, dtype=jnp.int32)[None, :]).astype(
        jnp.int32
    )
    before = jnp.cumsum(pair_hot, axis=0) - pair_hot
    placed = jnp.sum(before * pair_hot, axis=1)
    slot_id = jnp.where(placed < capacity, pair_expert * capacity + placed, experts_all * capacity)
    slot_pair = jnp.full((experts_all * capacity + 1,), pair_count, jnp.int32)
    slot_pair = slot_pair.at[slot_id].set(jnp.arange(pair_count, dtype=jnp.int32))
    return (slot_id, slot_pair[: experts_all * capacity])


def block_scores(queries, keys_all, block_ids, position, per_seq, query_rows):
    sequence = position // per_seq
    row_start = position % per_seq * query_rows
    query_part = lax.dynamic_slice_in_dim(queries[sequence], row_start, query_rows, 0)
    block_row = block_ids[sequence]
    block_part = lax.dynamic_slice_in_dim(block_row, row_start, query_rows, 0)
    scores = jnp.einsum(
        "qhe,khe->hqk", query_part, keys_all[sequence], preferred_element_type=jnp.float32
    ) * queries.shape[3] ** (-0.5)
    allowed = block_row[None, :] <= block_part[:, None]
    return (sequence, row_start, query_part, jnp.where(allowed[None], scores, masked_score))


def attention_forward(queries, keys_all, values_all, block_ids, query_rows):
    seq_count, seq_len = block_ids.shape
    per_seq = seq_len // query_rows

    def one_block(position):
        sequence, row_start, query_part, masked = block_scores(
            queries, keys_all, block_ids, position, per_seq, query_rows
        )
        largest = jnp.max(masked, axis=2, keepdims=True)
        exponent = jnp.exp(masked - largest)
        totals = jnp.sum(exponent, axis=2, keepdims=True)
        weights = (exponent / totals).astype(jnp.bfloat16)
        attended = jnp.einsum(
            "hqk,khe->qhe", weights, values_all[sequence], preferred_element_type=jnp.float32
        )
        return (attended.astype(jnp.bfloat16), largest + jnp.log(totals))

    attended, log_totals = lax.map(one_block, jnp.arange(seq_count * per_seq, dtype=jnp.int32))
    return (attended.reshape(seq_count, seq_len, queries.shape[2], queries.shape[3]), log_totals)


def attention_backward(queries, keys_all, values_all, block_ids, log_totals, out_grad, query_rows):
    seq_count, seq_len = block_ids.shape
    per_seq = seq_len // query_rows
    score_scale = queries.shape[3] ** (-0.5)

    def one_block(position):
        sequence, row_start, query_part, masked = block_scores(
            queries, keys_all, block_ids, position, per_seq, query_rows
        )
        probs = jnp.exp(masked - log_totals[position])
        weights = probs.astype(jnp.bfloat16)
        grad_part = lax.dynamic_slice_in_dim(out_grad[sequence], row_start, query_rows, 0)
        value_grad = jnp.einsum(
            "hqk,qhe->khe", weights, grad_part, preferred_element_type=jnp.float32
        )
        prob_grad = jnp.einsum(
            "qhe,khe->hqk", grad_part, values_all[sequence], preferred_element_type=jnp.float32
        )
        score_grad = (
            probs * (prob_grad - jnp.sum(prob_grad * probs, axis=2, keepdims=True))
        ).astype(jnp.bfloat16)
        query_grad = (
            jnp.einsum(
                "hqk,khe->qhe", score_grad, keys_all[sequence], preferred_element_type=jnp.float32
            )
            * score_scale
        )
        key_grad = (
            jnp.einsum("hqk,qhe->khe", score_grad, query_part, preferred_element_type=jnp.float32)
            * score_scale
        )
        return (query_grad, key_grad, value_grad)

    query_grad, key_grad, value_grad = lax.map(
        one_block, jnp.arange(seq_count * per_seq, dtype=jnp.int32)
    )
    heads_count, head_size = (queries.shape[2], queries.shape[3])
    query_grad = query_grad.reshape(seq_count, seq_len, heads_count, head_size)
    key_grad = jnp.sum(
        key_grad.reshape(seq_count, per_seq, seq_len, heads_count, head_size), axis=1
    )
    value_grad = jnp.sum(
        value_grad.reshape(seq_count, per_seq, seq_len, heads_count, head_size), axis=1
    )
    return (query_grad, key_grad, value_grad)


def on_device(
    tokens_in,
    cotangent,
    block_ids,
    expert_ids,
    scales,
    moment_scales,
    square_scales,
    attend,
    moment_attend,
    square_attend,
    output,
    moment_output,
    square_output,
    router,
    moment_router,
    square_router,
    widener,
    moment_widener,
    square_widener,
    reducer,
    moment_reducer,
    square_reducer,
    experts,
    moment_experts,
    square_experts,
    narrower,
    moment_narrower,
    square_narrower,
):
    wide_scales, wide_attend, wide_output, wide_router, wide_widener, wide_reducer = (
        lax.all_gather(scales.astype(jnp.bfloat16), ("exp", "shd"), axis=1, tiled=True),
        lax.all_gather(attend.astype(jnp.bfloat16), ("exp", "shd"), axis=1, tiled=True),
        lax.all_gather(output.astype(jnp.bfloat16), ("exp", "shd"), axis=0, tiled=True),
        lax.all_gather(router.astype(jnp.bfloat16), ("exp", "shd"), axis=0, tiled=True),
        lax.all_gather(widener.astype(jnp.bfloat16), ("exp", "shd"), axis=1, tiled=True),
        lax.all_gather(reducer.astype(jnp.bfloat16), ("exp", "shd"), axis=0, tiled=True),
    )
    expand_full, narrow_full = (
        lax.all_gather(experts.astype(jnp.bfloat16), "shd", axis=2, tiled=True),
        lax.all_gather(narrower.astype(jnp.bfloat16), "shd", axis=1, tiled=True),
    )
    seq_count, seq_len, width = tokens_in.shape
    token_count = seq_count * seq_len
    head_size = width // HEADS
    query_rows = min(512, seq_len)
    experts_all = wide_router.shape[1]
    exp_local = experts.shape[0]
    exp_devices = lax.axis_size("exp")
    capacity = CAP
    inputs = tokens_in.reshape(token_count, width).astype(jnp.float32)
    first = rms_scale(inputs)
    normed = inputs * first
    gain_one = wide_scales[0].astype(jnp.float32)
    gain_two = wide_scales[1].astype(jnp.float32)
    lifted = (normed * gain_one).astype(jnp.bfloat16)
    projected = jnp.einsum(
        "nd,tdf->tnf", lifted, wide_attend, preferred_element_type=jnp.float32
    ).astype(jnp.bfloat16)
    shaped = projected.reshape(3, seq_count, seq_len, HEADS, head_size)
    attended, log_totals = attention_forward(shaped[0], shaped[1], shaped[2], block_ids, query_rows)
    attended_rows = attended.reshape(token_count, width)
    middle = inputs + product(attended_rows, wide_output)
    second = rms_scale(middle)
    normed_two = middle * second
    lifted_two = (normed_two * gain_two).astype(jnp.bfloat16)
    router_probs = jax.nn.softmax(product(lifted_two, wide_router), axis=1)
    choices = expert_ids.reshape(token_count, TOP)
    picks = (choices[:, :, None] == jnp.arange(experts_all, dtype=jnp.int32)[None, None, :]).astype(
        jnp.float32
    )
    chosen = jnp.sum(router_probs[:, None, :] * picks, axis=2)
    slot_id, slot_pair = slot_tables(choices, experts_all, capacity)
    zero_row = jnp.zeros((1, width), jnp.bfloat16)
    padded = jnp.concatenate([lifted_two, zero_row], axis=0)
    slot_rows = padded[slot_pair // TOP].reshape(exp_devices, exp_local, capacity, width)
    received = lax.all_to_all(slot_rows, "exp", split_axis=0, concat_axis=0, tiled=True)
    paired = jnp.einsum(
        "sjcd,jgdf->gsjcf", received, expand_full, preferred_element_type=jnp.float32
    )
    active, slope = silu_parts(paired[0])
    hidden = (active * paired[1]).astype(jnp.bfloat16)
    produced = jnp.einsum(
        "sjcf,jfd->sjcd", hidden, narrow_full, preferred_element_type=jnp.float32
    ).astype(jnp.bfloat16)
    returned = lax.all_to_all(produced, "exp", split_axis=0, concat_axis=0, tiled=True).reshape(
        experts_all * capacity, width
    )
    pair_out = (
        jnp.concatenate([returned, zero_row], axis=0)[slot_id]
        .reshape(token_count, TOP, width)
        .astype(jnp.float32)
    )
    mixture = jnp.sum(chosen[:, :, None] * pair_out, axis=1)
    shared_pair = jnp.einsum(
        "nd,gdf->gnf", lifted_two, wide_widener, preferred_element_type=jnp.float32
    )
    shared_active, shared_slope = silu_parts(shared_pair[0])
    shared_hidden = (shared_active * shared_pair[1]).astype(jnp.bfloat16)
    shared_out = product(shared_hidden, wide_reducer)
    block_out = (middle + shared_out + mixture).astype(jnp.bfloat16).reshape(tokens_in.shape)
    incoming = cotangent.reshape(token_count, width).astype(jnp.float32)
    incoming_low = incoming.astype(jnp.bfloat16)
    pair_grad = (
        (chosen[:, :, None] * incoming[:, None, :])
        .astype(jnp.bfloat16)
        .reshape(token_count * TOP, width)
    )
    slot_grad = jnp.concatenate([pair_grad, zero_row], axis=0)[slot_pair].reshape(
        exp_devices, exp_local, capacity, width
    )
    chosen_grad = jnp.sum(pair_out * incoming[:, None, :], axis=2)
    back_rows = lax.all_to_all(slot_grad, "exp", split_axis=0, concat_axis=0, tiled=True)
    hidden_grad = jnp.einsum(
        "sjcd,jfd->sjcf", back_rows, narrow_full, preferred_element_type=jnp.float32
    )
    narrow_grad = jnp.einsum(
        "sjcf,sjcd->jfd", hidden, back_rows, preferred_element_type=jnp.float32
    )
    stacked = jnp.stack(
        [
            (hidden_grad * paired[1] * slope).astype(jnp.bfloat16),
            (hidden_grad * active).astype(jnp.bfloat16),
        ]
    )
    expand_grad = jnp.einsum(
        "sjcd,gsjcf->jgdf", received, stacked, preferred_element_type=jnp.float32
    )
    row_grad = jnp.einsum(
        "gsjcf,jgdf->sjcd", stacked, expand_full, preferred_element_type=jnp.float32
    ).astype(jnp.bfloat16)
    returned_grad = lax.all_to_all(
        row_grad, "exp", split_axis=0, concat_axis=0, tiled=True
    ).reshape(experts_all * capacity, width)
    pair_input = jnp.concatenate([returned_grad, zero_row], axis=0)[slot_id].reshape(
        token_count, TOP, width
    )
    mixture_input = jnp.sum(pair_input.astype(jnp.float32), axis=1)
    probs_grad = jnp.sum(chosen_grad[:, :, None] * picks, axis=1)
    logit_grad = (
        router_probs * (probs_grad - jnp.sum(probs_grad * router_probs, axis=1, keepdims=True))
    ).astype(jnp.bfloat16)
    router_grad = across_rows(lifted_two, logit_grad)
    router_input = against_rows(logit_grad, wide_router)
    reducer_grad = across_rows(shared_hidden, incoming_low)
    shared_hgrad = against_rows(incoming_low, wide_reducer)
    shared_stack = jnp.stack(
        [
            (shared_hgrad * shared_pair[1] * shared_slope).astype(jnp.bfloat16),
            (shared_hgrad * shared_active).astype(jnp.bfloat16),
        ]
    )
    widener_grad = jnp.einsum(
        "nd,gnf->gdf", lifted_two, shared_stack, preferred_element_type=jnp.float32
    )
    shared_input = jnp.einsum(
        "gnf,gdf->nd", shared_stack, wide_widener, preferred_element_type=jnp.float32
    )
    lifted_two_grad = mixture_input + router_input + shared_input
    gain_two_grad = jnp.sum(lifted_two_grad * normed_two, axis=0)
    middle_grad = incoming + norm_back(lifted_two_grad, normed_two, second, gain_two)
    middle_low = middle_grad.astype(jnp.bfloat16)
    output_grad = across_rows(attended_rows, middle_low)
    attended_grad = (
        against_rows(middle_low, wide_output)
        .astype(jnp.bfloat16)
        .reshape(seq_count, seq_len, HEADS, head_size)
    )
    query_grad, key_grad, value_grad = attention_backward(
        shaped[0], shaped[1], shaped[2], block_ids, log_totals, attended_grad, query_rows
    )
    projected_grad = (
        jnp.stack([query_grad, key_grad, value_grad])
        .astype(jnp.bfloat16)
        .reshape(3, token_count, width)
    )
    attend_grad = jnp.einsum(
        "nd,tnf->tdf", lifted, projected_grad, preferred_element_type=jnp.float32
    )
    lifted_grad = jnp.einsum(
        "tnf,tdf->nd", projected_grad, wide_attend, preferred_element_type=jnp.float32
    )
    gain_one_grad = jnp.sum(lifted_grad * normed, axis=0)
    input_grad = middle_grad + norm_back(lifted_grad, normed, first, gain_one)
    scales_grad = jnp.stack([gain_one_grad, gain_two_grad])
    dense_sum = (
        lax.psum_scatter(scales_grad, ("exp", "shd"), scatter_dimension=1, tiled=True),
        lax.psum_scatter(attend_grad, ("exp", "shd"), scatter_dimension=1, tiled=True),
        lax.psum_scatter(output_grad, ("exp", "shd"), scatter_dimension=0, tiled=True),
        lax.psum_scatter(router_grad, ("exp", "shd"), scatter_dimension=0, tiled=True),
        lax.psum_scatter(widener_grad, ("exp", "shd"), scatter_dimension=1, tiled=True),
        lax.psum_scatter(reducer_grad, ("exp", "shd"), scatter_dimension=0, tiled=True),
    )
    expert_sum = (
        lax.psum_scatter(expand_grad, "shd", scatter_dimension=2, tiled=True),
        lax.psum_scatter(narrow_grad, "shd", scatter_dimension=1, tiled=True),
    )
    masters = (scales, attend, output, router, widener, reducer, experts, narrower)
    moments = (
        moment_scales,
        moment_attend,
        moment_output,
        moment_router,
        moment_widener,
        moment_reducer,
        moment_experts,
        moment_narrower,
    )
    squares = (
        square_scales,
        square_attend,
        square_output,
        square_router,
        square_widener,
        square_reducer,
        square_experts,
        square_narrower,
    )
    reduced = lax.psum(
        (
            dense_sum[0],
            dense_sum[1],
            dense_sum[2],
            dense_sum[3],
            dense_sum[4],
            dense_sum[5],
            expert_sum[0],
            expert_sum[1],
        ),
        "grp",
    )
    updated = [
        adam_update(
            masters[kind],
            moments[kind],
            squares[kind],
            reduced[kind],
            learning_rates[kind],
            decay_rates[kind],
        )
        for kind in range(8)
    ]
    return (
        block_out,
        input_grad.reshape(tokens_in.shape),
        updated[0][0],
        updated[0][1],
        updated[0][2],
        updated[1][0],
        updated[1][1],
        updated[1][2],
        updated[2][0],
        updated[2][1],
        updated[2][2],
        updated[3][0],
        updated[3][1],
        updated[3][2],
        updated[4][0],
        updated[4][1],
        updated[4][2],
        updated[5][0],
        updated[5][1],
        updated[5][2],
        updated[6][0],
        updated[6][1],
        updated[6][2],
        updated[7][0],
        updated[7][1],
        updated[7][2],
    )


def solution(mesh):
    placed = (
        P(("grp", "exp", "shd"), None, None),
        P(("grp", "exp", "shd"), None, None),
        P(("grp", "exp", "shd"), None),
        P(("grp", "exp", "shd"), None, None),
        P(None, ("exp", "shd")),
        P(None, ("exp", "shd")),
        P(None, ("exp", "shd")),
        P(None, ("exp", "shd"), None),
        P(None, ("exp", "shd"), None),
        P(None, ("exp", "shd"), None),
        P(("exp", "shd"), None),
        P(("exp", "shd"), None),
        P(("exp", "shd"), None),
        P(("exp", "shd"), None),
        P(("exp", "shd"), None),
        P(("exp", "shd"), None),
        P(None, ("exp", "shd"), None),
        P(None, ("exp", "shd"), None),
        P(None, ("exp", "shd"), None),
        P(("exp", "shd"), None),
        P(("exp", "shd"), None),
        P(("exp", "shd"), None),
        P("exp", None, "shd", None),
        P("exp", None, "shd", None),
        P("exp", None, "shd", None),
        P("exp", "shd", None),
        P("exp", "shd", None),
        P("exp", "shd", None),
    )
    return jax.shard_map(
        on_device,
        mesh=mesh,
        in_specs=placed,
        out_specs=(
            P(("grp", "exp", "shd"), None, None),
            P(("grp", "exp", "shd"), None, None),
            P(None, ("exp", "shd")),
            P(None, ("exp", "shd")),
            P(None, ("exp", "shd")),
            P(None, ("exp", "shd"), None),
            P(None, ("exp", "shd"), None),
            P(None, ("exp", "shd"), None),
            P(("exp", "shd"), None),
            P(("exp", "shd"), None),
            P(("exp", "shd"), None),
            P(("exp", "shd"), None),
            P(("exp", "shd"), None),
            P(("exp", "shd"), None),
            P(None, ("exp", "shd"), None),
            P(None, ("exp", "shd"), None),
            P(None, ("exp", "shd"), None),
            P(("exp", "shd"), None),
            P(("exp", "shd"), None),
            P(("exp", "shd"), None),
            P("exp", None, "shd", None),
            P("exp", None, "shd", None),
            P("exp", None, "shd", None),
            P("exp", "shd", None),
            P("exp", "shd", None),
            P("exp", "shd", None),
        ),
        check_vma=False,
    )
```

profile of v0, /device:TPU:0, one launch (start us, length us, event | category | flops | bytes accessed | tf_op | source)
XLA Modules:
  0.0 2234.5 jit_solution(10971590021765672228)
XLA Ops:
  20.6 42.4 %all-gather = bf16[16,48,2]{1,2,0:T(2,128)(2,1)S(1)} all-gather(bf16[1,48,2]{1,2,0:T(2,128)(2,1)S(1)} %convert_bitcast_fusion.3), channel_id=1, replica_groups=mesh['grp'=2,'exp'=4,'shd'=4] {'exp','shd'}, dimensions={0}, use_global_device_ids=true | all-gather | bytes 3264 | tf_op jit(solution)/shard_map/all_gather | solution.py:185
  64.0 35.7 %all-gather.1 = bf16[16,48,4]{1,2,0:T(4,128)(2,1)S(1)} all-gather(bf16[1,48,4]{1,2,0:T(4,128)(2,1)S(1)} %convert_bitcast_fusion.2), channel_id=1, replica_groups=mesh['grp'=2,'exp'=4,'shd'=4] {'exp','shd'}, dimensions={0}, use_global_device_ids=true | all-gather | bytes 6528 | tf_op jit(solution)/shard_map/all_gather | solution.py:188
  135.5 78.6 %while.30 = (s32[]{:T(128)}, bf16[2,512,12,64]{1,3,2,0:T(8,128)(2,1)}, f32[2,12,512,1]{2,1,3,0:T(8,128)S(1)}, s32[1,1024]{1,0:T(1,128)S(1)}, s32[2]{0:T(128)S(1)...) while((s32[]{:T(128)}, ...), condition=%wide.region_4.5_spmd, body=%wide.region_1.4_spmd.sunk | while | flops 1687021568 | bytes 183208784 | solution.py:103
  138.5 11.9 fusion.218
  150.3 12.8 fusion.219
  178.0 12.0 fusion.218
  190.0 12.3 fusion.219
  253.2 17.1 all-to-all-done.2
  276.6 14.3 fusion.106
  290.9 17.3 all-to-all-done
  310.0 14.3 all-gather.17.cloned.1.call-done
  324.3 23.0 %convolution_bitcast_fusion = f32[2,4,1,576,2048]{4,3,0,1,2:T(8,128)} fusion(bf16[1,2,768,2048]{3,2,1,0:T(8,128)(2,1)} %all-gather.17.cloned.1.call-done, bf16[4,1,576,768]{3,2,1,0:T(8,128)(2,1)} %copy-done.29), kind=kOutput, calls=%fused_computation.85 | convolution fusion | flops 14495514624 | bytes 47579136 | tf_op jit(solution)/shard_map/sjcd,jgdf->gsjcf/dot_general | solution.py:231
  347.3 22.7 %fusion.75 = (bf16[1,4,1,576,2048]{4,3,1,2,0:T(8,128)(2,1)}, bf16[1,4,1,576,2048]{4,3,1,2,0:T(8,128)(2,1)}) fusion(f32[2,4,1,576,2048]{4,3,0,1,2:T(8,128)} %convolution_bitcast_fusion, f32[4,576,2048]{2,1,0:T(8,128)S(1)} %copy-done.11), kind=kLoop, calls=%fused_computation.92 | loop fusion | flops 61341696 | bytes 75497472 | tf_op jit(solution)/shard_map/stack | solution.py:273
  370.0 23.1 %fusion.88 = f32[1,2,768,2048]{2,3,1,0:T(8,128)} fusion(bf16[1,4,1,576,2048]{4,3,1,2,0:T(8,128)(2,1)} %get-tuple-element.489, bf16[1,4,1,576,2048]{4,3,1,2,0:T(8,128)(2,1)} %get-tuple-element.488, bf16[4,1,576,768]{3,2,1,0:T(8,128)(2,1)} %copy-done.29), kind=kOutput, calls=%fused_computation.118 | convolution fusion | flops 14504951808 | bytes 34996224 | tf_op jit(solution)/shard_map/sjcd,gsjcf->jgdf/dot_general | solution.py:279
  393.1 19.5 copy.279
  412.6 18.3 convert_bitcast_fusion.1
  436.4 21.3 fusion.103
  457.7 12.4 convolution_bitcast_fusion.1
  470.2 31.3 %all-gather.15.cloned.1.call-done = bf16[2048,768]{1,0:T(8,128)(2,1)} async-done(((bf16[128,768]{1,0:T(8,128)(2,1)}), bf16[2048,768]{1,0:T(8,128)(2,1)}) %all-gather.15.cloned.1.call-update) | async-done | bytes 3145744 | tf_op jit(solution)/shard_map/all_gather | solution.py:190
  501.5 12.3 fusion.99
  518.6 12.5 fusion.89
  531.1 19.4 copy.277
  552.8 10.1 gather_fusion.1
  571.0 17.2 multiply_reduce_fusion.1
  594.1 10.1 gather_fusion.3
  612.4 12.6 reduce_sum.177
  625.0 14.5 multiply_reduce_fusion.3
  643.4 159.7 %while.31 = (s32[]{:T(128)}, bf16[2,512,12,64]{1,3,2,0:T(8,128)(2,1)}, f32[2,1024,12,64]{1,3,2,0:T(8,128)}, f32[2,1024,12,64]{1,3,2,0:T(8,128)}, s32[1,1024]{1,0...) while((s32[]{:T(128)}, ...), condition=%wide.region_21.22_spmd, body=%wide.region_19.21_spmd.sunk | while | flops 4122601472 | bytes 257085328 | solution.py:140
  646.4 11.4 fusion.229
  659.4 18.2 multiply_reduce_fusion.8
  677.7 17.0 multiply_convert_fusion.8
  709.9 13.4 bitcast_dynamic-update-slice_fusion.11
  725.9 11.4 fusion.229
  739.0 18.2 multiply_reduce_fusion.8
  757.1 17.0 multiply_convert_fusion.8
  789.5 13.4 bitcast_dynamic-update-slice_fusion.11
  829.4 11.1 copy.274
  846.6 19.5 fusion.100
  867.6 12.9 fusion.97
  895.8 33.0 %all-reduce.14.cloned.1.call-done = f32[1,2,768,2048]{3,1,0,2:T(2,128)} async-done(((f32[1,2,768,2048]{3,1,0,2:T(2,128)}), f32[1,2,768,2048]{3,1,0,2:T(2,128)}) %all-reduce.14.cloned.1.call-update) | async-done | bytes 12582928
  935.6 589.4 %all-reduce.16.cloned.1.call-done = (f32[3,768,768]{2,0,1:T(4,128)}, f32[2,768,2048]{2,0,1:T(2,128)}) async-done(((f32[3,768,768]{2,0,1:T(4,128)}, f32[2,768,2048]{2,0,1:T(2,128)}), (f32[3,768,768]{2,0,1:T(4,128)}, f32[2,768,2048]{2,0,1:T(2,128)})) %all-reduce.16.cloned.1.call-update) | async-done | bytes 19660816
  1529.6 127.8 %reduce-scatter.10.cloned.1.call-done = f32[48,768]{1,0:T(8,128)} async-done(((f32[768,768]{1,0:T(8,128)}), f32[48,768]{1,0:T(8,128)}) %reduce-scatter.10.cloned.1.call-update) | async-done | bytes 147472 | tf_op jit(solution)/shard_map/reduce_scatter | solution.py:342
  1657.4 112.2 %reduce-scatter.14.cloned.1.call-done = f32[1,512,768]{2,1,0:T(8,128)} async-done(((f32[1,2048,768]{2,1,0:T(8,128)}), f32[1,512,768]{2,1,0:T(8,128)}) %reduce-scatter.14.cloned.1.call-update) | async-done | bytes 1572880 | tf_op jit(solution)/shard_map/reduce_scatter | solution.py:349
  1769.6 152.5 %reduce-scatter.12.cloned.1.call-done = f32[128,768]{1,0:T(8,128)} async-done(((f32[2048,768]{1,0:T(8,128)}), f32[128,768]{1,0:T(8,128)}) %reduce-scatter.12.cloned.1.call-update) | async-done | bytes 393232 | tf_op jit(solution)/shard_map/reduce_scatter | solution.py:345
  1930.3 11.8 fusion.136
  1942.1 106.2 %reduce-scatter.16.cloned.1.call-done = f32[48,2]{1,0:T(8,128)} async-done(((f32[768,2]{1,0:T(8,128)}), f32[48,2]{1,0:T(8,128)}) %reduce-scatter.16.cloned.1.call-update) | async-done | bytes 400
  2049.1 124.9 %reduce-scatter.18.cloned.1.call-done = f32[48,4]{1,0:T(8,128)} async-done(((f32[768,4]{1,0:T(8,128)}), f32[48,4]{1,0:T(8,128)}) %reduce-scatter.18.cloned.1.call-update) | async-done | bytes 784
  2178.6 32.0 %all-reduce.18.cloned.1.call-done = (f32[3,48,768]{2,1,0:T(8,128)}, f32[48,768]{1,0:T(8,128)}, f32[2,48,2048]{2,1,0:T(8,128)}, f32[128,768]{1,0:T(8,128)}, f32[1...) async-done(((f32[3,48,768]{2,1,0:T(8,128)}, f32[48,768]{1,0:T(8,128)}, f32[2,48,2048]{2,1,0:T(8,128)}, f32[128,768]{1,0:T(8,128)}, f32[1,2,192,2048]{3,2,1,0:T(8,128)}, ...) | async-done | bytes 6488080 | tf_op jit(solution)/shard_map/psum | solution.py:372
  (359 shorter events, 282.9 us)
Async XLA Ops:
  7.2 119.9 %all-gather.9.cloned.1.call-start = ((), (), s32[]{:S(2)}) async-start(), calls=%async_computation.9 | async-start | bytes 3760128 | tf_op jit(solution)/shard_map/all_gather | solution.py:186
  9.2 210.8 %all-gather.11.cloned.1.call-start = ((), (), s32[]{:S(2)}) async-start(), calls=%async_computation.10 | async-start | bytes 1253376 | tf_op jit(solution)/shard_map/all_gather | solution.py:187
  10.8 265.8 %all-gather.19.cloned.1.call-start = ((), (), s32[]{:S(2)}) async-start(), calls=%async_computation.14 | async-start | bytes 3932160 | tf_op jit(solution)/shard_map/all_gather | solution.py:194
  13.2 311.1 %all-gather.17.cloned.1.call-start = ((), (), s32[]{:S(2)}) async-start(), calls=%async_computation.13 | async-start | bytes 7864320 | tf_op jit(solution)/shard_map/all_gather | solution.py:193
  14.7 49.0 %copy-start.20 = (bf16[1,1024,768]{2,1,0:T(8,128)(2,1)S(1)}, bf16[1,1024,768]{2,1,0:T(8,128)(2,1)}, u32[]{:S(2)}) copy-start(bf16[1,1024,768]{2,1,0:T(8,128)(2,1)} %param.32) | copy-start | bytes 4718596
  14.7 49.4 %copy-start.79 = (f32[48,4]{0,1:T(4,128)S(1)}, f32[48,4]{0,1:T(4,128)}, u32[]{:S(2)}) copy-start(f32[48,4]{0,1:T(4,128)} %param.45) | copy-start | bytes 2308
  14.7 85.7 %copy-start.24 = (bf16[1,1024,768]{2,1,0:T(8,128)(2,1)S(1)}, bf16[1,1024,768]{2,1,0:T(8,128)(2,1)}, u32[]{:S(2)}) copy-start(bf16[1,1024,768]{2,1,0:T(8,128)(2,1)} %param.33) | copy-start | bytes 4718596
  14.7 443.0 %all-gather.13.cloned.1.call-start = ((), (), s32[]{:S(2)}) async-start(), calls=%async_computation.11 | async-start | bytes 6684672 | tf_op jit(solution)/shard_map/all_gather | solution.py:189
  63.6 63.5 %copy-start.75 = (f32[768]{0:T(1024)}, f32[768]{0:T(1024)S(1)}, u32[]{:S(2)}) copy-start(f32[768]{0:T(1024)S(1)} %get-tuple-element.411) | copy-start | bytes 9220
  64.0 63.1 %copy-start.77 = (f32[1024]{0:T(1024)}, f32[1024]{0:T(1024)S(1)}, u32[]{:S(2)}) copy-start(f32[1024]{0:T(1024)S(1)} %add_rsqrt_fusion.1) | copy-start | bytes 12292
  150.3 16.3 copy-start
  190.0 15.4 copy-start
  214.1 9.9 copy-start.2
  239.6 30.7 %all-to-all-start.2 = ((bf16[4,1,576,768]{3,2,1,0:T(8,128)(2,1)}), bf16[4,1,576,768]{3,2,1,0:T(8,128)(2,1)}, u32[]{:S(2)}, u32[]{:S(2)}) async-start(bf16[4,1,576,768]{3,2,1,0:T(8,128)(2,1)} %bitcast.485), calls=%async_computation.2 | async-start | bytes 7077888 | tf_op jit(solution)/shard_map/all_to_all | solution.py:266
  270.3 37.9 %all-to-all-start = ((bf16[4,1,576,768]{3,2,1,0:T(8,128)(2,1)}), bf16[4,1,576,768]{3,2,1,0:T(8,128)(2,1)S(1)}, u32[]{:S(2)}, u32[]{:S(2)}) async-start(bf16[4,1,576,768]{3,2,1,0:T(8,128)(2,1)} %bitcast.484), calls=%async_computation | async-start | bytes 7077888 | tf_op jit(solution)/shard_map/all_to_all | solution.py:230
  274.2 227.3 %all-gather.15.cloned.1.call-start = ((), (), s32[]{:S(2)}) async-start(), calls=%async_computation.12 | async-start | bytes 3342336 | tf_op jit(solution)/shard_map/all_gather | solution.py:190
  324.3 23.0 %copy-start.11 = (f32[4,576,2048]{2,1,0:T(8,128)S(1)}, f32[4,576,2048]{2,1,0:T(8,128)}, u32[]{:S(2)}) copy-start(f32[4,576,2048]{2,1,0:T(8,128)} %fusion.106) | copy-start | bytes 56623108
  393.1 19.5 copy-start.89
  430.9 82.9 %all-to-all-start.1 = ((bf16[4,1,576,768]{3,2,1,0:T(8,128)(2,1)}), bf16[4,1,576,768]{3,2,1,0:T(8,128)(2,1)}, u32[]{:S(2)}, u32[]{:S(2)}) async-start(bf16[4,1,576,768]{3,2,1,0:T(8,128)(2,1)} %convert_bitcast_fusion.1), calls=%async_computation.1 | async-start | bytes 7077888 | tf_op jit(solution)/shard_map/all_to_all | solution.py:239
  435.6 493.2 %all-reduce.14.cloned.1.call-start = ((), (), s32[]{:S(2)}) async-start(), calls=%async_computation.20 | async-start | bytes 25165824
  436.4 21.3 copy-start.9
  457.7 43.8 %copy-start.25 = (bf16[1,1024,768]{2,1,0:T(8,128)(2,1)S(1)}, bf16[1,1024,768]{2,1,0:T(8,128)(2,1)}, u32[]{:S(2)}) copy-start(bf16[1,1024,768]{2,1,0:T(8,128)(2,1)} %param.33) | copy-start | bytes 4718596
  513.8 78.1 %all-to-all-start.3 = ((bf16[4,1,576,768]{3,2,1,0:T(8,128)(2,1)}), bf16[4,1,576,768]{3,2,1,0:T(8,128)(2,1)}, u32[]{:S(2)}, u32[]{:S(2)}) async-start(bf16[4,1,576,768]{3,2,1,0:T(8,128)(2,1)} %fusion.103), calls=%async_computation.3 | async-start | bytes 7077888 | tf_op jit(solution)/shard_map/all_to_all | solution.py:285
  518.6 1006.4 %all-reduce.16.cloned.1.call-start = ((), (), s32[]{:S(2)}) async-start(), calls=%async_computation.21 | async-start | bytes 44040192
  570.9 18.5 copy-start.58
  570.9 18.6 copy-start.47
  570.9 18.6 copy-start.60
  571.0 18.6 copy-start.64
  571.0 18.6 copy-start.66
  612.4 12.6 copy-start.13
  612.4 12.6 copy-start.70
  612.4 12.6 copy-start.72
  625.0 14.5 copy-start.26
  840.5 816.9 %reduce-scatter.10.cloned.1.call-start = ((), (), s32[]{:S(2)}) async-start(), calls=%async_computation.15 | async-start | bytes 2506752 | tf_op jit(solution)/shard_map/reduce_scatter | solution.py:342
  846.6 923.0 %reduce-scatter.14.cloned.1.call-start = ((), (), s32[]{:S(2)}) async-start(), calls=%async_computation.17 | async-start | bytes 7864320 | tf_op jit(solution)/shard_map/reduce_scatter | solution.py:349
  866.2 1055.8 %reduce-scatter.12.cloned.1.call-start = ((), (), s32[]{:S(2)}) async-start(), calls=%async_computation.16 | async-start | bytes 6684672 | tf_op jit(solution)/shard_map/reduce_scatter | solution.py:345
  880.5 1167.8 %reduce-scatter.16.cloned.1.call-start = ((), (), s32[]{:S(2)}) async-start(), calls=%async_computation.18 | async-start | bytes 417792
  883.6 10.8 copy-start.10
  883.6 10.8 copy-start.62
  893.9 1280.0 %reduce-scatter.18.cloned.1.call-start = ((), (), s32[]{:S(2)}) async-start(), calls=%async_computation.19 | async-start | bytes 417792
  895.8 1314.8 %all-reduce.18.cloned.1.call-start = ((), (), s32[]{:S(2)}) async-start(), calls=%async_computation.22 | async-start | bytes 12976128 | tf_op jit(solution)/shard_map/psum | solution.py:372
  1930.2 247.2 %copy-start.85 = (f32[2,48]{1,0:T(2,128)S(1)}, f32[2,48]{1,0:T(2,128)}, u32[]{:S(2)}) copy-start(f32[2,48]{1,0:T(2,128)} %param.36) | copy-start | bytes 1156
  1930.2 247.2 %copy-start.86 = (f32[2,48]{1,0:T(2,128)S(1)}, f32[2,48]{1,0:T(2,128)}, u32[]{:S(2)}) copy-start(f32[2,48]{1,0:T(2,128)} %param.37) | copy-start | bytes 1156
  1930.2 247.2 %copy-start.87 = (f32[2,48]{1,0:T(2,128)S(1)}, f32[2,48]{1,0:T(2,128)}, u32[]{:S(2)}) copy-start(f32[2,48]{1,0:T(2,128)} %param.38) | copy-start | bytes 1156
  1930.2 247.8 %copy-start.80 = (f32[48,4]{0,1:T(4,128)S(1)}, f32[48,4]{0,1:T(4,128)}, u32[]{:S(2)}) copy-start(f32[48,4]{0,1:T(4,128)} %param.45) | copy-start | bytes 2308
  1930.2 247.8 %copy-start.82 = (f32[48,4]{0,1:T(4,128)S(1)}, f32[48,4]{0,1:T(4,128)}, u32[]{:S(2)}) copy-start(f32[48,4]{0,1:T(4,128)} %param.46) | copy-start | bytes 2308
  1930.2 247.8 %copy-start.83 = (f32[48,4]{0,1:T(4,128)S(1)}, f32[48,4]{0,1:T(4,128)}, u32[]{:S(2)}) copy-start(f32[48,4]{0,1:T(4,128)} %param.47) | copy-start | bytes 2308
  1930.2 280.3 %copy-start.19 = (f32[1,2,192,2048]{3,2,1,0:T(8,128)S(1)}, f32[1,2,192,2048]{3,2,1,0:T(8,128)}, u32[]{:S(2)}) copy-start(f32[1,2,192,2048]{3,2,1,0:T(8,128)} %param.54) | copy-start | bytes 9437188
  (65 other events, 231.0 us)
Sparse Core Ops, SparseCore 0:
  11.5 74.0 all-gather.8
  88.9 54.7 all-gather.10
  145.8 62.3 all-gather.18
  210.3 113.9 all-gather.16
  327.4 92.3 all-gather.12
  423.1 78.3 all-gather.14
  504.0 424.8 all-reduce.13
  935.3 589.6 all-reduce.15
  1529.9 127.4 reduce-scatter.9
  1659.7 109.8 reduce-scatter.13
  1775.6 146.3 reduce-scatter.11
  1927.8 120.4 reduce-scatter.15
  2053.5 120.4 reduce-scatter.17
  2178.5 32.0 all-reduce.17
where the time goes:
time: 2240 us; the launch traced here: 2230 us
  waiting for transfers between devices  1360 us (61%)
  matrix products  394 us (18%)
  local copies, waits for them, and re-layouts  192 us (9%)
  other arithmetic  162 us (7%)
  blocking collectives  80.7 us (4%)
    unnamed x18, waiting for transfers between devices  854 us
    reduce_scatter x1, waiting for transfers between devices, on_device(): lax.psum_scatter(reducer_grad, ('exp', 'shd'), scatter_dimension=0, tiled...  152 us
    reduce_scatter x1, waiting for transfers between devices, on_device(): lax.psum_scatter(output_grad, ('exp', 'shd'), scatter_dimension=0, tiled=...  128 us
    reduce_scatter x1, waiting for transfers between devices, on_device(): lax.psum_scatter(narrow_grad, 'shd', scatter_dimension=1, tiled=True)  112 us
    dot_general x4, matrix products, block_scores(): jnp.einsum('qhe,khe->hqk', query_part, keys_all[sequence], preferred_elem...  46.6 us
  transfers between devices with their start and end apart: 18, of which 12 were waited for; matrix products, arithmetic and copies ran while one was open for 32% of the time, Pallas kernels for 0%

commit v1 on v0

v1 whole, which is shorter than its diff:
```python
import functools

import jax
import jax.numpy as jnp
from jax import lax
from jax.experimental import pallas as pl
from jax.experimental.pallas import tpu as pltpu
from jax.sharding import PartitionSpec as P

HEADS = 12
CAP = 576
VMEM_LIMIT = 60 * 1024 * 1024

norm_eps = 1e-06
adam_eps = 1e-08
beta_one = 0.9
beta_two = 0.95
first_fix = 1.0 - 0.9**10
second_fix = 1.0 - 0.95**10
learning_rates = (0.3, 0.02, 0.15, 0.02, 0.02, 0.012, 0.02, 0.012)
decay_rates = (0.0, 0.1, 0.1, 0.1, 0.1, 0.1, 0.1, 0.1)
masked_score = -1e30
bf16 = jnp.bfloat16
f32 = jnp.float32


def mm(a, b):
    return jnp.dot(a, b, preferred_element_type=f32)


def mm_nt(a, b):
    return lax.dot_general(a, b, (((1,), (1,)), ((), ())), preferred_element_type=f32)


def mm_tn(a, b):
    return lax.dot_general(a, b, (((0,), (0,)), ((), ())), preferred_element_type=f32)


def params(semantics=None, **more):
    return pltpu.CompilerParams(
        dimension_semantics=semantics, vmem_limit_bytes=VMEM_LIMIT, **more
    )


def whole_spec(shape, **more):
    zeros = (0,) * len(shape)
    return pl.BlockSpec(shape, lambda *_: zeros, **more)


def once(shape):
    return whole_spec(shape, pipeline_mode=pl.Buffered(1))


def forward_kernel(
    tok_ref, bidr_ref, bidc_ref, gains_ref, wa_ref, wo_ref, wr_ref, wrt_ref,
    qkv_ref, lse_ref, o_ref, mid_ref, h2_ref, probs_ref, probst_ref, h1_ref,
):
    pair = pl.program_id(0)
    seq, width = tok_ref.shape
    tile = 256

    @pl.when(pair == 0)
    def _():
        for row in range(0, seq, tile):
            x = tok_ref[pl.ds(row, tile), :].astype(f32)
            r1 = lax.rsqrt(jnp.mean(x * x, axis=1, keepdims=True) + norm_eps)
            h1_ref[pl.ds(row, tile), :] = (x * r1 * gains_ref[0:1, :]).astype(bf16)

    h1 = h1_ref[...]
    for i in range(3):
        w = wa_ref[0, :, i].reshape(width, 128)
        qkv_ref[i] = mm(h1, w).astype(bf16)
    qs = qkv_ref[0] * jnp.asarray(0.125, bf16)
    k = qkv_ref[1]
    vt = qkv_ref[2].T
    lane = lax.broadcasted_iota(jnp.int32, (tile, 128), 1)
    for q0 in range(0, seq, tile):
        kl = min(seq, q0 + 2 * tile)
        qt = qs[q0 : q0 + tile]
        allowed = bidc_ref[q0:kl, :] <= bidr_ref[0:1, q0 : q0 + tile]
        parts = []
        for head in range(2):
            qm = jnp.where((lane // 64) == head, qt, jnp.zeros_like(qt))
            tail = jnp.where(allowed, mm_nt(k[q0:kl], qm), masked_score)
            top = jnp.max(tail, axis=0, keepdims=True)
            if q0:
                lead = mm_nt(k[:q0], qm)
                top = jnp.maximum(top, jnp.max(lead, axis=0, keepdims=True))
                lead = jnp.exp(lead - top)
            tail = jnp.exp(tail - top)
            total = jnp.sum(tail, axis=0, keepdims=True)
            if q0:
                total = total + jnp.sum(lead, axis=0, keepdims=True)
            inverse = 1.0 / total
            vh = vt[64 * head : 64 * head + 64]
            ot = mm(vh[:, q0:kl], (tail * inverse).astype(bf16))
            if q0:
                ot = ot + mm(vh[:, :q0], (lead * inverse).astype(bf16))
            lse_ref[0, head : head + 1, q0 : q0 + tile] = top + jnp.log(total)
            parts.append(ot)
        out = jnp.concatenate(parts, axis=0).T.astype(bf16)
        o_ref[q0 : q0 + tile, pl.ds(pl.multiple_of(pair * 128, 128), 128)] = out

    @pl.when(pair == pl.num_programs(0) - 1)
    def _():
        half = wo_ref.shape[2]
        for row in range(0, seq, tile):
            rows = pl.ds(row, tile)
            o = o_ref[rows, :]
            add = jnp.concatenate([mm(o, wo_ref[0]), mm(o, wo_ref[1])], axis=1)
            mid = tok_ref[rows, :].astype(f32) + add
            mid_ref[rows, :] = mid
            r2 = lax.rsqrt(jnp.mean(mid * mid, axis=1, keepdims=True) + norm_eps)
            h2 = (mid * r2 * gains_ref[1:2, :]).astype(bf16)
            h2_ref[rows, :] = h2
            logits = mm(h2, wr_ref[...])
            spot = lax.broadcasted_iota(jnp.int32, logits.shape, 1)
            logits = jnp.where(spot < 4, logits, masked_score)
            e = jnp.exp(logits - jnp.max(logits, axis=1, keepdims=True))
            probs_ref[rows, :] = e / jnp.sum(e, axis=1, keepdims=True)
        logits = mm_nt(wrt_ref[...], h2_ref[...])
        spot = lax.broadcasted_iota(jnp.int32, logits.shape, 0)
        logits = jnp.where(spot < 4, logits, masked_score)
        e = jnp.exp(logits - jnp.max(logits, axis=0, keepdims=True))
        probst_ref[...] = e / jnp.sum(e, axis=0, keepdims=True)


def attention_forward(tokens, bid_row, bid_col, gains, wa, wo, wr, wrt):
    seq, width = tokens.shape
    pairs = width // 128
    per_half = pairs // 2
    return pl.pallas_call(
        forward_kernel,
        grid=(pairs,),
        in_specs=[
            once((seq, width)),
            once(bid_row.shape),
            once(bid_col.shape),
            once(gains.shape),
            pl.BlockSpec(
                (1, wa.shape[1], 3, wa.shape[3], 128),
                lambda i: (i // per_half, 0, 0, 0, i % per_half),
            ),
            once(wo.shape),
            once(wr.shape),
            once(wrt.shape),
        ],
        out_specs=[
            pl.BlockSpec((3, seq, 128), lambda i: (0, 0, i)),
            pl.BlockSpec((1, 8, seq), lambda i: (i, 0, 0)),
            whole_spec((seq, width)),
            whole_spec((seq, width)),
            whole_spec((seq, width)),
            whole_spec((seq, 128)),
            whole_spec((16, seq)),
        ],
        out_shape=[
            jax.ShapeDtypeStruct((3, seq, width), bf16),
            jax.ShapeDtypeStruct((pairs, 8, seq), f32),
            jax.ShapeDtypeStruct((seq, width), bf16),
            jax.ShapeDtypeStruct((seq, width), f32),
            jax.ShapeDtypeStruct((seq, width), bf16),
            jax.ShapeDtypeStruct((seq, 128), f32),
            jax.ShapeDtypeStruct((16, seq), f32),
        ],
        scratch_shapes=[pltpu.VMEM((seq, width), bf16)],
        compiler_params=params(("arbitrary",)),
        cost_estimate=pl.CostEstimate(
            flops=30_000_000_000, bytes_accessed=20_000_000, transcendentals=12_000_000
        ),
        name="attention_forward",
    )(tokens, bid_row, bid_col, gains, wa, wo, wr, wrt)


def dispatch_kernel(h2_ref, g_ref, place_ref, probst_ref, rows_ref, grads_ref):
    expert = pl.program_id(0)
    seq = h2_ref.shape[0]
    cap = rows_ref.shape[1]
    slot = lax.broadcasted_iota(jnp.int32, (cap, seq), 0)
    hit = slot == place_ref[pl.ds(expert, 1), :]
    chosen = jnp.sum(
        jnp.where(hit, probst_ref[pl.ds(expert, 1), :], 0.0), axis=1, keepdims=True
    )
    hot = hit.astype(f32).astype(bf16)
    rows_ref[0] = mm(hot, h2_ref[...]).astype(bf16)
    grads_ref[0] = (mm(hot, g_ref[...]) * chosen).astype(bf16)


def dispatch(h2, g, place_row, probst, experts_all, cap):
    seq, width = h2.shape
    return pl.pallas_call(
        dispatch_kernel,
        grid=(experts_all,),
        in_specs=[once(h2.shape), once(g.shape), once(place_row.shape), once(probst.shape)],
        out_specs=[pl.BlockSpec((1, cap, width), lambda e: (e, 0, 0))] * 2,
        out_shape=[jax.ShapeDtypeStruct((experts_all, cap, width), bf16)] * 2,
        compiler_params=params(("arbitrary",)),
        cost_estimate=pl.CostEstimate(
            flops=8_000_000_000, bytes_accessed=10_000_000, transcendentals=0
        ),
        name="dispatch",
    )(h2, g, place_row, probst)


def ffn_kernel(
    x_ref, g_ref, wg_ref, wu_ref, wn_ref,
    out_ref, gin_ref, dwg_ref, dwu_ref, dwn_ref,
    acc_out, acc_gin, hid_s, gg_s, ug_s,
    *, tile,
):
    f = pl.program_id(0)
    last = pl.num_programs(0) - 1
    rows_all = x_ref.shape[0]

    @pl.when(f == 0)
    def _():
        acc_out[...] = jnp.zeros_like(acc_out)
        acc_gin[...] = jnp.zeros_like(acc_gin)

    wg, wu, wn = wg_ref[0], wu_ref[0], wn_ref[...]
    for row in range(0, rows_all, tile):
        rows = pl.ds(row, tile)
        x, g = x_ref[rows, :], g_ref[rows, :]
        gate, up = mm(x, wg), mm(x, wu)
        sig = 1.0 / (1.0 + jnp.exp(-gate))
        active = gate * sig
        slope = sig * (1.0 + gate * (1.0 - sig))
        hidden = (active * up).astype(bf16)
        hgrad = mm_nt(g, wn)
        gg = (hgrad * up * slope).astype(bf16)
        ug = (hgrad * active).astype(bf16)
        hid_s[rows, :], gg_s[rows, :], ug_s[rows, :] = hidden, gg, ug
        acc_out[rows, :] += mm(hidden, wn)
        acc_gin[rows, :] += mm_nt(gg, wg) + mm_nt(ug, wu)
    dwg_ref[0] = mm_tn(x_ref[...], gg_s[...]).astype(dwg_ref.dtype)
    dwu_ref[0] = mm_tn(x_ref[...], ug_s[...]).astype(dwu_ref.dtype)
    dwn_ref[...] = mm_tn(hid_s[...], g_ref[...]).astype(dwn_ref.dtype)

    @pl.when(f == last)
    def _():
        out_ref[...] = acc_out[...].astype(out_ref.dtype)
        gin_ref[...] = acc_gin[...].astype(gin_ref.dtype)


def ffn(x, g, wgu, wn, out_type, tile, name):
    rows, width = x.shape
    hidden = wn.shape[0]
    ft = 512
    return pl.pallas_call(
        functools.partial(ffn_kernel, tile=tile),
        grid=(hidden // ft,),
        in_specs=[
            once((rows, width)),
            once((rows, width)),
            pl.BlockSpec((1, width, ft), lambda f: (0, 0, f)),
            pl.BlockSpec((1, width, ft), lambda f: (1, 0, f)),
            pl.BlockSpec((ft, width), lambda f: (f, 0)),
        ],
        out_specs=[
            once((rows, width)),
            once((rows, width)),
            pl.BlockSpec((1, width, ft), lambda f: (0, 0, f)),
            pl.BlockSpec((1, width, ft), lambda f: (0, 0, f)),
            pl.BlockSpec((ft, width), lambda f: (f, 0)),
        ],
        out_shape=[
            jax.ShapeDtypeStruct((rows, width), out_type),
            jax.ShapeDtypeStruct((rows, width), out_type),
            jax.ShapeDtypeStruct((1, width, hidden), bf16),
            jax.ShapeDtypeStruct((1, width, hidden), bf16),
            jax.ShapeDtypeStruct((hidden, width), bf16),
        ],
        scratch_shapes=[
            pltpu.VMEM((rows, width), f32),
            pltpu.VMEM((rows, width), f32),
            pltpu.VMEM((rows, ft), bf16),
            pltpu.VMEM((rows, ft), bf16),
            pltpu.VMEM((rows, ft), bf16),
        ],
        compiler_params=params(("arbitrary",)),
        cost_estimate=pl.CostEstimate(
            flops=18 * rows * width * hidden,
            bytes_accessed=12 * width * hidden + 8 * rows * width,
            transcendentals=rows * hidden,
        ),
        name=name,
    )(x, g, wgu, wgu, wn)


def combine_kernel(
    mid_ref, sout_ref, sin_ref, g_ref, h2_ref, probs_ref, place_ref, eout_ref, ein_ref,
    gains_ref, wr_ref, wo_ref,
    block_ref, midg_ref, midb_ref, og_ref, gain_ref, rgrad_ref,
):
    step = pl.program_id(0)
    tile, width = mid_ref.shape
    experts_all, cap = eout_ref.shape[0], eout_ref.shape[1]
    slot = lax.broadcasted_iota(jnp.int32, (tile, cap), 1)
    g = g_ref[...].astype(f32)
    probs = probs_ref[...]
    spot = lax.broadcasted_iota(jnp.int32, probs.shape, 1)
    mixture = jnp.zeros((tile, width), f32)
    moe_in = jnp.zeros((tile, width), f32)
    pgrad = jnp.zeros(probs.shape, f32)
    for e in range(experts_all):
        hot = (slot == place_ref[:, e : e + 1]).astype(f32).astype(bf16)
        pair_out = mm(hot, eout_ref[e])
        mixture += probs[:, e : e + 1] * pair_out
        grad = jnp.sum(g * pair_out, axis=1, keepdims=True)
        pgrad = jnp.where(spot == e, grad, pgrad)
        moe_in += mm(hot, ein_ref[e])
    mid = mid_ref[...]
    block_ref[...] = (mid + sout_ref[...] + mixture).astype(bf16)
    inner = jnp.sum(pgrad * probs, axis=1, keepdims=True)
    lgrad = (probs * (pgrad - inner)).astype(bf16)
    h2_grad = moe_in + mm_nt(lgrad, wr_ref[...]) + sin_ref[...]
    r2 = lax.rsqrt(jnp.mean(mid * mid, axis=1, keepdims=True) + norm_eps)
    n2 = mid * r2
    d2 = h2_grad * gains_ref[1:2, :]
    mid_grad = g + r2 * (d2 - n2 * jnp.mean(d2 * n2, axis=1, keepdims=True))
    midb = mid_grad.astype(bf16)
    midg_ref[...] = mid_grad
    midb_ref[...] = midb
    half = wo_ref.shape[2]
    og = mm_nt(midb[:, :half], wo_ref[0]) + mm_nt(midb[:, half:], wo_ref[1])
    og_ref[...] = og.astype(bf16)
    gsum = jnp.sum(h2_grad * n2, axis=0, keepdims=True)
    rsum = mm_tn(lgrad, h2_ref[...])[:16]

    @pl.when(step == 0)
    def _():
        gain_ref[...] = jnp.zeros_like(gain_ref)
        rgrad_ref[...] = jnp.zeros_like(rgrad_ref)

    gain_ref[0:1, :] += gsum
    rgrad_ref[...] += rsum


def combine(mid, sout, sin, g, h2, probs, place_col, eout, ein, gains, wr, wo):
    seq, width = mid.shape
    tile = 256
    by_rows = pl.BlockSpec((tile, width), lambda i: (i, 0))
    lanes = pl.BlockSpec((tile, 128), lambda i: (i, 0))
    return pl.pallas_call(
        combine_kernel,
        grid=(seq // tile,),
        in_specs=[
            by_rows, by_rows, by_rows, by_rows, by_rows, lanes, lanes,
            once(eout.shape), once(ein.shape), once(gains.shape), once(wr.shape), once(wo.shape),
        ],
        out_specs=[by_rows, by_rows, by_rows, by_rows, whole_spec((8, width)), whole_spec((16, width))],
        out_shape=[
            jax.ShapeDtypeStruct((seq, width), bf16),
            jax.ShapeDtypeStruct((seq, width), f32),
            jax.ShapeDtypeStruct((seq, width), bf16),
            jax.ShapeDtypeStruct((seq, width), bf16),
            jax.ShapeDtypeStruct((8, width), f32),
            jax.ShapeDtypeStruct((16, width), f32),
        ],
        compiler_params=params(("arbitrary",)),
        cost_estimate=pl.CostEstimate(
            flops=11_000_000_000, bytes_accessed=30_000_000, transcendentals=0
        ),
        name="combine",
    )(mid, sout, sin, g, h2, probs, place_col, eout, ein, gains, wr, wo)


def backward_kernel(qkv_ref, og_ref, lse_ref, bidr_ref, bidc_ref, grad_ref, dk_s, dv_s):
    seq = og_ref.shape[0]
    tile = 256
    qs = qkv_ref[0] * jnp.asarray(0.125, bf16)
    k = qkv_ref[1]
    v = qkv_ref[2]
    kt = k.T
    og = og_ref[...]
    lane = lax.broadcasted_iota(jnp.int32, (tile, 128), 1)
    dk_s[...] = jnp.zeros_like(dk_s)
    dv_s[...] = jnp.zeros_like(dv_s)
    for q0 in range(0, seq, tile):
        kl = min(seq, q0 + 2 * tile)
        qt, ot = qs[q0 : q0 + tile], og[q0 : q0 + tile]
        allowed = bidc_ref[q0:kl, :] <= bidr_ref[0:1, q0 : q0 + tile]
        parts = []
        for head in range(2):
            own = (lane // 64) == head
            qm = jnp.where(own, qt, jnp.zeros_like(qt))
            om = jnp.where(own, ot, jnp.zeros_like(ot))
            lse = lse_ref[0, head : head + 1, q0 : q0 + tile]
            spans = ([(0, q0)] if q0 else []) + [(q0, kl)]
            kept = []
            delta = jnp.zeros((1, tile), f32)
            for low, high in spans:
                s = mm_nt(k[low:high], qm)
                if low == q0:
                    s = jnp.where(allowed, s, masked_score)
                p = jnp.exp(s - lse)
                dp = mm_nt(v[low:high], om)
                delta = delta + jnp.sum(p * dp, axis=0, keepdims=True)
                kept.append((low, high, p, dp))
            dq = jnp.zeros((64, tile), f32)
            for low, high, p, dp in kept:
                ds = (p * (dp - delta)).astype(bf16)
                dv_s[low:high, :] += mm(p.astype(bf16), om)
                dk_s[low:high, :] += mm(ds, qm)
                dq = dq + mm(kt[64 * head : 64 * head + 64, low:high], ds)
            parts.append(dq)
        dq = jnp.concatenate(parts, axis=0).T * 0.125
        grad_ref[0, q0 : q0 + tile, :] = dq.astype(bf16)
    grad_ref[1] = dk_s[...].astype(bf16)
    grad_ref[2] = dv_s[...].astype(bf16)


def attention_backward(qkv, og, lse, bid_row, bid_col):
    _, seq, width = qkv.shape
    pairs = width // 128
    return pl.pallas_call(
        backward_kernel,
        grid=(pairs,),
        in_specs=[
            pl.BlockSpec((3, seq, 128), lambda i: (0, 0, i)),
            pl.BlockSpec((seq, 128), lambda i: (0, i)),
            pl.BlockSpec((1, 8, seq), lambda i: (i, 0, 0)),
            once(bid_row.shape),
            once(bid_col.shape),
        ],
        out_specs=pl.BlockSpec((3, seq, 128), lambda i: (0, 0, i)),
        out_shape=jax.ShapeDtypeStruct((3, seq, width), bf16),
        scratch_shapes=[pltpu.VMEM((seq, 128), f32), pltpu.VMEM((seq, 128), f32)],
        compiler_params=params(("arbitrary",)),
        cost_estimate=pl.CostEstimate(
            flops=35_000_000_000, bytes_accessed=12_000_000, transcendentals=12_000_000
        ),
        name="attention_backward",
    )(qkv, og, lse, bid_row, bid_col)


def adam_update(weight, moment, square, gradient, step_rate, shrink_rate):
    moment_next = beta_one * moment + (1.0 - beta_one) * gradient
    square_next = beta_two * square + (1.0 - beta_two) * gradient * gradient
    direction = moment_next / first_fix / (jnp.sqrt(square_next / second_fix) + adam_eps)
    return (weight - step_rate * (direction + shrink_rate * weight), moment_next, square_next)


def pick(array, axis, index):
    return lax.dynamic_index_in_dim(array, index, axis, keepdims=False)


def sum_parts(array):
    return jnp.sum(array.astype(f32), axis=0)


def reduce_scatter(stacked, axes, groups, core):
    own, other = pick(stacked, 0, core), pick(stacked, 0, 1 - core)
    swap = [(i, i ^ 1) for i in range(groups)]
    arrived = lax.ppermute(other, "grp", swap)
    part = (own.astype(f32) + arrived.astype(f32)).astype(bf16)
    for axis in axes[:-1]:
        size = lax.axis_size(axis)
        part = part.reshape((size, part.shape[0] // size) + part.shape[1:])
        part = lax.all_to_all(part, axis, 0, 0, tiled=True)
        part = sum_parts(part).astype(bf16)
    part = sum_parts(lax.all_to_all(part, axes[-1], 0, 0, tiled=True))
    both = jnp.zeros((2,) + part.shape, f32)
    both = lax.dynamic_update_index_in_dim(both, part, core, 0)
    if groups > 2:
        return lax.psum(both, "grp")
    return lax.dynamic_update_index_in_dim(both, lax.ppermute(part, "grp", swap), 1 - core, 0)


def on_device(
    tokens_in, cotangent, block_ids, expert_ids,
    scales, moment_scales, square_scales, attend, moment_attend, square_attend,
    output, moment_output, square_output, router, moment_router, square_router,
    widener, moment_widener, square_widener, reducer, moment_reducer, square_reducer,
    experts, moment_experts, square_experts, narrower, moment_narrower, square_narrower,
):
    groups, exps, shds = (lax.axis_size(a) for a in ("grp", "exp", "shd"))
    spread = exps * shds
    core = lax.rem(lax.axis_index("grp"), 2)
    _, seq, width = tokens_in.shape
    hidden = reducer.shape[1 - 1] * spread
    experts_all = exps * experts.shape[0]
    rows = output.shape[0]
    half = width // 2
    tokens, g = tokens_in.reshape(seq, width), cotangent.reshape(seq, width)

    def gather(part, axes, order):
        names = ("grp",) + axes if order == "first" else axes + ("grp",)
        if groups == 2:
            return lax.all_gather(part, names, axis=0, tiled=False).reshape((-1,) + part.shape)
        wide = lax.all_gather(part, names, axis=0, tiled=False)
        shape = (groups, -1) if order == "first" else (-1, groups)
        wide = wide.reshape(shape + part.shape)
        wide = wide[:2] if order == "first" else wide[:, :2]
        return wide.reshape((-1,) + part.shape)

    both = ("exp", "shd")
    small = jnp.concatenate([router.reshape(-1), scales.reshape(-1)])
    small = jnp.pad(small, (0, half - small.shape[0])).reshape(1, half)
    small = jnp.pad(small, ((0, 15), (0, 0))).astype(bf16)
    columns = lambda a, n: pick(a.astype(bf16).reshape(n, 2, half), 1, core)
    payload = jnp.concatenate(
        [columns(attend, 3 * rows), columns(output, rows), small], axis=0
    )
    first = gather(payload, both, "first").reshape(2, spread, payload.shape[0], half)
    w_experts = gather(pick(experts.astype(bf16)[0], 0, core), ("shd",), "first").reshape(2, width, hidden)
    w_narrower = gather(
        pick(narrower.astype(bf16).reshape(2, -1, width), 0, core), ("shd",), "last"
    ).reshape(hidden, width)
    w_widener = gather(pick(widener.astype(bf16), 0, core), both, "first").reshape(2, width, hidden)
    w_reducer = gather(
        pick(reducer.astype(bf16).reshape(2, -1, width), 0, core), both, "last"
    ).reshape(hidden, width)

    wa = first[:, :, : 3 * rows].reshape(2, spread, 3, rows, half)
    wo = first[:, :, 3 * rows : 4 * rows].reshape(2, width, half)
    packed = first[0, :, 4 * rows]
    count = rows * experts_all
    w_router = packed[:, :count].reshape(width, experts_all)
    gains = packed[:, count : count + 2 * rows].reshape(spread, 2, rows)
    gains = gains.transpose(1, 0, 2).reshape(2, width).astype(f32)
    gains = jnp.pad(gains, ((0, 6), (0, 0)))
    wr = jnp.pad(w_router, ((0, 0), (0, 128 - experts_all)))
    wrt = jnp.pad(w_router.T, ((0, 16 - experts_all), (0, 0)))

    ids = expert_ids.reshape(seq, 2)
    every = jnp.arange(128, dtype=jnp.int32)[None, :]
    hot = (ids[:, 0:1] == every) | (ids[:, 1:2] == every)
    order = jnp.arange(seq, dtype=jnp.int32)
    before = (order[:, None] > order[None, :]).astype(bf16)
    placed = mm(before, hot.astype(bf16)).astype(jnp.int32)
    place_col = jnp.where(hot, placed, -1)
    place_row = place_col[:, :16].T
    bid = block_ids.reshape(1, seq)
    bid_row = jnp.broadcast_to(bid, (8, seq))
    bid_col = jnp.broadcast_to(bid.reshape(seq, 1), (seq, 256))

    qkv, lse, o, mid, h2, probs, probst = attention_forward(
        tokens, bid_row, bid_col, gains, wa, wo, wr, wrt
    )
    slot_rows, slot_grad = dispatch(h2, g, place_row, probst, experts_all, CAP)
    swap_rows = functools.partial(lax.all_to_all, axis_name="exp", split_axis=0, concat_axis=0, tiled=True)
    received, back_rows = swap_rows(slot_rows), swap_rows(slot_grad)
    sout, sin, dsg, dsu, dsn = ffn(h2, g, w_widener, w_reducer, f32, 256, "shared")
    eout, ein, dwg, dwu, dwn = ffn(
        received.reshape(-1, width), back_rows.reshape(-1, width), w_experts, w_narrower, bf16, 384, "routed"
    )
    eout = swap_rows(eout.reshape(experts_all, CAP, width))
    ein = swap_rows(ein.reshape(experts_all, CAP, width))
    block_out, mid_grad, midb, og, gain_two, rgrad = combine(
        mid, sout, sin, g, h2, probs, place_col, eout, ein, gains, wr, wo
    )
    dqkv = attention_backward(qkv, og, lse, bid_row, bid_col)

    x = tokens.astype(f32)
    r1 = lax.rsqrt(jnp.mean(x * x, axis=1, keepdims=True) + norm_eps)
    n1 = x * r1
    h1 = (n1 * gains[0:1]).astype(bf16)
    attend_grad = jnp.einsum("nd,tnf->tdf", h1, dqkv, preferred_element_type=f32)
    output_grad = mm_tn(o, midb)
    w_full = wa.transpose(2, 1, 3, 0, 4).reshape(3, width, width)
    h1_grad = jnp.einsum("tnf,tdf->nd", dqkv, w_full, preferred_element_type=f32)
    gain_one = jnp.sum(h1_grad * n1, axis=0)
    d1 = h1_grad * gains[0:1]
    input_grad = mid_grad + r1 * (d1 - n1 * jnp.mean(d1 * n1, axis=1, keepdims=True))

    g_experts = reduce_scatter(
        jnp.concatenate([dwg, dwu], axis=0).reshape(2, shds, width // shds, hidden), ("shd",), groups, core
    )
    g_narrower = reduce_scatter(
        dwn.reshape(shds, 2, -1, width).transpose(1, 0, 2, 3), ("shd",), groups, core
    )
    small = jnp.concatenate(
        [rgrad[:experts_all], gain_one[None, :], gain_two[0:1]], axis=0
    ).reshape(-1, spread, rows).transpose(1, 0, 2).reshape(spread, 1, -1)
    small = jnp.pad(small, ((0, 0), (0, 15), (0, width - small.shape[2])))
    dense = jnp.concatenate(
        [
            attend_grad.astype(bf16).reshape(3, spread, rows, width).transpose(1, 0, 2, 3).reshape(spread, -1, width),
            output_grad.astype(bf16).reshape(spread, rows, width),
            jnp.concatenate([dsg, dsu], axis=0).reshape(2, spread, rows, hidden).transpose(1, 0, 2, 3).reshape(spread, -1, width),
            dsn.reshape(spread, -1, width),
            small.astype(bf16),
        ],
        axis=1,
    )
    total = dense.shape[1]
    dense = dense.reshape(spread, 2, total // 2, width).transpose(1, 0, 2, 3)
    dense = reduce_scatter(dense, both, groups, core).reshape(total, width)
    sizes = (3 * rows, rows, 2 * rows * hidden // width, reducer.shape[0])
    starts = (0, sizes[0], sizes[0] + sizes[1], sum(sizes[:3]))
    cut = lambda i, shape: dense[starts[i] : starts[i] + sizes[i]].reshape(shape)
    tiny = dense[sum(sizes)][: (experts_all + 2) * rows].reshape(experts_all + 2, rows)
    grads = (
        tiny[experts_all:],
        cut(0, attend.shape),
        cut(1, output.shape),
        tiny[:experts_all].T,
        cut(2, widener.shape),
        cut(3, reducer.shape),
        g_experts.reshape(experts.shape),
        g_narrower.reshape(narrower.shape),
    )
    masters = (scales, attend, output, router, widener, reducer, experts, narrower)
    moments = (
        moment_scales, moment_attend, moment_output, moment_router,
        moment_widener, moment_reducer, moment_experts, moment_narrower,
    )
    squares = (
        square_scales, square_attend, square_output, square_router,
        square_widener, square_reducer, square_experts, square_narrower,
    )
    results = [block_out.reshape(tokens_in.shape), input_grad.reshape(tokens_in.shape)]
    for kind in range(8):
        results.extend(
            adam_update(
                masters[kind], moments[kind], squares[kind], grads[kind],
                learning_rates[kind], decay_rates[kind],
            )
        )
    return tuple(results)


def solution(mesh):
    tokens = P(("grp", "exp", "shd"), None, None)
    both = ("exp", "shd")
    kinds = (
        P(None, both), P(None, both, None), P(both, None), P(both, None),
        P(None, both, None), P(both, None), P("exp", None, "shd", None), P("exp", "shd", None),
    )
    thrice = tuple(kind for kind in kinds for _ in range(3))
    return jax.shard_map(
        on_device,
        mesh=mesh,
        in_specs=(tokens, tokens, P(("grp", "exp", "shd"), None), tokens) + thrice,
        out_specs=(tokens, tokens) + thrice,
        check_vma=False,
    )
```

time: 2240 us -> 825 us (0.37)
  waiting for transfers between devices: 1360 us -> 372 us
  matrix products: 394 us -> 16.3 us
  Pallas kernels: 0 us -> 236 us
  local copies, waits for them, and re-layouts: 192 us -> 80.5 us
  other arithmetic: 162 us -> 63.5 us
  blocking collectives: 80.7 us -> 0 us
    unnamed x18 -> x5, waiting for transfers between devices: 854 us -> 0.08 us
    reduce_scatter x3 -> x0, waiting for transfers between devices: 392 us -> none  [the longest x1 152 us: on_device(): lax.psum_scatter(reducer_grad, ('exp', 'shd'), scatter_dimension=0, tiled...]
    dot_general x34 -> x4, matrix products: 392 us -> 16.3 us  [the longest x1 8.18 us: on_device(): jnp.einsum('nd,tnf->tdf', h1, dqkv, preferred_element_type=f32)]
    all_to_all x4 -> x8, waiting for transfers between devices: 34.4 us -> 294 us  [the longest x3 118 us: reduce_scatter(): part = sum_parts(lax.all_to_all(part, axes[-1], 0, 0, tiled=True))]
    pallas_call x0 -> x6, Pallas kernels: none -> 236 us  [the longest x2 116 us: ffn(): pl.pallas_call(functools.partial(ffn_kernel, tile=tile), grid=(hidden //...]
    all_gather x2 -> x0, blocking collectives: 78 us -> none  [the longest x1 42.4 us: on_device(): lax.all_gather(scales.astype(jnp.bfloat16), ('exp', 'shd'), axis=1, tiled...]
    reduce_sum x12 -> x5, other arithmetic: 63.2 us -> 12.7 us  [the longest x4 10.9 us: sum_parts(): return jnp.sum(array.astype(f32), axis=0)]
    transpose x3, local copies, waits for them, and re-layouts: 50 us -> 6.21 us  [the longest x1 5.38 us: on_device(): w_full = wa.transpose(2, 1, 3, 0, 4).reshape(3, width, width)]
  transfers between devices with their start and end apart: 18 -> 19, of which waited for: 12 -> 10; matrix products, arithmetic and copies ran while one was open for 32% -> 12% of each run, Pallas kernels for 0% -> 21%
where the time goes in v1:
time: 825 us; the launch traced here: 820 us
  waiting for transfers between devices  372 us (45%)
  Pallas kernels  236 us (29%)
  local copies, waits for them, and re-layouts  80.5 us (10%)
  other arithmetic  63.5 us (8%)
  starting transfers between devices  37.3 us (5%)
  matrix products  16.3 us (2%)
  between operations  14.8 us (2%)
    all_to_all x3, waiting for transfers between devices, reduce_scatter(): part = sum_parts(lax.all_to_all(part, axes[-1], 0, 0, tiled=True))  118 us
    pallas_call x2, Pallas kernels, ffn(): pl.pallas_call(functools.partial(ffn_kernel, tile=tile), grid=(hidden //...  116 us
    all_to_all x2, waiting for transfers between devices, on_device(): received, back_rows = (swap_rows(slot_rows), swap_rows(slot_grad))  88 us
    all_to_all x1, waiting for transfers between devices, reduce_scatter(): part = lax.all_to_all(part, axis, 0, 0, tiled=True)  67.9 us
    all_gather x5, waiting for transfers between devices, gather(): lax.all_gather(part, names, axis=0, tiled=False).reshape((-1,) + part.shape)  60.9 us
    pallas_call x1, Pallas kernels, attention_forward(): pl.pallas_call(forward_kernel, grid=(pairs,), in_specs=[once((seq, width)...  45.9 us
    pallas_call x1, Pallas kernels, attention_backward(): pl.pallas_call(backward_kernel, grid=(pairs,), in_specs=[pl.BlockSpec((3,...  38.6 us
    pallas_call x1, Pallas kernels, combine(): pl.pallas_call(combine_kernel, grid=(seq // tile,), in_specs=[by_rows, by...  24.2 us
  transfers between devices with their start and end apart: 19, of which 10 were waited for; matrix products, arithmetic and copies ran while one was open for 12% of the time, Pallas kernels for 21%

profile of v1, /device:TPU:0, one launch (start us, length us, event | category | flops | bytes accessed | tf_op | source)
XLA Modules:
  0.0 820.5 jit_solution(3706369415860901443)
XLA Ops:
  13.3 2.4 dynamic-slice_convert_fusion
  19.1 60.9 %all-gather.14.cloned.1.call-done = bf16[6656,384]{1,0:T(8,128)(2,1)} async-done(((bf16[208,384]{1,0:T(8,128)(2,1)}), bf16[6656,384]{1,0:T(8,128)(2,1)}) %all-gather.14.cloned.1.call-update) | async-done | bytes 5111824 | tf_op jit(solution)/shard_map/all_gather | solution.py:490
  80.8 4.1 slice.89
  85.0 2.4 slice.90
  91.8 45.9 %attention_forward.1 = (bf16[3,1024,768]{2,1,0:T(8,128)(2,1)}, f32[6,8,1024]{2,1,0:T(8,128)}, bf16[1024,768]{1,0:T(8,128)(2,1)}, f32[1024,768]{1,0:T(8,128)}, bf...) custom-call(bf16[1024,768]{1,0:T(8,128)(2,1)} %bitcast.141, ...), custom_call_target="tpu_custom_call" | custom-call | flops 30000001024 | bytes 20000000 | tf_op jit(solution)/shard_map/attention_forward/pallas_call | solution.py:132
  137.7 11.1 %dispatch.1 = (bf16[4,576,768]{2,1,0:T(8,128)(2,1)}, bf16[4,576,768]{2,1,0:T(8,128)(2,1)}) custom-call(bf16[1024,768]{1,0:T(8,128)(2,1)} %get-tuple-element.52.x_ref.h2_ref, bf16[1024,768]{1,0:T(8,128)(2,1)} %bitcast.176, s32[16,1024]{1,0:T(8,128)} %copy.105.place_ref, f32[16,1024]{1,0:T(8,128)} %get-tuple-element.56.probst_ref), custom_call_target="tpu_custom_call" | custom-call | flops 8000000000 | bytes 10000000 | tf_op jit(solution)/shard_map/dispatch/pallas_call | solution.py:191
  148.8 3.7 all-to-all-start
  154.3 39.3 %all-to-all-done = bf16[4,576,768]{2,1,0:T(8,128)(2,1)S(1)} async-done(((bf16[4,576,768]{2,1,0:T(8,128)(2,1)}), bf16[4,576,768]{2,1,0:T(8,128)(2,1)S(1)}, u32[]{:S(2)}, u32[]{:S(2)}) %all-to-all-start) | async-done | bytes 3538976 | tf_op jit(solution)/shard_map/all_to_all | solution.py:543
  195.3 4.7 all-to-all-start.1
  200.1 48.7 %all-to-all-done.1 = bf16[4,576,768]{2,1,0:T(8,128)(2,1)} async-done(((bf16[4,576,768]{2,1,0:T(8,128)(2,1)}), bf16[4,576,768]{2,1,0:T(8,128)(2,1)}, u32[]{:S(2)}, u32[]{:S(2)}) %all-to-all-start.1) | async-done | bytes 3538976 | tf_op jit(solution)/shard_map/all_to_all | solution.py:543
  248.8 78.0 %routed.1 = (bf16[2304,768]{1,0:T(8,128)(2,1)}, bf16[2304,768]{1,0:T(8,128)(2,1)}, bf16[1,768,2048]{2,1,0:T(8,128)(2,1)}, bf16[1,768,2048]{2,1,0:T(8,128)(2,1)}, bf16[2048,768]{1,0:T(8,128)(2,1)}) custom-call(bf16[2304,768]{1,0:T(8,128)(2,1)} %bitcast.146, bf16[2304,768]{1,0:T(8,128)(2,1)} %bitcast.17.g_ref, bf16[2,768,2048]{2,1,0:T(8,128)(2,1)} %bitcast.170, ...), custom_call_target="tpu_custom_call" | custom-call | flops 65229815808 | bytes 33030144 | tf_op jit(solution)/shard_map/routed/pallas_call | solution.py:249
  326.8 5.0 all-to-all-start.2
  335.7 5.4 copy.106
  341.0 8.9 %reshape.295 = bf16[3,768,768]{2,1,0:T(8,128)(2,1)} reshape(bf16[3,16,48,2,384]{4,3,2,1,0:T(2,128)(2,1)} %copy.106) | data formatting | bytes 7077888 | tf_op jit(solution)/shard_map/reshape | solution.py:561
  349.9 20.5 %all-to-all-done.2.eout_ref = bf16[4,576,768]{2,1,0:T(8,128)(2,1)} async-done(((bf16[4,576,768]{2,1,0:T(8,128)(2,1)}), bf16[4,576,768]{2,1,0:T(8,128)(2,1)}, u32[]{:S(2)}, u32[]{:S(2)}) %all-to-all-start.2) | async-done | bytes 3538976 | tf_op jit(solution)/shard_map/all_to_all | solution.py:548
  370.4 3.7 all-to-all-start.3
  374.2 38.0 %shared.1 = (f32[1024,768]{1,0:T(8,128)}, f32[1024,768]{1,0:T(8,128)}, bf16[1,768,2048]{2,1,0:T(8,128)(2,1)}, bf16[1,768,2048]{2,1,0:T(8,128)(2,1)}, bf16[2048,768]{1,0:T(8,128)(2,1)}) custom-call(bf16[1024,768]{1,0:T(8,128)(2,1)} %get-tuple-element.52.x_ref.h2_ref, bf16[1024,768]{1,0:T(8,128)(2,1)} %bitcast.177, bf16[2,768,2048]{2,1,0:T(8,128)(2,1)} %bitcast.172, ...), custom_call_target="tpu_custom_call" | custom-call | flops 28991029248 | bytes 25165824 | tf_op jit(solution)/shard_map/shared/pallas_call | solution.py:249
  412.2 3.4 pad_maximum_fusion
  415.7 3.2 copy.125
  418.8 12.1 %reshape.301 = bf16[16,256,768]{2,1,0:T(8,128)(2,1)} reshape(bf16[16,2,48,2048]{3,2,1,0:T(8,128)(2,1)} %bitcast.131) | data formatting | bytes 12582912 | tf_op jit(solution)/shard_map/reshape | solution.py:581
  432.7 24.2 %combine.1 = (bf16[1024,768]{1,0:T(8,128)(2,1)}, f32[1024,768]{1,0:T(8,128)}, bf16[1024,768]{1,0:T(8,128)(2,1)}, bf16[1024,768]{1,0:T(8,128)(2,1)}, f32[8,768]{1,0:T(8,128)}, /*index=5*/f32[16,768]{1,0:T(8,128)}) custom-call(f32[1024,768]{1,0:T(8,128)} %get-tuple-element.51.mid_ref, f32[1024,768]{1,0:T(8,128)} %get-tuple-element.53.sout_ref, ...), custom_call_target="tpu_custom_call" | custom-call | flops 11000000512 | bytes 30000000 | tf_op jit(solution)/shard_map/combine/pallas_call | solution.py:344
  456.9 38.6 %attention_backward.1 = bf16[3,1024,768]{2,1,0:T(8,128)(2,1)} custom-call(bf16[3,1024,768]{2,1,0:T(8,128)(2,1)} %get-tuple-element.63.qkv_ref, bf16[1024,768]{1,0:T(8,128)(2,1)} %get-tuple-element.64.og_ref, f32[6,8,1024]{2,1,0:T(8,128)} %get-tuple-element.65.lse_ref, s32[8,1024]{1,0:T(8,128)} %broadcast_in_dim.49.bidr_ref, ...), custom_call_target="tpu_custom_call" | custom-call | flops 35000000512 | bytes 12000000 | tf_op jit(solution)/shard_map/attention_backward/pallas_call | solution.py:416
  495.5 8.2 convolution_convert_fusion
  503.7 5.8 fusion.13
  511.5 2.3 copy.108
  513.8 2.0 constant_dynamic-update-slice_fusion.3
  518.5 3.1 constant_dynamic-update-slice_fusion.1
  524.3 6.6 dynamic-slice_bitcast_fusion
  531.6 11.4 %collective-permute-done.4 = bf16[4,256,768]{2,1,0:T(8,128)(2,1)S(1)} collective-permute-done((bf16[4,256,768]{2,1,0:T(8,128)(2,1)S(1)}, bf16[4,256,768]{2,1,0:T(8,128)(2,1)S(1)}, u32[]{:S(2)}, u32[]{:S(2)}) %collective-permute-start.4) | collective-permute-done | bytes 1572896 | tf_op jit(solution)/shard_map/ppermute | solution.py:455
  544.6 4.9 all-to-all-start.7
  549.5 10.0 %fusion = bf16[16,296,768]{2,1,0:T(8,128)(2,1)} fusion(bf16[16,296,768]{2,1,0:T(8,128)(2,1)} %collective-permute-done, bf16[16,2,296,768]{3,2,1,0:T(8,128)(2,1)} %bitcast.37, s32[]{:T(128)S(6)} %select_n.38), kind=kLoop, calls=%fused_computation.1 | loop fusion | flops 14548992 | bytes 21823492 | tf_op jit(solution)/shard_map/convert_element_type | solution.py:456
  559.5 27.5 %all-to-all-done.7 = bf16[4,256,768]{2,1,0:T(8,128)(2,1)S(1)} async-done(((bf16[4,256,768]{2,1,0:T(8,128)(2,1)}), bf16[4,256,768]{2,1,0:T(8,128)(2,1)S(1)}, u32[]{:S(2)}, u32[]{:S(2)}) %all-to-all-start.7) | async-done | bytes 1572896 | tf_op jit(solution)/shard_map/all_to_all | solution.py:462
  588.1 5.4 all-to-all-start.4
  593.6 3.4 pad_maximum_fusion.1
  597.3 5.6 collective-permute-done.2
  603.0 3.0 fusion.1
  606.0 67.9 %all-to-all-done.4 = bf16[4,4,296,768]{3,2,1,0:T(8,128)(2,1)} async-done(((bf16[4,4,296,768]{3,2,1,0:T(8,128)(2,1)}), bf16[4,4,296,768]{3,2,1,0:T(8,128)(2,1)}, u32[]{:S(2)}, u32[]{:S(2)}) %all-to-all-start.4) | async-done | bytes 7274528 | tf_op jit(solution)/shard_map/all_to_all | solution.py:460
  673.9 4.3 all-to-all-start.6
  678.2 2.6 convert_reduce_fusion.2
  680.8 5.9 reduce_sum.69
  686.6 61.5 %all-to-all-done.6 = bf16[4,192,2048]{2,1,0:T(8,128)(2,1)S(1)} async-done(((bf16[4,192,2048]{2,1,0:T(8,128)(2,1)}), bf16[4,192,2048]{2,1,0:T(8,128)(2,1)S(1)}, u32[]{:S(2)}, u32[]{:S(2)}) %all-to-all-start.6) | async-done | bytes 3145760 | tf_op jit(solution)/shard_map/all_to_all | solution.py:462
  748.1 4.4 all-to-all-start.5
  752.5 5.7 fusion.11
  761.7 3.0 multiply_subtract_fusion.1
  765.4 28.9 %all-to-all-done.5 = bf16[4,296,768]{2,1,0:T(8,128)(2,1)} async-done(((bf16[4,296,768]{2,1,0:T(8,128)(2,1)}), bf16[4,296,768]{2,1,0:T(8,128)(2,1)}, u32[]{:S(2)}, u32[]{:S(2)}) %all-to-all-start.5) | async-done | bytes 1818656 | tf_op jit(solution)/shard_map/all_to_all | solution.py:462
  796.3 6.8 multiply_subtract_fusion
  804.8 2.6 multiply_subtract_fusion.4
  807.4 1.9 multiply_subtract_fusion.5
  (179 shorter events, 46.6 us)
Async XLA Ops:
  7.2 5.2 copy-start.3
  7.2 72.7 %all-gather.14.cloned.1.call-start = ((), (), s32[]{:S(2)}) async-start(), calls=%async_computation.11 | async-start | bytes 5271552 | tf_op jit(solution)/shard_map/all_gather | solution.py:490
  11.6 4.2 copy-start.12
  12.3 4.2 copy-start.25
  12.3 187.8 %all-gather.12.cloned.1.call-start = ((), (), s32[]{:S(2)}) async-start(), calls=%async_computation.10 | async-start | bytes 3538944 | tf_op jit(solution)/shard_map/all_gather | solution.py:490
  13.3 186.8 %all-gather.16.cloned.1.call-start = ((), (), s32[]{:S(2)}) async-start(), calls=%async_computation.12 | async-start | bytes 7077888 | tf_op jit(solution)/shard_map/all_gather | solution.py:490
  15.7 358.4 %all-gather.10.cloned.1.call-start = ((), (), s32[]{:S(2)}) async-start(), calls=%async_computation.9 | async-start | bytes 3244032 | tf_op jit(solution)/shard_map/all_gather | solution.py:490
  85.0 5.0 copy-start.22
  148.8 44.8 %all-to-all-start = ((bf16[4,576,768]{2,1,0:T(8,128)(2,1)}), bf16[4,576,768]{2,1,0:T(8,128)(2,1)S(1)}, u32[]{:S(2)}, u32[]{:S(2)}) async-start(bf16[4,576,768]{2,1,0:T(8,128)(2,1)} %get-tuple-element.57), calls=%async_computation | async-start | bytes 7077888 | tf_op jit(solution)/shard_map/all_to_all | solution.py:543
  152.5 221.7 %all-gather.8.cloned.1.call-start = ((), (), s32[]{:S(2)}) async-start(), calls=%async_computation.8 | async-start | bytes 6488064 | tf_op jit(solution)/shard_map/all_gather | solution.py:490
  195.3 53.5 %all-to-all-start.1 = ((bf16[4,576,768]{2,1,0:T(8,128)(2,1)}), bf16[4,576,768]{2,1,0:T(8,128)(2,1)}, u32[]{:S(2)}, u32[]{:S(2)}) async-start(bf16[4,576,768]{2,1,0:T(8,128)(2,1)} %get-tuple-element.58), calls=%async_computation.1 | async-start | bytes 7077888 | tf_op jit(solution)/shard_map/all_to_all | solution.py:543
  326.8 8.8 %copy-start = (bf16[2,16,144,384]{3,2,1,0:T(8,128)(2,1)S(1)}, bf16[2,16,144,384]{3,2,1,0:T(8,128)(2,1)}, u32[]{:S(2)}) copy-start(bf16[2,16,144,384]{3,2,1,0:T(8,128)(2,1)} %slice.89) | copy-start | bytes 10616836
  326.8 43.6 %all-to-all-start.2 = ((bf16[4,576,768]{2,1,0:T(8,128)(2,1)}), bf16[4,576,768]{2,1,0:T(8,128)(2,1)}, u32[]{:S(2)}, u32[]{:S(2)}) async-start(bf16[4,576,768]{2,1,0:T(8,128)(2,1)} %bitcast.147), calls=%async_computation.2 | async-start | bytes 7077888 | tf_op jit(solution)/shard_map/all_to_all | solution.py:548
  370.4 60.5 %all-to-all-start.3 = ((bf16[4,576,768]{2,1,0:T(8,128)(2,1)}), bf16[4,576,768]{2,1,0:T(8,128)(2,1)S(1)}, u32[]{:S(2)}, u32[]{:S(2)}) async-start(bf16[4,576,768]{2,1,0:T(8,128)(2,1)} %bitcast.22), calls=%async_computation.3 | async-start | bytes 7077888 | tf_op jit(solution)/shard_map/all_to_all | solution.py:549
  456.9 38.6 %copy-start.2 = (bf16[1,1024,768]{2,1,0:T(8,128)(2,1)S(1)}, bf16[1,1024,768]{2,1,0:T(8,128)(2,1)}, u32[]{:S(2)}) copy-start(bf16[1,1024,768]{2,1,0:T(8,128)(2,1)} %param.28) | copy-start | bytes 4718596
  456.9 38.6 %copy-start.23 = (f32[1024]{0:T(1024)S(1)}, f32[1024]{0:T(1024)}, u32[]{:S(2)}) copy-start(f32[1024]{0:T(1024)} %add_rsqrt_fusion) | copy-start | bytes 12292
  495.5 8.2 %copy-start.5 = (bf16[3,768,768]{2,1,0:T(8,128)(2,1)S(1)}, bf16[3,768,768]{2,1,0:T(8,128)(2,1)}, u32[]{:S(2)}) copy-start(bf16[3,768,768]{2,1,0:T(8,128)(2,1)} %reshape.295) | copy-start | bytes 10616836
  495.5 8.2 %copy-start.33 = (bf16[3,1024,768]{2,1,0:T(8,128)(2,1)S(1)}, bf16[3,1024,768]{2,1,0:T(8,128)(2,1)}, u32[]{:S(2)}) copy-start(bf16[3,1024,768]{2,1,0:T(8,128)(2,1)} %attention_backward.1) | copy-start | bytes 14155780
  511.5 4.4 copy-start.32
  513.8 4.7 slice-start
  518.5 3.1 copy-start.9
  524.3 6.6 copy-start.8
  530.9 18.6 %collective-permute-start = (bf16[16,296,768]{2,1,0:T(8,128)(2,1)}, bf16[16,296,768]{2,1,0:T(8,128)(2,1)}, u32[]{:S(2)}, u32[]{:S(2)}) collective-permute-start(bf16[16,296,768]{2,1,0:T(8,128)(2,1)} %dynamic-slice_bitcast_fusion), channel_id=1, source_target_pairs={{0,16},{16,0},{1,17},{17,1},{2,18},{18,2},{3,19},{19,3},{4,20},{20... | collective-permute-start | bytes 21823496 | tf_op jit(solution)/shard_map/ppermute | solution.py:455
  531.0 12.0 %collective-permute-start.4 = (bf16[4,256,768]{2,1,0:T(8,128)(2,1)S(1)}, bf16[4,256,768]{2,1,0:T(8,128)(2,1)S(1)}, u32[]{:S(2)}, u32[]{:S(2)}) collective-permute-start(bf16[4,256,768]{2,1,0:T(8,128)(2,1)S(1)} %dynamic-slice_bitcast_fusion.2), channel_id=1, source_target_pairs={{0,16},{16,0},{1,17},{17,1},{2,18},{18,2},{3,19},{19,3},{4,20},{20... | collective-permute-start | bytes 4718600 | tf_op jit(solution)/shard_map/ppermute | solution.py:455
  544.6 42.4 %all-to-all-start.7 = ((bf16[4,256,768]{2,1,0:T(8,128)(2,1)}), bf16[4,256,768]{2,1,0:T(8,128)(2,1)S(1)}, u32[]{:S(2)}, u32[]{:S(2)}) async-start(bf16[4,256,768]{2,1,0:T(8,128)(2,1)} %fusion.16), calls=%async_computation.7 | async-start | bytes 3145728 | tf_op jit(solution)/shard_map/all_to_all | solution.py:462
  588.1 85.7 %all-to-all-start.4 = ((bf16[4,4,296,768]{3,2,1,0:T(8,128)(2,1)}), bf16[4,4,296,768]{3,2,1,0:T(8,128)(2,1)}, u32[]{:S(2)}, u32[]{:S(2)}) async-start(bf16[4,4,296,768]{3,2,1,0:T(8,128)(2,1)} %bitcast.125), calls=%async_computation.4 | async-start | bytes 14548992 | tf_op jit(solution)/shard_map/all_to_all | solution.py:460
  597.2 5.7 collective-permute-start.2
  673.9 74.3 %all-to-all-start.6 = ((bf16[4,192,2048]{2,1,0:T(8,128)(2,1)}), bf16[4,192,2048]{2,1,0:T(8,128)(2,1)S(1)}, u32[]{:S(2)}, u32[]{:S(2)}) async-start(bf16[4,192,2048]{2,1,0:T(8,128)(2,1)} %fusion.1), calls=%async_computation.6 | async-start | bytes 6291456 | tf_op jit(solution)/shard_map/all_to_all | solution.py:462
  680.8 79.7 %collective-permute-start.5 = (f32[256,768]{1,0:T(8,128)}, f32[256,768]{1,0:T(8,128)}, u32[]{:S(2)}, u32[]{:S(2)}) collective-permute-start(f32[256,768]{1,0:T(8,128)} %convert_reduce_fusion.2), channel_id=1, source_target_pairs={{0,16},{16,0},{1,17},{17,1},{2,18},{18,2},{3,19},{19,3},{4,20},{20... | collective-permute-start | bytes 2359304 | tf_op jit(solution)/shard_map/ppermute | solution.py:467
  748.1 46.2 %all-to-all-start.5 = ((bf16[4,296,768]{2,1,0:T(8,128)(2,1)}), bf16[4,296,768]{2,1,0:T(8,128)(2,1)}, u32[]{:S(2)}, u32[]{:S(2)}) async-start(bf16[4,296,768]{2,1,0:T(8,128)(2,1)} %reduce_sum.69), calls=%async_computation.5 | async-start | bytes 3637248 | tf_op jit(solution)/shard_map/all_to_all | solution.py:462
  758.8 2.8 copy-start.4
  758.9 2.8 copy-start.13
  758.9 6.3 collective-permute-start.3
  796.2 7.1 collective-permute-start.1
  803.4 3.9 copy-start.18
  804.8 4.5 copy-start.15
  804.8 4.5 copy-start.16
  804.8 4.5 copy-start.17
  807.3 3.9 copy-start.10
  807.3 3.9 copy-start.11
  807.4 3.9 copy-start.20
  807.4 3.8 copy-start.21
  809.3 3.2 copy-start.24
  809.3 3.2 copy-start.26
  809.3 3.2 copy-start.27
  809.4 3.8 copy-start.28
  809.4 3.8 copy-start.29
  809.4 3.8 copy-start.30
  (7 other events, 13.0 us)
Sparse Core Ops, SparseCore 0:
  12.4 67.4 all-gather.13
  82.1 37.1 all-gather.11
  121.5 63.6 all-gather.15
  188.6 67.2 all-gather.9
  259.2 67.9 all-gather.7

commit v2 on v1

--- a/solution.py
+++ b/solution.py
@@ -51,11 +51,47 @@
     return whole_spec(shape, pipeline_mode=pl.Buffered(1))
 
 
+MESH = pl.DeviceIdType.MESH
+ANY = pl.BlockSpec(memory_space=pl.ANY)
+
+
+def greet(targets):
+    barrier = pltpu.get_barrier_semaphore()
+    for target in targets:
+        pl.semaphore_signal(barrier, inc=1, device_id=target, device_id_type=MESH)
+    pl.semaphore_wait(barrier, len(targets))
+
+
+def send(src, dst, send_sem, recv_sem, target):
+    return pltpu.make_async_remote_copy(
+        src_ref=src, dst_ref=dst, send_sem=send_sem, recv_sem=recv_sem,
+        device_id=target, device_id_type=MESH,
+    )
+
+
 def forward_kernel(
-    tok_ref, bidr_ref, bidc_ref, gains_ref, wa_ref, wo_ref, wr_ref, wrt_ref,
-    qkv_ref, lse_ref, o_ref, mid_ref, h2_ref, probs_ref, probst_ref, h1_ref,
+    exps,
+    tok_ref, bidr_ref, bidc_ref, gains_ref, wa_ref, wo_ref, wr_ref, wrt_ref, slots_ref,
+    qkv_ref, lse_ref, o_ref, mid_ref, h2_ref, probs_ref, probst_ref, landed_ref, h1_ref,
+    send_sem, recv_sem,
 ):
     pair = pl.program_id(0)
+    me = lax.axis_index("exp")
+
+    def copies():
+        made = [pltpu.make_async_copy(slots_ref.at[me], landed_ref.at[0], send_sem.at[0])]
+        for k in range(1, exps):
+            peer = lax.bitwise_xor(me, k)
+            made.append(
+                send(slots_ref.at[peer], landed_ref.at[k], send_sem.at[k], recv_sem.at[k], {"exp": peer})
+            )
+        return made
+
+    @pl.when(pair == 0)
+    def _():
+        greet([{"exp": lax.bitwise_xor(me, k)} for k in range(1, exps)])
+        for copy in copies():
+            copy.start()
     seq, width = tok_ref.shape
     tile = 256
 
@@ -123,14 +159,17 @@
         logits = jnp.where(spot < 4, logits, masked_score)
         e = jnp.exp(logits - jnp.max(logits, axis=0, keepdims=True))
         probst_ref[...] = e / jnp.sum(e, axis=0, keepdims=True)
-
-
-def attention_forward(tokens, bid_row, bid_col, gains, wa, wo, wr, wrt):
+        for copy in copies():
+            copy.wait()
+
+
+def attention_forward(tokens, bid_row, bid_col, gains, wa, wo, wr, wrt, slots):
+    exps = slots.shape[0]
     seq, width = tokens.shape
     pairs = width // 128
     per_half = pairs // 2
     return pl.pallas_call(
-        forward_kernel,
+        functools.partial(forward_kernel, exps),
         grid=(pairs,),
         in_specs=[
             once((seq, width)),
@@ -144,6 +183,7 @@
             once(wo.shape),
             once(wr.shape),
             once(wrt.shape),
+            ANY,
         ],
         out_specs=[
             pl.BlockSpec((3, seq, 128), lambda i: (0, 0, i)),
@@ -153,6 +193,7 @@
             whole_spec((seq, width)),
             whole_spec((seq, 128)),
             whole_spec((16, seq)),
+            ANY,
         ],
         out_shape=[
             jax.ShapeDtypeStruct((3, seq, width), bf16),
@@ -162,58 +203,263 @@
             jax.ShapeDtypeStruct((seq, width), bf16),
             jax.ShapeDtypeStruct((seq, 128), f32),
             jax.ShapeDtypeStruct((16, seq), f32),
-        ],
-        scratch_shapes=[pltpu.VMEM((seq, width), bf16)],
-        compiler_params=params(("arbitrary",)),
+            jax.ShapeDtypeStruct(slots.shape, bf16),
+        ],
+        scratch_shapes=[
+            pltpu.VMEM((seq, width), bf16),
+            pltpu.SemaphoreType.DMA((exps,)),
+            pltpu.SemaphoreType.DMA((exps,)),
+        ],
+        compiler_params=params(("arbitrary",), collective_id=1, has_side_effects=True),
         cost_estimate=pl.CostEstimate(
             flops=30_000_000_000, bytes_accessed=20_000_000, transcendentals=12_000_000
         ),
         name="attention_forward",
-    )(tokens, bid_row, bid_col, gains, wa, wo, wr, wrt)
-
-
-def dispatch_kernel(h2_ref, g_ref, place_ref, probst_ref, rows_ref, grads_ref):
+    )(tokens, bid_row, bid_col, gains, wa, wo, wr, wrt, slots)
+
+
+def slots_of(place_row, cap):
+    slot = lax.broadcasted_iota(jnp.int32, (cap, place_row.shape[1]), 0)
+    return (slot == place_row).astype(f32).astype(bf16)
+
+
+def place_kernel(g_ref, place_ref, rows_ref):
+    hot = slots_of(place_ref[pl.ds(pl.program_id(0), 1), :], rows_ref.shape[1])
+    rows_ref[0] = mm(hot, g_ref[...]).astype(bf16)
+
+
+def place_gradients(g, place_row, experts_all, cap):
+    return pl.pallas_call(
+        place_kernel,
+        grid=(experts_all,),
+        in_specs=[once(g.shape), once(place_row.shape)],
+        out_specs=pl.BlockSpec((1, cap, g.shape[1]), lambda e: (e, 0, 0)),
+        out_shape=jax.ShapeDtypeStruct((experts_all, cap, g.shape[1]), bf16),
+        compiler_params=params(("arbitrary",)),
+        cost_estimate=pl.CostEstimate(
+            flops=4_000_000_000, bytes_accessed=6_000_000, transcendentals=0
+        ),
+        name="place_gradients",
+    )(g, place_row)
+
+
+def dispatch_kernel(h2_ref, place_ref, probst_ref, rows_ref, chosen_ref):
     expert = pl.program_id(0)
-    seq = h2_ref.shape[0]
     cap = rows_ref.shape[1]
-    slot = lax.broadcasted_iota(jnp.int32, (cap, seq), 0)
-    hit = slot == place_ref[pl.ds(expert, 1), :]
-    chosen = jnp.sum(
-        jnp.where(hit, probst_ref[pl.ds(expert, 1), :], 0.0), axis=1, keepdims=True
-    )
-    hot = hit.astype(f32).astype(bf16)
-    rows_ref[0] = mm(hot, h2_ref[...]).astype(bf16)
-    grads_ref[0] = (mm(hot, g_ref[...]) * chosen).astype(bf16)
-
-
-def dispatch(h2, g, place_row, probst, experts_all, cap):
+    lanes = chosen_ref.shape[2]
+    row = place_ref[pl.ds(expert, 1), :]
+    rows_ref[0] = mm(slots_of(row, cap), h2_ref[...]).astype(bf16)
+    value = probst_ref[pl.ds(expert, 1), :]
+    high = value.astype(bf16)
+    rest = value - high.astype(f32)
+    middle = rest.astype(bf16)
+    low = (rest - middle.astype(f32)).astype(bf16)
+    eight = lambda a: jnp.broadcast_to(a.astype(f32), (8, row.shape[1])).astype(bf16)
+    hot = slots_of(row, lanes)
+    chosen = mm_nt(eight(high), hot) + mm_nt(eight(middle), hot) + mm_nt(eight(low), hot)
+    chosen_ref[0] = chosen
+
+
+def dispatch(h2, place_row, probst, experts_all, cap, lanes):
     seq, width = h2.shape
     return pl.pallas_call(
         dispatch_kernel,
         grid=(experts_all,),
-        in_specs=[once(h2.shape), once(g.shape), once(place_row.shape), once(probst.shape)],
-        out_specs=[pl.BlockSpec((1, cap, width), lambda e: (e, 0, 0))] * 2,
-        out_shape=[jax.ShapeDtypeStruct((experts_all, cap, width), bf16)] * 2,
+        in_specs=[once(h2.shape), once(place_row.shape), once(probst.shape)],
+        out_specs=[
+            pl.BlockSpec((1, cap, width), lambda e: (e, 0, 0)),
+            pl.BlockSpec((1, 8, lanes), lambda e: (e, 0, 0)),
+        ],
+        out_shape=[
+            jax.ShapeDtypeStruct((experts_all, cap, width), bf16),
+            jax.ShapeDtypeStruct((experts_all, 8, lanes), f32),
+        ],
         compiler_params=params(("arbitrary",)),
         cost_estimate=pl.CostEstimate(
-            flops=8_000_000_000, bytes_accessed=10_000_000, transcendentals=0
+            flops=5_000_000_000, bytes_accessed=6_000_000, transcendentals=0
         ),
         name="dispatch",
-    )(h2, g, place_row, probst)
+    )(h2, place_row, probst)
+
+
+def gated(x, g, wg, wu, wn):
+    gate, up = mm(x, wg), mm(x, wu)
+    sig = 1.0 / (1.0 + jnp.exp(-gate))
+    active = gate * sig
+    slope = sig * (1.0 + gate * (1.0 - sig))
+    hidden = (active * up).astype(bf16)
+    hgrad = mm_nt(g, wn)
+    return hidden, (hgrad * up * slope).astype(bf16), (hgrad * active).astype(bf16)
+
+
+def routed_kernel(
+    exps, shds,
+    rows_ref, chosen_ref, grads_ref, we_ref, wn_ref,
+    eout_ref, ein_ref, sums_ref,
+    x_s, g_s, c_s, w_s, n_s, hid_s, gg_s, ug_s, out_s, gin_s, acc_o, acc_i,
+    load_sem, x_send, x_recv, c_send, c_recv, o_send, o_recv, i_send, i_recv, w_sem,
+):
+    me = lax.axis_index("exp")
+    _, cap, width = x_s.shape
+    hidden = hid_s.shape[1]
+    rows_all = exps * cap
+    peers = [lax.bitwise_xor(me, k) for k in range(exps)]
+    greet([{"exp": peer} for peer in peers[1:]])
+
+    chosen, arriving = [], []
+    for k in range(1, exps):
+        target = {"exp": peers[k]}
+        chosen.append(send(chosen_ref.at[peers[k]], c_s.at[k], c_send.at[k], c_recv.at[k], target))
+        arriving.append(send(rows_ref.at[peers[k]], x_s.at[k], x_send.at[k], x_recv.at[k], target))
+    for copy in chosen + arriving:
+        copy.start()
+    loads = [
+        pltpu.make_async_copy(rows_ref.at[me], x_s.at[0], load_sem.at[0]),
+        pltpu.make_async_copy(chosen_ref.at[me], c_s.at[0], load_sem.at[1]),
+        pltpu.make_async_copy(grads_ref, g_s, load_sem.at[2]),
+        pltpu.make_async_copy(we_ref, w_s, load_sem.at[3]),
+        pltpu.make_async_copy(wn_ref, n_s, load_sem.at[4]),
+    ]
+    for copy in loads:
+        copy.start()
+    for copy in loads:
+        copy.wait()
+
+    ft = 256
+    returns = []
+    for k in range(exps):
+        if k:
+            chosen[k - 1].wait()
+            arriving[k - 1].wait()
+        scale = c_s[k].T[:cap, 0:1]
+        g_s[k] = (g_s[k].astype(f32) * scale).astype(bf16)
+        acc_o[...] = jnp.zeros_like(acc_o)
+        acc_i[...] = jnp.zeros_like(acc_i)
+
+        @pl.loop(0, hidden // ft)
+        def _(f):
+            columns = pl.ds(pl.multiple_of(f * ft, ft), ft)
+            wg = w_s[0, :, :, columns].reshape(width, ft)
+            wu = w_s[1, :, :, columns].reshape(width, ft)
+            wn = n_s[f // 2, f % 2]
+            hid, gg, ug = gated(x_s[k], g_s[k], wg, wu, wn)
+            hid_s[pl.ds(k * cap, cap), columns] = hid
+            gg_s[pl.ds(k * cap, cap), columns] = gg
+            ug_s[pl.ds(k * cap, cap), columns] = ug
+            acc_o[...] += mm(hid, wn)
+            acc_i[...] += mm_nt(gg, wg) + mm_nt(ug, wu)
+
+        out_s[k] = acc_o[...].astype(bf16)
+        gin_s[k] = acc_i[...].astype(bf16)
+        if k:
+            target = {"exp": peers[k]}
+            made = [
+                send(out_s.at[k], eout_ref.at[me], o_send.at[k], o_recv.at[k], target),
+                send(gin_s.at[k], ein_ref.at[me], i_send.at[k], i_recv.at[k], target),
+            ]
+        else:
+            made = [
+                pltpu.make_async_copy(out_s.at[0], eout_ref.at[me], o_send.at[0]),
+                pltpu.make_async_copy(gin_s.at[0], ein_ref.at[me], i_send.at[0]),
+            ]
+        for copy in made:
+            copy.start()
+        returns.extend(made)
+
+    wide = hidden // shds
+
+    @pl.loop(0, shds)
+    def _(f):
+        columns = pl.ds(pl.multiple_of(f * wide, wide), wide)
+        x = x_s[...].reshape(rows_all, width)
+        g = g_s[...].reshape(rows_all, width)
+        part = w_s.shape[1:3] + (wide,)
+        w_s[0, :, :, columns] = mm_tn(x, gg_s[:, columns]).astype(bf16).reshape(part)
+        w_s[1, :, :, columns] = mm_tn(x, ug_s[:, columns]).astype(bf16).reshape(part)
+        n_s[f] = mm_tn(hid_s[:, columns], g).astype(bf16).reshape(n_s.shape[1:])
+
+    stores = []
+    deep = w_s.shape[2]
+    base = hidden // 256 * deep
+    tall = n_s.shape[2]
+    for c in range(2):
+        for b in range(hidden // 256):
+            stores.append((w_s.at[c, :, :, pl.ds(256 * b, 256)], sums_ref.at[c, :, pl.ds(b * deep, deep), :]))
+        for b in range(width // 256):
+            stores.append((n_s.at[:, c, :, pl.ds(256 * b, 256)], sums_ref.at[c, :, pl.ds(base + b * tall, tall), :]))
+    stores = [pltpu.make_async_copy(a, b, w_sem.at[i]) for i, (a, b) in enumerate(stores)]
+    for copy in stores:
+        copy.start()
+    for copy in stores + returns:
+        copy.wait()
+
+
+def routed(slot_rows, chosen, grads, w_experts, w_narrower, shds):
+    exps, cap, width = slot_rows.shape
+    hidden = w_experts.shape[2]
+    deep, tall = width // shds, hidden // shds // 2
+    height = hidden // 256 * deep + width // 256 * tall
+    big = lambda *shape: pltpu.VMEM(shape, bf16)
+    sems = lambda n: pltpu.SemaphoreType.DMA((n,))
+    return pl.pallas_call(
+        functools.partial(routed_kernel, exps, shds),
+        in_specs=[ANY] * 5,
+        out_specs=[ANY] * 3,
+        out_shape=[
+            jax.ShapeDtypeStruct((exps, cap, width), bf16),
+            jax.ShapeDtypeStruct((exps, cap, width), bf16),
+            jax.ShapeDtypeStruct((2, shds, height, 256), bf16),
+        ],
+        scratch_shapes=[
+            big(exps, cap, width),
+            big(exps, cap, width),
+            pltpu.VMEM(chosen.shape, f32),
+            big(2, shds, deep, hidden),
+            big(shds, 2, tall, width),
+            big(exps * cap, hidden),
+            big(exps * cap, hidden),
+            big(exps * cap, hidden),
+            big(exps, cap, width),
+            big(exps, cap, width),
+            pltpu.VMEM((cap, width), f32),
+            pltpu.VMEM((cap, width), f32),
+            sems(5), sems(exps), sems(exps), sems(exps), sems(exps),
+            sems(exps), sems(exps), sems(exps), sems(exps),
+            sems(2 * (hidden // 256 + width // 256)),
+        ],
+        compiler_params=params(collective_id=2, has_side_effects=True),
+        cost_estimate=pl.CostEstimate(
+            flops=18 * exps * cap * width * hidden,
+            bytes_accessed=40_000_000,
+            transcendentals=exps * cap * hidden,
+        ),
+        name="routed",
+    )(
+        slot_rows, chosen, grads,
+        w_experts.reshape(2, shds, deep, hidden),
+        w_narrower.reshape(shds, 2, tall, width),
+    )
 
 
 def ffn_kernel(
-    x_ref, g_ref, wg_ref, wu_ref, wn_ref,
-    out_ref, gin_ref, dwg_ref, dwu_ref, dwn_ref,
-    acc_out, acc_gin, hid_s, gg_s, ug_s,
+    x_ref, g_ref, wg_ref, wu_ref, wn_ref, sums_ref,
+    out_ref, gin_ref, dwg_ref, dwu_ref, dwn_ref, swapped_ref,
+    acc_out, acc_gin, hid_s, gg_s, ug_s, send_sem, recv_sem,
     *, tile,
 ):
     f = pl.program_id(0)
     last = pl.num_programs(0) - 1
     rows_all = x_ref.shape[0]
+    group = lax.axis_index("grp")
+    partner = {"grp": lax.bitwise_xor(group, 1)}
+    swap = lambda: send(
+        sums_ref.at[1 - lax.rem(group, 2)], swapped_ref, send_sem, recv_sem, partner
+    )
 
     @pl.when(f == 0)
     def _():
+        greet([partner])
+        swap().start()
         acc_out[...] = jnp.zeros_like(acc_out)
         acc_gin[...] = jnp.zeros_like(acc_gin)
 
@@ -221,14 +467,7 @@
     for row in range(0, rows_all, tile):
         rows = pl.ds(row, tile)
         x, g = x_ref[rows, :], g_ref[rows, :]
-        gate, up = mm(x, wg), mm(x, wu)
-        sig = 1.0 / (1.0 + jnp.exp(-gate))
-        active = gate * sig
-        slope = sig * (1.0 + gate * (1.0 - sig))
-        hidden = (active * up).astype(bf16)
-        hgrad = mm_nt(g, wn)
-        gg = (hgrad * up * slope).astype(bf16)
-        ug = (hgrad * active).astype(bf16)
+        hidden, gg, ug = gated(x, g, wg, wu, wn)
         hid_s[rows, :], gg_s[rows, :], ug_s[rows, :] = hidden, gg, ug
         acc_out[rows, :] += mm(hidden, wn)
         acc_gin[rows, :] += mm_nt(gg, wg) + mm_nt(ug, wu)
@@ -240,9 +479,10 @@
     def _():
         out_ref[...] = acc_out[...].astype(out_ref.dtype)
         gin_ref[...] = acc_gin[...].astype(gin_ref.dtype)
-
-
-def ffn(x, g, wgu, wn, out_type, tile, name):
+        swap().wait()
+
+
+def ffn(x, g, wgu, wn, sums, out_type, tile, name):
     rows, width = x.shape
     hidden = wn.shape[0]
     ft = 512
@@ -255,6 +495,7 @@
             pl.BlockSpec((1, width, ft), lambda f: (0, 0, f)),
             pl.BlockSpec((1, width, ft), lambda f: (1, 0, f)),
             pl.BlockSpec((ft, width), lambda f: (f, 0)),
+            ANY,
         ],
         out_specs=[
             once((rows, width)),
@@ -262,6 +503,7 @@
             pl.BlockSpec((1, width, ft), lambda f: (0, 0, f)),
             pl.BlockSpec((1, width, ft), lambda f: (0, 0, f)),
             pl.BlockSpec((ft, width), lambda f: (f, 0)),
+            ANY,
         ],
         out_shape=[
             jax.ShapeDtypeStruct((rows, width), out_type),
@@ -269,6 +511,7 @@
             jax.ShapeDtypeStruct((1, width, hidden), bf16),
             jax.ShapeDtypeStruct((1, width, hidden), bf16),
             jax.ShapeDtypeStruct((hidden, width), bf16),
+            jax.ShapeDtypeStruct(sums.shape[1:], bf16),
         ],
         scratch_shapes=[
             pltpu.VMEM((rows, width), f32),
@@ -276,15 +519,17 @@
             pltpu.VMEM((rows, ft), bf16),
             pltpu.VMEM((rows, ft), bf16),
             pltpu.VMEM((rows, ft), bf16),
-        ],
-        compiler_params=params(("arbitrary",)),
+            pltpu.SemaphoreType.DMA,
+            pltpu.SemaphoreType.DMA,
+        ],
+        compiler_params=params(("arbitrary",), collective_id=3, has_side_effects=True),
         cost_estimate=pl.CostEstimate(
             flops=18 * rows * width * hidden,
             bytes_accessed=12 * width * hidden + 8 * rows * width,
             transcendentals=rows * hidden,
         ),
         name=name,
-    )(x, g, wgu, wgu, wn)
+    )(x, g, wgu, wgu, wn, sums)
 
 
 def combine_kernel(
@@ -459,8 +704,12 @@
         part = part.reshape((size, part.shape[0] // size) + part.shape[1:])
         part = lax.all_to_all(part, axis, 0, 0, tiled=True)
         part = sum_parts(part).astype(bf16)
-    part = sum_parts(lax.all_to_all(part, axes[-1], 0, 0, tiled=True))
-    both = jnp.zeros((2,) + part.shape, f32)
+    return share(sum_parts(lax.all_to_all(part, axes[-1], 0, 0, tiled=True)), groups, core)
+
+
+def share(part, groups, core):
+    swap = [(i, i ^ 1) for i in range(groups)]
+    both = jnp.zeros((2,) + part.shape, part.dtype)
     both = lax.dynamic_update_index_in_dim(both, part, core, 0)
     if groups > 2:
         return lax.psum(both, "grp")
@@ -535,18 +784,16 @@
     bid_row = jnp.broadcast_to(bid, (8, seq))
     bid_col = jnp.broadcast_to(bid.reshape(seq, 1), (seq, 256))
 
-    qkv, lse, o, mid, h2, probs, probst = attention_forward(
-        tokens, bid_row, bid_col, gains, wa, wo, wr, wrt
-    )
-    slot_rows, slot_grad = dispatch(h2, g, place_row, probst, experts_all, CAP)
-    swap_rows = functools.partial(lax.all_to_all, axis_name="exp", split_axis=0, concat_axis=0, tiled=True)
-    received, back_rows = swap_rows(slot_rows), swap_rows(slot_grad)
-    sout, sin, dsg, dsu, dsn = ffn(h2, g, w_widener, w_reducer, f32, 256, "shared")
-    eout, ein, dwg, dwu, dwn = ffn(
-        received.reshape(-1, width), back_rows.reshape(-1, width), w_experts, w_narrower, bf16, 384, "routed"
-    )
-    eout = swap_rows(eout.reshape(experts_all, CAP, width))
-    ein = swap_rows(ein.reshape(experts_all, CAP, width))
+    lanes = -(-CAP // 128) * 128
+    g_slots = place_gradients(g, place_row, experts_all, CAP)
+    qkv, lse, o, mid, h2, probs, probst, g_landed = attention_forward(
+        tokens, bid_row, bid_col, gains, wa, wo, wr, wrt, g_slots
+    )
+    slot_rows, chosen = dispatch(h2, place_row, probst, experts_all, CAP, lanes)
+    eout, ein, sums = routed(slot_rows, chosen, g_landed, w_experts, w_narrower, shds)
+    sout, sin, dsg, dsu, dsn, swapped = ffn(h2, g, w_widener, w_reducer, sums, f32, 256, "shared")
+    part = (pick(sums, 0, core).astype(f32) + swapped.astype(f32)).astype(bf16)
+    part = lax.psum_scatter(part, "shd", scatter_dimension=0, tiled=False)
     block_out, mid_grad, midb, og, gain_two, rgrad = combine(
         mid, sout, sin, g, h2, probs, place_col, eout, ein, gains, wr, wo
     )
@@ -564,12 +811,13 @@
     d1 = h1_grad * gains[0:1]
     input_grad = mid_grad + r1 * (d1 - n1 * jnp.mean(d1 * n1, axis=1, keepdims=True))
 
-    g_experts = reduce_scatter(
-        jnp.concatenate([dwg, dwu], axis=0).reshape(2, shds, width // shds, hidden), ("shd",), groups, core
-    )
-    g_narrower = reduce_scatter(
-        dwn.reshape(shds, 2, -1, width).transpose(1, 0, 2, 3), ("shd",), groups, core
-    )
+    expert_sums = share(part, groups, core)
+    deep = width // shds
+    cut_at = hidden // 256 * deep
+    g_experts = expert_sums[:, :cut_at].reshape(2, hidden // 256, deep, 256)
+    g_experts = g_experts.transpose(0, 2, 1, 3).reshape(2, deep, hidden)
+    g_narrower = expert_sums[:, cut_at:].reshape(2, width // 256, -1, 256)
+    g_narrower = g_narrower.transpose(0, 2, 1, 3)
     small = jnp.concatenate(
         [rgrad[:experts_all], gain_one[None, :], gain_two[0:1]], axis=0
     ).reshape(-1, spread, rows).transpose(1, 0, 2).reshape(spread, 1, -1)

time: 825 us -> 708 us (0.86)
  waiting for transfers between devices: 372 us -> 106 us
  blocking collectives: 0 us -> 88.9 us
  Pallas kernels: 236 us -> 302 us
  starting transfers between devices: 37.3 us -> 5.19 us
  local copies, waits for them, and re-layouts: 80.5 us -> 109 us
    all_to_all x8 -> x1, waiting for transfers between devices: 294 us -> 0.01 us  [reduce_scatter(): lax.all_to_all(part, axes[-1], 0, 0, tiled=True)]
    pallas_call x1 -> x3, Pallas kernels: 45.9 us -> 190 us  [the longest x1 135 us: routed(): pl.pallas_call(functools.partial(routed_kernel, exps, shds), in_specs=[AN...]
    all_to_all x0 -> x1, blocking collectives: none -> 88.9 us  [reduce_scatter(): part = lax.all_to_all(part, axis, 0, 0, tiled=True)]
    pallas_call x2 -> x1, Pallas kernels: 116 us -> 38.6 us  [ffn(): pl.pallas_call(functools.partial(ffn_kernel, tile=tile), grid=(hidden //...]
    all_gather x5, waiting for transfers between devices: 60.9 us -> 100 us  [gather(): lax.all_gather(part, names, axis=0, tiled=False).reshape((-1,) + part.shape)]
    all_to_all x8 -> x1, starting transfers between devices: 36.3 us -> 4.06 us  [reduce_scatter(): lax.all_to_all(part, axes[-1], 0, 0, tiled=True)]
    unnamed x79 -> x97, local copies, waits for them, and re-layouts: 13.8 us -> 26.7 us
    ppermute x3 -> x1, waiting for transfers between devices: 17.1 us -> 5.95 us  [reduce_scatter(): arrived = lax.ppermute(other, 'grp', swap)]
  transfers between devices with their start and end apart: 19 -> 10, of which waited for: 10 -> 4; matrix products, arithmetic and copies ran while one was open for 12% -> 16% of each run, Pallas kernels for 21% -> 29%
where the time goes in v2:
time: 708 us; the launch traced here: 699 us
  Pallas kernels  302 us (43%)
  local copies, waits for them, and re-layouts  109 us (15%)
  waiting for transfers between devices  106 us (15%)
  blocking collectives  88.9 us (13%)
  other arithmetic  56.9 us (8%)
  matrix products  16.2 us (2%)
  between operations  15.2 us (2%)
    pallas_call x1, Pallas kernels, routed(): pl.pallas_call(functools.partial(routed_kernel, exps, shds), in_specs=[AN...  135 us
    all_gather x5, waiting for transfers between devices, gather(): lax.all_gather(part, names, axis=0, tiled=False).reshape((-1,) + part.shape)  100 us
    all_to_all x1, blocking collectives, reduce_scatter(): part = lax.all_to_all(part, axis, 0, 0, tiled=True)  88.9 us
    pallas_call x1, Pallas kernels, attention_forward(): pl.pallas_call(functools.partial(forward_kernel, exps), grid=(pairs,), in...  47.8 us
    pallas_call x1, Pallas kernels, attention_backward(): pl.pallas_call(backward_kernel, grid=(pairs,), in_specs=[pl.BlockSpec((3,...  38.8 us
    pallas_call x1, Pallas kernels, ffn(): pl.pallas_call(functools.partial(ffn_kernel, tile=tile), grid=(hidden //...  38.6 us
    unnamed x97, local copies, waits for them, and re-layouts  26.7 us
    pallas_call x1, Pallas kernels, combine(): pl.pallas_call(combine_kernel, grid=(seq // tile,), in_specs=[by_rows, by...  23.8 us
  transfers between devices with their start and end apart: 10, of which 4 were waited for; matrix products, arithmetic and copies ran while one was open for 16% of the time, Pallas kernels for 29%

profile of v2, /device:TPU:0, one launch (start us, length us, event | category | flops | bytes accessed | tf_op | source)
XLA Modules:
  0.0 699.3 jit_solution(6976993212008139187)
XLA Ops:
  13.3 2.4 dynamic-slice_convert_fusion
  16.6 1.7 dynamic-slice_convert_fusion.1
  21.9 6.7 place_gradients.1.slots_ref
  28.6 51.3 %all-gather.14.cloned.1.call-done = bf16[6656,384]{1,0:T(8,128)(2,1)} async-done(((bf16[208,384]{1,0:T(8,128)(2,1)}), bf16[6656,384]{1,0:T(8,128)(2,1)}) %all-gather.14.cloned.1.call-update) | async-done | bytes 5111824 | tf_op jit(solution)/shard_map/all_gather | solution.py:739
  80.8 2.4 slice.97
  83.2 3.3 slice.98
  92.5 1.7 pad.30.wr_ref
  96.1 5.4 copy.137
  101.5 8.9 %reshape.306 = bf16[3,768,768]{2,1,0:T(8,128)(2,1)} reshape(bf16[3,16,48,2,384]{4,3,2,1,0:T(2,128)(2,1)} %copy.137) | data formatting | bytes 7077888 | tf_op jit(solution)/shard_map/reshape | solution.py:808
  112.9 47.8 %attention_forward.1 = (bf16[3,1024,768]{2,1,0:T(8,128)(2,1)}, f32[6,8,1024]{2,1,0:T(8,128)}, bf16[1024,768]{1,0:T(8,128)(2,1)}, f32[1024,768]{1,0:T(8,128)}, bf...) custom-call(bf16[1024,768]{1,0:T(8,128)(2,1)} %bitcast.125, ...), custom_call_target="tpu_custom_call" | custom-call | flops 30000001024 | bytes 20000000 | tf_op jit(solution)/shard_map/attention_forward/pallas_call | solution.py:171
  160.8 10.5 %dispatch.1 = (bf16[4,576,768]{2,1,0:T(8,128)(2,1)}, f32[4,8,640]{2,1,0:T(8,128)}) custom-call(bf16[1024,768]{1,0:T(8,128)(2,1)} %get-tuple-element.52.h2_ref.x_ref, s32[16,1024]{1,0:T(8,128)} %copy.135.place_ref, f32[16,1024]{1,0:T(8,128)} %get-tuple-element.53.probst_ref), custom_call_target="tpu_custom_call" | custom-call | flops 5000000000 | bytes 6000000 | tf_op jit(solution)/shard_map/dispatch/pallas_call | solution.py:265
  171.3 13.9 %all-gather.16.cloned.1.call-done = bf16[8,1,192,2048]{3,2,1,0:T(8,128)(2,1)} async-done(((bf16[1,1,192,2048]{3,2,1,0:T(8,128)(2,1)}), bf16[8,1,192,2048]{3,2,1,0:T(8,128)(2,1)}) %all-gather.16.cloned.1.call-update) | async-done | bytes 6291472 | tf_op jit(solution)/shard_map/all_gather | solution.py:739
  185.1 135.4 %routed.1 = (bf16[4,576,768]{2,1,0:T(8,128)(2,1)}, bf16[4,576,768]{2,1,0:T(8,128)(2,1)}, bf16[2,4,2304,256]{3,2,1,0:T(8,128)(2,1)}) custom-call(bf16[4,576,768]{2,1,0:T(8,128)(2,1)} %get-tuple-element.54.rows_ref, f32[4,8,640]{2,1,0:T(8,128)} %get-tuple-element.55.chosen_ref, bf16[4,576,768]{2,1,0:T(8,128)(2,1)} %get-tuple-element.56.grads_ref, ...), custom_call_target="tpu_custom_call" | custom-call | flops 65229815808 | bytes 40000000 | tf_op jit(solution)/shard_map/routed/pallas_call | solution.py:404
  320.6 35.1 %all-gather.8.cloned.1.call-done = bf16[32,48,2048]{2,1,0:T(8,128)(2,1)} async-done(((bf16[1,48,2048]{2,1,0:T(8,128)(2,1)}), bf16[32,48,2048]{2,1,0:T(8,128)(2,1)}) %all-gather.8.cloned.1.call-update) | async-done | bytes 6291472 | tf_op jit(solution)/shard_map/all_gather | solution.py:739
  355.7 38.6 %shared.1 = (f32[1024,768]{1,0:T(8,128)}, f32[1024,768]{1,0:T(8,128)}, bf16[1,768,2048]{2,1,0:T(8,128)(2,1)}, bf16[1,768,2048]{2,1,0:T(8,128)(2,1)}, bf16[2048,7...) custom-call(bf16[1024,768]{1,0:T(8,128)(2,1)} %get-tuple-element.52.h2_ref.x_ref, bf16[1024,768]{1,0:T(8,128)(2,1)} %bitcast.159, ...), custom_call_target="tpu_custom_call" | custom-call | flops 28991029248 | bytes 25165824 | tf_op jit(solution)/shard_map/shared/pallas_call | solution.py:489
  394.4 23.8 %combine.1 = (bf16[1024,768]{1,0:T(8,128)(2,1)}, f32[1024,768]{1,0:T(8,128)}, bf16[1024,768]{1,0:T(8,128)(2,1)}, bf16[1024,768]{1,0:T(8,128)(2,1)}, f32[8,768]{1,0:T(8,128)}, /*index=5*/f32[16,768]{1,0:T(8,128)}) custom-call(f32[1024,768]{1,0:T(8,128)} %get-tuple-element.51.mid_ref, f32[1024,768]{1,0:T(8,128)} %get-tuple-element.58.sout_ref, ...), custom_call_target="tpu_custom_call" | custom-call | flops 11000000512 | bytes 30000000 | tf_op jit(solution)/shard_map/combine/pallas_call | solution.py:589
  418.3 38.8 %attention_backward.1 = bf16[3,1024,768]{2,1,0:T(8,128)(2,1)} custom-call(bf16[3,1024,768]{2,1,0:T(8,128)(2,1)} %get-tuple-element.65.qkv_ref, bf16[1024,768]{1,0:T(8,128)(2,1)} %get-tuple-element.66.og_ref, f32[6,8,1024]{2,1,0:T(8,128)} %get-tuple-element.67.lse_ref, s32[8,1024]{1,0:T(8,128)} %broadcast_in_dim.41.bidr_ref, ...), custom_call_target="tpu_custom_call" | custom-call | flops 35000000512 | bytes 12000000 | tf_op jit(solution)/shard_map/attention_backward/pallas_call | solution.py:661
  457.1 8.0 %convolution_convert_fusion = bf16[3,768,768]{1,2,0:T(8,128)(2,1)} fusion(bf16[3,1024,768]{2,1,0:T(8,128)(2,1)} %attention_backward.1, f32[768]{0:T(1024)S(1)} %copy-done.26, f32[1024]{0:T(1024)S(1)} %copy-done.27, bf16[1,1024,768]{2,1,0:T(8,128)(2,1)S(1)} %copy-done.7), kind=kOutput, calls=%fused_computation.28 | convolution fusion | flops 3628793856 | bytes 9837568 | tf_op jit(solution)/shard_map/nd,tnf->tdf/dot_general | solution.py:806
  465.1 5.8 fusion.13
  473.5 3.4 pad_maximum_fusion
  476.9 3.2 copy.165
  480.1 12.4 %reshape.312 = bf16[16,256,768]{2,1,0:T(8,128)(2,1)} reshape(bf16[16,2,48,2048]{3,2,1,0:T(8,128)(2,1)} %bitcast.114) | data formatting | bytes 12582912 | tf_op jit(solution)/shard_map/reshape | solution.py:829
  492.8 2.1 constant_dynamic-update-slice_fusion.3
  498.2 3.1 constant_dynamic-update-slice_fusion.1
  501.3 1.9 constant_dynamic-update-slice_fusion
  504.0 6.6 dynamic-slice_bitcast_fusion
  510.9 5.7 fusion.1
  516.6 6.0 collective-permute-done
  522.5 10.0 %fusion = bf16[16,296,768]{2,1,0:T(8,128)(2,1)} fusion(bf16[16,296,768]{2,1,0:T(8,128)(2,1)} %collective-permute-done, bf16[16,2,296,768]{3,2,1,0:T(8,128)(2,1)} %bitcast.33, s32[]{:T(128)S(6)} %select_n.31), kind=kLoop, calls=%fused_computation.1 | loop fusion | flops 14548992 | bytes 21823492 | tf_op jit(solution)/shard_map/convert_element_type | solution.py:701
  532.5 88.9 %all_to_all.10 = bf16[4,4,296,768]{3,2,1,0:T(8,128)(2,1)} all-to-all(bf16[4,4,296,768]{3,2,1,0:T(8,128)(2,1)} %bitcast.110), channel_id=1, replica_groups=mesh['grp'=2,'exp'=4,'shd'=4] {'exp'}, dimensions={0} | all-to-all | bytes 14548992 | tf_op jit(solution)/shard_map/all_to_all | solution.py:705
  621.4 5.9 reduce_sum.51
  627.3 4.1 all-to-all-start.1
  631.5 1.6 copy.150
  633.1 3.1 copy.146
  636.3 3.0 copy.148
  639.3 5.3 fusion.11
  648.4 2.0 copy.145
  650.4 3.9 reshape_reshape.11
  654.3 3.0 copy.147
  657.3 3.1 reshape.322
  660.4 5.1 multiply_subtract_fusion.1
  665.5 3.1 copy.151
  668.7 1.6 copy.152
  670.3 3.1 copy.153
  674.3 7.1 %multiply_subtract_fusion = (f32[1,2,192,2048]{3,2,1,0:T(8,128)}, f32[1,2,192,2048]{3,2,1,0:T(8,128)}, f32[1,2,192,2048]{3,2,1,0:T(8,128)}) fusion(f32[1,2,192,2048]{3,2,1,0:T(8,128)} %param.50, bf16[1,2,192,2048]{3,2,1,0:T(8,128)(2,1)S(1)} %copy-done.4, f32[1,2,192,2048]{3,2,1,0:T(8,128)} %param.51, f32[1,2,192,2048]{3,2,1,0:T(8,128)} %param.52), kind=kLoop, calls=%fused_computation.25 | loop fusion | flops 13369344 | bytes 20447232 | tf_op jit(solution)/shard_map/sub | solution.py:686
  683.0 2.6 multiply_subtract_fusion.4
  685.6 1.9 multiply_subtract_fusion.5
  687.6 1.8 multiply_subtract_fusion.2
  (180 shorter events, 37.7 us)
Async XLA Ops:
  7.2 5.2 copy-start.1
  7.2 72.7 %all-gather.14.cloned.1.call-start = ((), (), s32[]{:S(2)}) async-start(), calls=%async_computation.7 | async-start | bytes 5271552 | tf_op jit(solution)/shard_map/all_gather | solution.py:739
  11.6 4.2 copy-start.14
  12.3 6.1 copy-start.29
  12.3 159.0 %all-gather.12.cloned.1.call-start = ((), (), s32[]{:S(2)}) async-start(), calls=%async_computation.5 | async-start | bytes 3538944 | tf_op jit(solution)/shard_map/all_gather | solution.py:739
  13.3 171.9 %all-gather.16.cloned.1.call-start = ((), (), s32[]{:S(2)}) async-start(), calls=%async_computation.8 | async-start | bytes 7077888 | tf_op jit(solution)/shard_map/all_gather | solution.py:739
  15.7 5.2 copy-start.6
  15.7 304.9 %all-gather.10.cloned.1.call-start = ((), (), s32[]{:S(2)}) async-start(), calls=%async_computation.4 | async-start | bytes 3244032 | tf_op jit(solution)/shard_map/all_gather | solution.py:739
  16.5 339.2 %all-gather.8.cloned.1.call-start = ((), (), s32[]{:S(2)}) async-start(), calls=%async_computation.3 | async-start | bytes 6488064 | tf_op jit(solution)/shard_map/all_gather | solution.py:739
  18.3 613.1 %reduce-scatter.2.cloned.1.call-start = ((), (), s32[]{:S(2)}) async-start(), calls=%async_computation.6 | async-start | bytes 5898240 | tf_op jit(solution)/shard_map/reduce_scatter | solution.py:796
  83.2 18.3 %copy-start = (bf16[2,16,144,384]{3,2,1,0:T(8,128)(2,1)}, bf16[2,16,144,384]{3,2,1,0:T(8,128)(2,1)S(1)}, u32[]{:S(2)}) copy-start(bf16[2,16,144,384]{3,2,1,0:T(8,128)(2,1)S(1)} %slice.97) | copy-start | bytes 10616836
  101.5 9.0 %copy-start.24 = (f32[2,768]{1,0:T(2,128)S(1)}, f32[2,768]{1,0:T(2,128)}, u32[]{:S(2)}) copy-start(f32[2,768]{1,0:T(2,128)} %convert_element_type.142) | copy-start | bytes 18436
  101.5 9.6 %copy-start.25 = (s32[1,1024]{1,0:T(1,128)S(1)}, s32[1,1024]{1,0:T(1,128)}, u32[]{:S(2)}) copy-start(s32[1,1024]{1,0:T(1,128)} %param.30) | copy-start | bytes 12292
  418.2 38.8 %copy-start.7 = (bf16[1,1024,768]{2,1,0:T(8,128)(2,1)S(1)}, bf16[1,1024,768]{2,1,0:T(8,128)(2,1)}, u32[]{:S(2)}) copy-start(bf16[1,1024,768]{2,1,0:T(8,128)(2,1)} %param.28) | copy-start | bytes 4718596
  418.3 38.8 %copy-start.26 = (f32[768]{0:T(1024)S(1)}, f32[768]{0:T(1024)}, u32[]{:S(2)}) copy-start(f32[768]{0:T(1024)} %mul.379) | copy-start | bytes 9220
  418.3 38.8 %copy-start.27 = (f32[1024]{0:T(1024)S(1)}, f32[1024]{0:T(1024)}, u32[]{:S(2)}) copy-start(f32[1024]{0:T(1024)} %add_rsqrt_fusion) | copy-start | bytes 12292
  457.1 8.0 %copy-start.9 = (bf16[3,768,768]{2,1,0:T(8,128)(2,1)S(1)}, bf16[3,768,768]{2,1,0:T(8,128)(2,1)}, u32[]{:S(2)}) copy-start(bf16[3,768,768]{2,1,0:T(8,128)(2,1)} %reshape.306) | copy-start | bytes 10616836
  457.1 8.0 %copy-start.37 = (bf16[3,1024,768]{2,1,0:T(8,128)(2,1)S(1)}, bf16[3,1024,768]{2,1,0:T(8,128)(2,1)}, u32[]{:S(2)}) copy-start(bf16[3,1024,768]{2,1,0:T(8,128)(2,1)} %attention_backward.1) | copy-start | bytes 14155780
  480.1 12.4 %copy-start.10 = (bf16[3,768,768]{1,2,0:T(8,128)(2,1)S(1)}, bf16[3,768,768]{1,2,0:T(8,128)(2,1)}, u32[]{:S(2)}) copy-start(bf16[3,768,768]{1,2,0:T(8,128)(2,1)} %convolution_convert_fusion) | copy-start | bytes 10616836
  492.8 2.8 copy-start.35
  492.8 5.4 slice-start
  495.6 2.6 slice-start.1
  498.2 3.1 copy-start.11
  504.0 6.9 slice-start.2
  504.0 6.9 slice-start.3
  510.6 11.9 %collective-permute-start = (bf16[16,296,768]{2,1,0:T(8,128)(2,1)}, bf16[16,296,768]{2,1,0:T(8,128)(2,1)}, u32[]{:S(2)}, u32[]{:S(2)}) collective-permute-start(bf16[16,296,768]{2,1,0:T(8,128)(2,1)} %dynamic-slice_bitcast_fusion), channel_id=1, source_target_pairs={{0,16},{16,0},{1,17},{17,1},{2,18},{18,2},{3,19},{19,3},{4,20},{20... | collective-permute-start | bytes 21823496 | tf_op jit(solution)/shard_map/ppermute | solution.py:700
  627.3 4.2 copy-start.2
  627.3 46.1 %all-to-all-start.1 = ((bf16[4,296,768]{2,1,0:T(8,128)(2,1)}), bf16[4,296,768]{2,1,0:T(8,128)(2,1)S(1)}, u32[]{:S(2)}, u32[]{:S(2)}) async-start(bf16[4,296,768]{2,1,0:T(8,128)(2,1)} %reduce_sum.51), calls=%async_computation.1 | async-start | bytes 3637248 | tf_op jit(solution)/shard_map/all_to_all | solution.py:707
  631.4 14.5 %collective-permute-start.2 = (bf16[2304,256]{1,0:T(8,128)(2,1)}, bf16[2304,256]{1,0:T(8,128)(2,1)}, u32[]{:S(2)}, u32[]{:S(2)}) collective-permute-start(bf16[2304,256]{1,0:T(8,128)(2,1)} %bitcast.136), channel_id=1, source_target_pairs={{0,16},{16,0},{1,17},{17,1},{2,18},{18,2},{3,19},{19,3},{4,20},{20... | collective-permute-start | bytes 3538952 | tf_op jit(solution)/shard_map/ppermute | solution.py:716
  633.1 6.2 copy-start.8
  650.4 10.0 %copy-start.3 = (f32[1,512,768]{1,2,0:T(8,128)S(1)}, f32[1,512,768]{1,2,0:T(8,128)}, u32[]{:S(2)}) copy-start(f32[1,512,768]{1,2,0:T(8,128)} %copy.150) | copy-start | bytes 4718596
  665.5 3.1 copy-start.5
  670.3 4.0 copy-start.4
  673.7 7.9 %collective-permute-start.1 = (f32[296,768]{1,0:T(8,128)S(1)}, f32[296,768]{1,0:T(8,128)S(1)}, u32[]{:S(2)}, u32[]{:S(2)}) collective-permute-start(f32[296,768]{1,0:T(8,128)S(1)} %convert_reduce_fusion), channel_id=1, source_target_pairs={{0,16},{16,0},{1,17},{17,1},{2,18},{18,2},{3,19},{19,3},{4,20},{20... | collective-permute-start | bytes 2727944 | tf_op jit(solution)/shard_map/ppermute | solution.py:716
  681.6 3.9 copy-start.19
  683.0 4.5 copy-start.15
  683.0 4.5 copy-start.17
  683.0 4.5 copy-start.18
  685.6 3.9 copy-start.12
  685.6 3.9 copy-start.13
  685.6 3.9 copy-start.21
  685.6 3.8 copy-start.22
  687.5 3.2 copy-start.28
  687.6 3.2 copy-start.30
  687.6 3.2 copy-start.31
  687.6 3.8 copy-start.32
  687.6 3.8 copy-start.33
  687.6 3.8 copy-start.34
  (4 other events, 6.3 us)
Sparse Core Ops, SparseCore 0:
  12.4 67.4 all-gather.13
  82.1 37.1 all-gather.11
  121.5 63.6 all-gather.15
  188.6 64.4 all-gather.9
  256.4 99.2 all-gather.7
  516.7 83.7 reduce-scatter.1

commit v3 on v2

--- a/solution.py
+++ b/solution.py
@@ -69,10 +69,116 @@
     )
 
 
+def others(axis, count):
+    me = lax.axis_index(axis)
+    return [lax.bitwise_xor(me, k) for k in range(count)]
+
+
+def gather_kernel(
+    exps, shds,
+    mine_ref, tiny_ref, g_ref, place_ref, full_ref, every_ref, slots_ref,
+    own_sem, z_send, z_recv, p_send, p_recv, c_send, c_recv,
+):
+    columns, layers = others("exp", exps), others("shd", shds)
+    group = lax.axis_index("grp")
+    core = lax.rem(group, 2)
+    partner = {"grp": lax.bitwise_xor(group, 1)}
+    rows = mine_ref.shape[1]
+
+    def spots(kz, kx):
+        at = pl.ds(pl.multiple_of((columns[kx] * shds + layers[kz]) * rows, 16), rows)
+        return full_ref.at[pl.ds(2 * core, 2), at, :], every_ref.at[at, :]
+
+    greet(
+        [{"shd": layer} for layer in layers[1:]]
+        + [{"exp": column} for column in columns[1:]]
+        + [partner]
+    )
+    started = []
+
+    def begin(copies):
+        for copy in copies:
+            copy.start()
+        started.extend(copies)
+        return copies
+
+    def both(sources, kz, kx, sem, far, index, target):
+        return [
+            send(a, b, sem.at[index + (i,)], far.at[index + (i,)], target)
+            for i, (a, b) in enumerate(zip(sources, spots(kz, kx)))
+        ]
+
+    mine = (mine_ref, tiny_ref)
+    local = [
+        pltpu.make_async_copy(a, b, own_sem.at[i])
+        for i, (a, b) in enumerate(zip(mine, spots(0, 0)))
+    ]
+    for copy in local:
+        copy.start()
+    down = [both(mine, 0, 0, z_send, z_recv, (k,), {"shd": layers[k]}) for k in range(1, shds)]
+    for copies in down:
+        begin(copies)
+    across = {}
+    for kx in range(1, exps):
+        across[0, kx] = begin(both(mine, 0, 0, p_send, p_recv, (0, kx), {"exp": columns[kx]}))
+    swaps = [send(mine_ref, spots(0, 0)[0], c_send.at[0, 0], c_recv.at[0, 0], partner)]
+    swaps[0].start()
+    for e in range(slots_ref.shape[0]):
+        hot = slots_of(place_ref[e : e + 1, :], slots_ref.shape[1])
+        slots_ref[e] = mm(hot, g_ref[...]).astype(bf16)
+
+    def swap(kz, kx):
+        here = spots(kz, kx)[0]
+        copy = send(here, here, c_send.at[kz, kx], c_recv.at[kz, kx], partner)
+        copy.start()
+        swaps.append(copy)
+
+    for kz in range(1, shds):
+        for copy in down[kz - 1]:
+            copy.wait_recv()
+        for kx in range(1, exps):
+            across[kz, kx] = begin(both(spots(kz, 0), kz, 0, p_send, p_recv, (kz, kx), {"exp": columns[kx]}))
+        swap(kz, 0)
+    for kz in range(shds):
+        for kx in range(1, exps):
+            for copy in across[kz, kx]:
+                copy.wait_recv()
+            swap(kz, kx)
+    for copy in started:
+        copy.wait_send()
+    for copy in swaps + local:
+        copy.wait()
+
+
+def gather_first(mine, tiny, g, place_row, exps, shds, experts_all, cap):
+    _, rows, width = mine.shape
+    tall = exps * shds * rows
+    sems = lambda *shape: pltpu.SemaphoreType.DMA(shape)
+    return pl.pallas_call(
+        functools.partial(gather_kernel, exps, shds),
+        in_specs=[ANY, ANY, pl.BlockSpec(memory_space=pltpu.VMEM), pl.BlockSpec(memory_space=pltpu.VMEM)],
+        out_specs=[ANY, ANY, pl.BlockSpec(memory_space=pltpu.VMEM)],
+        out_shape=[
+            jax.ShapeDtypeStruct((4, tall, width), bf16),
+            jax.ShapeDtypeStruct((tall, 128), bf16),
+            jax.ShapeDtypeStruct((experts_all, cap, width), bf16),
+        ],
+        scratch_shapes=[
+            sems(2), sems(shds, 2), sems(shds, 2), sems(shds, exps, 2), sems(shds, exps, 2),
+            sems(shds, exps), sems(shds, exps),
+        ],
+        compiler_params=params(collective_id=4, has_side_effects=True),
+        cost_estimate=pl.CostEstimate(
+            flops=40_000_000_000, bytes_accessed=10_000_000, transcendentals=0
+        ),
+        name="gather_first",
+    )(mine, tiny, g, place_row)
+
+
 def forward_kernel(
     exps,
-    tok_ref, bidr_ref, bidc_ref, gains_ref, wa_ref, wo_ref, wr_ref, wrt_ref, slots_ref,
-    qkv_ref, lse_ref, o_ref, mid_ref, h2_ref, probs_ref, probst_ref, landed_ref, h1_ref,
+    tok_ref, bidr_ref, bidc_ref, wa_ref, wo_ref, wr_ref, slots_ref,
+    qkv_ref, lse_ref, o_ref, mid_ref, h2_ref, probs_ref, probst_ref, gains_ref, landed_ref, h1_ref,
     send_sem, recv_sem,
 ):
     pair = pl.program_id(0)
@@ -97,15 +203,15 @@
 
     @pl.when(pair == 0)
     def _():
+        gains_ref[...] = wr_ref[...].astype(f32).T[:8]
         for row in range(0, seq, tile):
             x = tok_ref[pl.ds(row, tile), :].astype(f32)
             r1 = lax.rsqrt(jnp.mean(x * x, axis=1, keepdims=True) + norm_eps)
-            h1_ref[pl.ds(row, tile), :] = (x * r1 * gains_ref[0:1, :]).astype(bf16)
+            h1_ref[pl.ds(row, tile), :] = (x * r1 * gains_ref[4:5, :]).astype(bf16)
 
     h1 = h1_ref[...]
     for i in range(3):
-        w = wa_ref[0, :, i].reshape(width, 128)
-        qkv_ref[i] = mm(h1, w).astype(bf16)
+        qkv_ref[i] = mm(h1, wa_ref[i]).astype(bf16)
     qs = qkv_ref[0] * jnp.asarray(0.125, bf16)
     k = qkv_ref[1]
     vt = qkv_ref[2].T
@@ -139,22 +245,20 @@
 
     @pl.when(pair == pl.num_programs(0) - 1)
     def _():
-        half = wo_ref.shape[2]
         for row in range(0, seq, tile):
             rows = pl.ds(row, tile)
-            o = o_ref[rows, :]
-            add = jnp.concatenate([mm(o, wo_ref[0]), mm(o, wo_ref[1])], axis=1)
-            mid = tok_ref[rows, :].astype(f32) + add
+            mid = tok_ref[rows, :].astype(f32) + mm(o_ref[rows, :], wo_ref[0])
             mid_ref[rows, :] = mid
             r2 = lax.rsqrt(jnp.mean(mid * mid, axis=1, keepdims=True) + norm_eps)
-            h2 = (mid * r2 * gains_ref[1:2, :]).astype(bf16)
+            h2 = (mid * r2 * gains_ref[5:6, :]).astype(bf16)
             h2_ref[rows, :] = h2
             logits = mm(h2, wr_ref[...])
             spot = lax.broadcasted_iota(jnp.int32, logits.shape, 1)
             logits = jnp.where(spot < 4, logits, masked_score)
             e = jnp.exp(logits - jnp.max(logits, axis=1, keepdims=True))
             probs_ref[rows, :] = e / jnp.sum(e, axis=1, keepdims=True)
-        logits = mm_nt(wrt_ref[...], h2_ref[...])
+        routers = gains_ref[...].astype(bf16)
+        logits = mm_nt(jnp.concatenate([routers, routers], axis=0), h2_ref[...])
         spot = lax.broadcasted_iota(jnp.int32, logits.shape, 0)
         logits = jnp.where(spot < 4, logits, masked_score)
         e = jnp.exp(logits - jnp.max(logits, axis=0, keepdims=True))
@@ -163,11 +267,10 @@
             copy.wait()
 
 
-def attention_forward(tokens, bid_row, bid_col, gains, wa, wo, wr, wrt, slots):
+def attention_forward(tokens, bid_row, bid_col, full, wr, slots):
     exps = slots.shape[0]
     seq, width = tokens.shape
     pairs = width // 128
-    per_half = pairs // 2
     return pl.pallas_call(
         functools.partial(forward_kernel, exps),
         grid=(pairs,),
@@ -175,14 +278,9 @@
             once((seq, width)),
             once(bid_row.shape),
             once(bid_col.shape),
-            once(gains.shape),
-            pl.BlockSpec(
-                (1, wa.shape[1], 3, wa.shape[3], 128),
-                lambda i: (i // per_half, 0, 0, 0, i % per_half),
-            ),
-            once(wo.shape),
+            pl.BlockSpec((3, width, 128), lambda i: (0, 0, i)),
+            pl.BlockSpec((1, width, width), lambda i: (3, 0, 0), pipeline_mode=pl.Buffered(1)),
             once(wr.shape),
-            once(wrt.shape),
             ANY,
         ],
         out_specs=[
@@ -193,6 +291,7 @@
             whole_spec((seq, width)),
             whole_spec((seq, 128)),
             whole_spec((16, seq)),
+            whole_spec((8, width)),
             ANY,
         ],
         out_shape=[
@@ -203,6 +302,7 @@
             jax.ShapeDtypeStruct((seq, width), bf16),
             jax.ShapeDtypeStruct((seq, 128), f32),
             jax.ShapeDtypeStruct((16, seq), f32),
+            jax.ShapeDtypeStruct((8, width), f32),
             jax.ShapeDtypeStruct(slots.shape, bf16),
         ],
         scratch_shapes=[
@@ -215,32 +315,12 @@
             flops=30_000_000_000, bytes_accessed=20_000_000, transcendentals=12_000_000
         ),
         name="attention_forward",
-    )(tokens, bid_row, bid_col, gains, wa, wo, wr, wrt, slots)
+    )(tokens, bid_row, bid_col, full, full, wr, slots)
 
 
 def slots_of(place_row, cap):
     slot = lax.broadcasted_iota(jnp.int32, (cap, place_row.shape[1]), 0)
     return (slot == place_row).astype(f32).astype(bf16)
-
-
-def place_kernel(g_ref, place_ref, rows_ref):
-    hot = slots_of(place_ref[pl.ds(pl.program_id(0), 1), :], rows_ref.shape[1])
-    rows_ref[0] = mm(hot, g_ref[...]).astype(bf16)
-
-
-def place_gradients(g, place_row, experts_all, cap):
-    return pl.pallas_call(
-        place_kernel,
-        grid=(experts_all,),
-        in_specs=[once(g.shape), once(place_row.shape)],
-        out_specs=pl.BlockSpec((1, cap, g.shape[1]), lambda e: (e, 0, 0)),
-        out_shape=jax.ShapeDtypeStruct((experts_all, cap, g.shape[1]), bf16),
-        compiler_params=params(("arbitrary",)),
-        cost_estimate=pl.CostEstimate(
-            flops=4_000_000_000, bytes_accessed=6_000_000, transcendentals=0
-        ),
-        name="place_gradients",
-    )(g, place_row)
 
 
 def dispatch_kernel(h2_ref, place_ref, probst_ref, rows_ref, chosen_ref):
@@ -294,17 +374,25 @@
 
 def routed_kernel(
     exps, shds,
-    rows_ref, chosen_ref, grads_ref, we_ref, wn_ref,
-    eout_ref, ein_ref, sums_ref,
+    rows_ref, chosen_ref, grads_ref, packed_ref,
+    eout_ref, ein_ref, own_ref, swapped_ref,
     x_s, g_s, c_s, w_s, n_s, hid_s, gg_s, ug_s, out_s, gin_s, acc_o, acc_i,
-    load_sem, x_send, x_recv, c_send, c_recv, o_send, o_recv, i_send, i_recv, w_sem,
+    load_sem, x_send, x_recv, c_send, c_recv, o_send, o_recv, i_send, i_recv, w_sem, s_send, s_recv,
 ):
     me = lax.axis_index("exp")
     _, cap, width = x_s.shape
     hidden = hid_s.shape[1]
     rows_all = exps * cap
     peers = [lax.bitwise_xor(me, k) for k in range(exps)]
-    greet([{"exp": peer} for peer in peers[1:]])
+    group = lax.axis_index("grp")
+    core = lax.rem(group, 2)
+    partner = {"grp": lax.bitwise_xor(group, 1)}
+    greet([{"exp": peer} for peer in peers[1:]] + [partner])
+    deep, tall = w_s.shape[2], n_s.shape[2]
+    base = hidden // 256 * deep
+    wide_at = lambda b: pl.ds(pl.multiple_of(b * deep, 16), deep)
+    narrow_at = lambda b: pl.ds(base + b * tall, tall)
+    lanes_at = lambda b: pl.ds(pl.multiple_of(256 * b, 256), 256)
 
     chosen, arriving = [], []
     for k in range(1, exps):
@@ -317,9 +405,20 @@
         pltpu.make_async_copy(rows_ref.at[me], x_s.at[0], load_sem.at[0]),
         pltpu.make_async_copy(chosen_ref.at[me], c_s.at[0], load_sem.at[1]),
         pltpu.make_async_copy(grads_ref, g_s, load_sem.at[2]),
-        pltpu.make_async_copy(we_ref, w_s, load_sem.at[3]),
-        pltpu.make_async_copy(wn_ref, n_s, load_sem.at[4]),
     ]
+    for c in range(2):
+        for b in range(hidden // 256):
+            loads.append(
+                pltpu.make_async_copy(
+                    packed_ref.at[c, :, wide_at(b), :], w_s.at[c, :, :, lanes_at(b)], load_sem.at[len(loads)]
+                )
+            )
+        for b in range(width // 256):
+            loads.append(
+                pltpu.make_async_copy(
+                    packed_ref.at[c, :, narrow_at(b), :], n_s.at[:, c, :, lanes_at(b)], load_sem.at[len(loads)]
+                )
+            )
     for copy in loads:
         copy.start()
     for copy in loads:
@@ -367,6 +466,25 @@
         returns.extend(made)
 
     wide = hidden // shds
+    per = wide // 256
+
+    def stores(f):
+        made = []
+        for b in range(per):
+            block = per * f + b
+            here = (slice(None), wide_at(block), slice(None))
+            made.append((w_s.at[core, :, :, lanes_at(block)], own_ref.at[here]))
+            made.append((w_s.at[1 - core, :, :, lanes_at(block)], swapped_ref.at[here]))
+        for b in range(width // 256):
+            made.append((n_s.at[f, core, :, lanes_at(b)], own_ref.at[f, narrow_at(b), :]))
+            made.append((n_s.at[f, 1 - core, :, lanes_at(b)], swapped_ref.at[f, narrow_at(b), :]))
+        copies = []
+        for i, (a, b) in enumerate(made):
+            if i % 2:
+                copies.append(send(a, b, s_send.at[f, i // 2], s_recv.at[f, i // 2], partner))
+            else:
+                copies.append(pltpu.make_async_copy(a, b, w_sem.at[f, i // 2]))
+        return copies
 
     @pl.loop(0, shds)
     def _(f):
@@ -377,38 +495,34 @@
         w_s[0, :, :, columns] = mm_tn(x, gg_s[:, columns]).astype(bf16).reshape(part)
         w_s[1, :, :, columns] = mm_tn(x, ug_s[:, columns]).astype(bf16).reshape(part)
         n_s[f] = mm_tn(hid_s[:, columns], g).astype(bf16).reshape(n_s.shape[1:])
-
-    stores = []
-    deep = w_s.shape[2]
-    base = hidden // 256 * deep
-    tall = n_s.shape[2]
-    for c in range(2):
-        for b in range(hidden // 256):
-            stores.append((w_s.at[c, :, :, pl.ds(256 * b, 256)], sums_ref.at[c, :, pl.ds(b * deep, deep), :]))
-        for b in range(width // 256):
-            stores.append((n_s.at[:, c, :, pl.ds(256 * b, 256)], sums_ref.at[c, :, pl.ds(base + b * tall, tall), :]))
-    stores = [pltpu.make_async_copy(a, b, w_sem.at[i]) for i, (a, b) in enumerate(stores)]
-    for copy in stores:
-        copy.start()
-    for copy in stores + returns:
+        for copy in stores(f):
+            copy.start()
+
+    for copy in returns:
         copy.wait()
 
-
-def routed(slot_rows, chosen, grads, w_experts, w_narrower, shds):
+    @pl.loop(0, shds)
+    def _(f):
+        for copy in stores(f):
+            copy.wait()
+
+
+def routed(slot_rows, chosen, grads, packed, hidden):
     exps, cap, width = slot_rows.shape
-    hidden = w_experts.shape[2]
+    shds, height = packed.shape[1:3]
     deep, tall = width // shds, hidden // shds // 2
-    height = hidden // 256 * deep + width // 256 * tall
+    pieces = hidden // shds // 256 + width // 256
     big = lambda *shape: pltpu.VMEM(shape, bf16)
-    sems = lambda n: pltpu.SemaphoreType.DMA((n,))
+    sems = lambda *n: pltpu.SemaphoreType.DMA(n)
     return pl.pallas_call(
         functools.partial(routed_kernel, exps, shds),
-        in_specs=[ANY] * 5,
-        out_specs=[ANY] * 3,
+        in_specs=[ANY] * 4,
+        out_specs=[ANY] * 4,
         out_shape=[
             jax.ShapeDtypeStruct((exps, cap, width), bf16),
             jax.ShapeDtypeStruct((exps, cap, width), bf16),
-            jax.ShapeDtypeStruct((2, shds, height, 256), bf16),
+            jax.ShapeDtypeStruct((shds, height, 256), bf16),
+            jax.ShapeDtypeStruct((shds, height, 256), bf16),
         ],
         scratch_shapes=[
             big(exps, cap, width),
@@ -423,9 +537,10 @@
             big(exps, cap, width),
             pltpu.VMEM((cap, width), f32),
             pltpu.VMEM((cap, width), f32),
-            sems(5), sems(exps), sems(exps), sems(exps), sems(exps),
+            sems(3 + 2 * (hidden // 256 + width // 256)),
             sems(exps), sems(exps), sems(exps), sems(exps),
-            sems(2 * (hidden // 256 + width // 256)),
+            sems(exps), sems(exps), sems(exps), sems(exps),
+            sems(shds, pieces), sems(shds, pieces), sems(shds, pieces),
         ],
         compiler_params=params(collective_id=2, has_side_effects=True),
         cost_estimate=pl.CostEstimate(
@@ -434,36 +549,57 @@
             transcendentals=exps * cap * hidden,
         ),
         name="routed",
-    )(
-        slot_rows, chosen, grads,
-        w_experts.reshape(2, shds, deep, hidden),
-        w_narrower.reshape(shds, 2, tall, width),
-    )
+    )(slot_rows, chosen, grads, packed)
 
 
 def ffn_kernel(
-    x_ref, g_ref, wg_ref, wu_ref, wn_ref, sums_ref,
-    out_ref, gin_ref, dwg_ref, dwu_ref, dwn_ref, swapped_ref,
-    acc_out, acc_gin, hid_s, gg_s, ug_s, send_sem, recv_sem,
+    x_ref, g_ref, wg_ref, wu_ref, wn_ref,
+    out_ref, gin_ref, own_a, swapped_a, own_b, swapped_b,
+    acc_out, acc_gin, hid_s, gg_s, ug_s, wide_s, narrow_s, own_sem, send_sem, recv_sem,
     *, tile,
 ):
     f = pl.program_id(0)
     last = pl.num_programs(0) - 1
-    rows_all = x_ref.shape[0]
+    rows_all, width = x_ref.shape
     group = lax.axis_index("grp")
+    core = lax.rem(group, 2)
     partner = {"grp": lax.bitwise_xor(group, 1)}
-    swap = lambda: send(
-        sums_ref.at[1 - lax.rem(group, 2)], swapped_ref, send_sem, recv_sem, partner
-    )
+    _, _, _, ft = wide_s.shape
+    _, shards, _, tall, _ = narrow_s.shape
+
+    def stores(step):
+        columns = pl.ds(pl.multiple_of(step * ft, ft), ft)
+        at = pl.ds(step * shards, shards)
+        return [
+            pltpu.make_async_copy(wide_s.at[step, core], own_a.at[:, columns], own_sem.at[step, 0]),
+            pltpu.make_async_copy(narrow_s.at[step, :, core], own_b.at[at], own_sem.at[step, 1]),
+            send(
+                wide_s.at[step, 1 - core], swapped_a.at[:, columns],
+                send_sem.at[step, 0], recv_sem.at[step, 0], partner,
+            ),
+            send(
+                narrow_s.at[step, :, 1 - core], swapped_b.at[at],
+                send_sem.at[step, 1], recv_sem.at[step, 1], partner,
+            ),
+        ]
 
     @pl.when(f == 0)
     def _():
         greet([partner])
-        swap().start()
         acc_out[...] = jnp.zeros_like(acc_out)
         acc_gin[...] = jnp.zeros_like(acc_gin)
 
-    wg, wu, wn = wg_ref[0], wu_ref[0], wn_ref[...]
+    deep = wg_ref.shape[2] // 2
+    wide = lambda ref: jnp.concatenate(
+        [ref[0, :, :deep].reshape(width, 256), ref[0, :, deep:].reshape(width, 256)], axis=1
+    )
+    wg, wu = wide(wg_ref), wide(wu_ref)
+    narrow = [
+        jnp.concatenate([wn_ref[c, s, tall * b : tall * (b + 1)] for b in range(width // 256)], axis=1)
+        for s in range(shards)
+        for c in range(2)
+    ]
+    wn = jnp.concatenate(narrow, axis=0)
     for row in range(0, rows_all, tile):
         rows = pl.ds(row, tile)
         x, g = x_ref[rows, :], g_ref[rows, :]
@@ -471,47 +607,51 @@
         hid_s[rows, :], gg_s[rows, :], ug_s[rows, :] = hidden, gg, ug
         acc_out[rows, :] += mm(hidden, wn)
         acc_gin[rows, :] += mm_nt(gg, wg) + mm_nt(ug, wu)
-    dwg_ref[0] = mm_tn(x_ref[...], gg_s[...]).astype(dwg_ref.dtype)
-    dwu_ref[0] = mm_tn(x_ref[...], ug_s[...]).astype(dwu_ref.dtype)
-    dwn_ref[...] = mm_tn(hid_s[...], g_ref[...]).astype(dwn_ref.dtype)
+    wide_s[f, 0] = mm_tn(x_ref[...], gg_s[...]).astype(bf16)
+    wide_s[f, 1] = mm_tn(x_ref[...], ug_s[...]).astype(bf16)
+    narrow_s[f] = mm_tn(hid_s[...], g_ref[...]).astype(bf16).reshape(narrow_s.shape[1:])
+    for copy in stores(f):
+        copy.start()
 
     @pl.when(f == last)
     def _():
         out_ref[...] = acc_out[...].astype(out_ref.dtype)
         gin_ref[...] = acc_gin[...].astype(gin_ref.dtype)
-        swap().wait()
-
-
-def ffn(x, g, wgu, wn, sums, out_type, tile, name):
+
+        @pl.loop(0, pl.num_programs(0))
+        def _(step):
+            for copy in stores(step):
+                copy.wait()
+
+
+def ffn(x, g, packed, hidden, out_type, tile, name):
     rows, width = x.shape
-    hidden = wn.shape[0]
+    _, spread, height, _ = packed.shape
     ft = 512
+    steps = hidden // ft
+    deep, tall = width // spread, hidden // spread // 2
+    shards = spread // steps
+    base = hidden // 256 * deep
+    narrow_high = height - base
+    sems = pltpu.SemaphoreType.DMA((steps, 2))
     return pl.pallas_call(
         functools.partial(ffn_kernel, tile=tile),
-        grid=(hidden // ft,),
+        grid=(steps,),
         in_specs=[
             once((rows, width)),
             once((rows, width)),
-            pl.BlockSpec((1, width, ft), lambda f: (0, 0, f)),
-            pl.BlockSpec((1, width, ft), lambda f: (1, 0, f)),
-            pl.BlockSpec((ft, width), lambda f: (f, 0)),
-            ANY,
-        ],
-        out_specs=[
-            once((rows, width)),
-            once((rows, width)),
-            pl.BlockSpec((1, width, ft), lambda f: (0, 0, f)),
-            pl.BlockSpec((1, width, ft), lambda f: (0, 0, f)),
-            pl.BlockSpec((ft, width), lambda f: (f, 0)),
-            ANY,
-        ],
+            pl.BlockSpec((1, spread, 2 * deep, 256), lambda f: (0, 0, f, 0)),
+            pl.BlockSpec((1, spread, 2 * deep, 256), lambda f: (1, 0, f, 0)),
+            pl.BlockSpec((2, shards, narrow_high, 256), lambda f: (0, f, base // narrow_high, 0)),
+        ],
+        out_specs=[once((rows, width)), once((rows, width)), ANY, ANY, ANY, ANY],
         out_shape=[
             jax.ShapeDtypeStruct((rows, width), out_type),
             jax.ShapeDtypeStruct((rows, width), out_type),
-            jax.ShapeDtypeStruct((1, width, hidden), bf16),
-            jax.ShapeDtypeStruct((1, width, hidden), bf16),
-            jax.ShapeDtypeStruct((hidden, width), bf16),
-            jax.ShapeDtypeStruct(sums.shape[1:], bf16),
+            jax.ShapeDtypeStruct((width, hidden), bf16),
+            jax.ShapeDtypeStruct((width, hidden), bf16),
+            jax.ShapeDtypeStruct((spread, tall, width), bf16),
+            jax.ShapeDtypeStruct((spread, tall, width), bf16),
         ],
         scratch_shapes=[
             pltpu.VMEM((rows, width), f32),
@@ -519,8 +659,9 @@
             pltpu.VMEM((rows, ft), bf16),
             pltpu.VMEM((rows, ft), bf16),
             pltpu.VMEM((rows, ft), bf16),
-            pltpu.SemaphoreType.DMA,
-            pltpu.SemaphoreType.DMA,
+            pltpu.VMEM((steps, 2, width, ft), bf16),
+            pltpu.VMEM((steps, shards, 2, tall, width), bf16),
+            sems, sems, sems,
         ],
         compiler_params=params(("arbitrary",), collective_id=3, has_side_effects=True),
         cost_estimate=pl.CostEstimate(
@@ -529,15 +670,51 @@
             transcendentals=rows * hidden,
         ),
         name=name,
-    )(x, g, wgu, wgu, wn, sums)
+    )(x, g, packed, packed, packed)
+
+
+def plane_copies(exps, part_ref, landed_ref, send_sem, recv_sem):
+    columns = others("exp", exps)
+    made = [pltpu.make_async_copy(part_ref.at[columns[0]], landed_ref.at[0], send_sem.at[0])]
+    for k in range(1, exps):
+        made.append(
+            send(
+                part_ref.at[columns[k]], landed_ref.at[k],
+                send_sem.at[k], recv_sem.at[k], {"exp": columns[k]},
+            )
+        )
+    return made
+
+
+def plane_begin(exps, *refs):
+    greet([{"exp": column} for column in others("exp", exps)[1:]])
+    for copy in plane_copies(exps, *refs):
+        copy.start()
+
+
+def plane_end(exps, *refs):
+    for copy in plane_copies(exps, *refs):
+        copy.wait()
+
+
+def pair_sems(count):
+    return [pltpu.SemaphoreType.DMA((count,)), pltpu.SemaphoreType.DMA((count,))]
 
 
 def combine_kernel(
     mid_ref, sout_ref, sin_ref, g_ref, h2_ref, probs_ref, place_ref, eout_ref, ein_ref,
-    gains_ref, wr_ref, wo_ref,
-    block_ref, midg_ref, midb_ref, og_ref, gain_ref, rgrad_ref,
+    gains_ref, wr_ref, wo_ref, part_ref,
+    block_ref, midg_ref, midb_ref, og_ref, gain_ref, rgrad_ref, landed_ref,
+    send_sem, recv_sem,
 ):
     step = pl.program_id(0)
+    exps = part_ref.shape[0]
+    exchange = (exps, part_ref, landed_ref, send_sem, recv_sem)
+
+    @pl.when(step == 0)
+    def _():
+        plane_begin(*exchange)
+
     tile, width = mid_ref.shape
     experts_all, cap = eout_ref.shape[0], eout_ref.shape[1]
     slot = lax.broadcasted_iota(jnp.int32, (tile, cap), 1)
@@ -561,16 +738,14 @@
     h2_grad = moe_in + mm_nt(lgrad, wr_ref[...]) + sin_ref[...]
     r2 = lax.rsqrt(jnp.mean(mid * mid, axis=1, keepdims=True) + norm_eps)
     n2 = mid * r2
-    d2 = h2_grad * gains_ref[1:2, :]
+    d2 = h2_grad * gains_ref[5:6, :]
     mid_grad = g + r2 * (d2 - n2 * jnp.mean(d2 * n2, axis=1, keepdims=True))
     midb = mid_grad.astype(bf16)
     midg_ref[...] = mid_grad
     midb_ref[...] = midb
-    half = wo_ref.shape[2]
-    og = mm_nt(midb[:, :half], wo_ref[0]) + mm_nt(midb[:, half:], wo_ref[1])
-    og_ref[...] = og.astype(bf16)
+    og_ref[...] = mm_nt(midb, wo_ref[0]).astype(bf16)
     gsum = jnp.sum(h2_grad * n2, axis=0, keepdims=True)
-    rsum = mm_tn(lgrad, h2_ref[...])[:16]
+    rsum = mm_tn(lgrad, h2_ref[...])[:8]
 
     @pl.when(step == 0)
     def _():
@@ -580,8 +755,12 @@
     gain_ref[0:1, :] += gsum
     rgrad_ref[...] += rsum
 
-
-def combine(mid, sout, sin, g, h2, probs, place_col, eout, ein, gains, wr, wo):
+    @pl.when(step == pl.num_programs(0) - 1)
+    def _():
+        plane_end(*exchange)
+
+
+def combine(mid, sout, sin, g, h2, probs, place_col, eout, ein, gains, wr, full, part):
     seq, width = mid.shape
     tile = 256
     by_rows = pl.BlockSpec((tile, width), lambda i: (i, 0))
@@ -591,26 +770,41 @@
         grid=(seq // tile,),
         in_specs=[
             by_rows, by_rows, by_rows, by_rows, by_rows, lanes, lanes,
-            once(eout.shape), once(ein.shape), once(gains.shape), once(wr.shape), once(wo.shape),
-        ],
-        out_specs=[by_rows, by_rows, by_rows, by_rows, whole_spec((8, width)), whole_spec((16, width))],
+            once(eout.shape), once(ein.shape), once(gains.shape), once(wr.shape),
+            pl.BlockSpec((1, width, width), lambda i: (3, 0, 0), pipeline_mode=pl.Buffered(1)),
+            ANY,
+        ],
+        out_specs=[by_rows, by_rows, by_rows, by_rows, whole_spec((8, width)), whole_spec((8, width)), ANY],
         out_shape=[
             jax.ShapeDtypeStruct((seq, width), bf16),
             jax.ShapeDtypeStruct((seq, width), f32),
             jax.ShapeDtypeStruct((seq, width), bf16),
             jax.ShapeDtypeStruct((seq, width), bf16),
             jax.ShapeDtypeStruct((8, width), f32),
-            jax.ShapeDtypeStruct((16, width), f32),
-        ],
-        compiler_params=params(("arbitrary",)),
+            jax.ShapeDtypeStruct((8, width), f32),
+            jax.ShapeDtypeStruct(part.shape, bf16),
+        ],
+        scratch_shapes=pair_sems(part.shape[0]),
+        compiler_params=params(("arbitrary",), collective_id=5, has_side_effects=True),
         cost_estimate=pl.CostEstimate(
             flops=11_000_000_000, bytes_accessed=30_000_000, transcendentals=0
         ),
         name="combine",
-    )(mid, sout, sin, g, h2, probs, place_col, eout, ein, gains, wr, wo)
-
-
-def backward_kernel(qkv_ref, og_ref, lse_ref, bidr_ref, bidc_ref, grad_ref, dk_s, dv_s):
+    )(mid, sout, sin, g, h2, probs, place_col, eout, ein, gains, wr, full, part)
+
+
+def backward_kernel(
+    qkv_ref, og_ref, lse_ref, bidr_ref, bidc_ref, part_ref,
+    grad_ref, landed_ref, dk_s, dv_s, send_sem, recv_sem,
+):
+    step = pl.program_id(0)
+    exps = part_ref.shape[0]
+    exchange = (exps, part_ref, landed_ref, send_sem, recv_sem)
+
+    @pl.when(step == 0)
+    def _():
+        plane_begin(*exchange)
+
     seq = og_ref.shape[0]
     tile = 256
     qs = qkv_ref[0] * jnp.asarray(0.125, bf16)
@@ -654,8 +848,12 @@
     grad_ref[1] = dk_s[...].astype(bf16)
     grad_ref[2] = dv_s[...].astype(bf16)
 
-
-def attention_backward(qkv, og, lse, bid_row, bid_col):
+    @pl.when(step == pl.num_programs(0) - 1)
+    def _():
+        plane_end(*exchange)
+
+
+def attention_backward(qkv, og, lse, bid_row, bid_col, part):
     _, seq, width = qkv.shape
     pairs = width // 128
     return pl.pallas_call(
@@ -667,16 +865,221 @@
             pl.BlockSpec((1, 8, seq), lambda i: (i, 0, 0)),
             once(bid_row.shape),
             once(bid_col.shape),
-        ],
-        out_specs=pl.BlockSpec((3, seq, 128), lambda i: (0, 0, i)),
-        out_shape=jax.ShapeDtypeStruct((3, seq, width), bf16),
-        scratch_shapes=[pltpu.VMEM((seq, 128), f32), pltpu.VMEM((seq, 128), f32)],
-        compiler_params=params(("arbitrary",)),
+            ANY,
+        ],
+        out_specs=[pl.BlockSpec((3, seq, 128), lambda i: (0, 0, i)), ANY],
+        out_shape=[
+            jax.ShapeDtypeStruct((3, seq, width), bf16),
+            jax.ShapeDtypeStruct(part.shape, bf16),
+        ],
+        scratch_shapes=[pltpu.VMEM((seq, 128), f32), pltpu.VMEM((seq, 128), f32)]
+        + pair_sems(part.shape[0]),
+        compiler_params=params(("arbitrary",), collective_id=6, has_side_effects=True),
         cost_estimate=pl.CostEstimate(
             flops=35_000_000_000, bytes_accessed=12_000_000, transcendentals=12_000_000
         ),
         name="attention_backward",
-    )(qkv, og, lse, bid_row, bid_col)
+    )(qkv, og, lse, bid_row, bid_col, part)
+
+
+def finish_kernel(
+    exps, shds,
+    dqkv_ref, tok_ref, midg_ref, o_ref, midb_ref, w_ref, gains_ref, gain2_ref, rgrad_ref, la_ref, lb_ref,
+    igrad_ref, sw_ref, sa_ref, sb_ref, st_ref,
+    h1_s, stack_s, pair_s, tiny_s, tpair_s, plane_s, tplane_s, qa_s, qb_s, za_s, zb_s, r_s, zr_s, tr_s, tz_s,
+    fw_s, fa_s, fb_s,
+    pair_send, pair_recv, plane_send, plane_recv, line_send, line_recv, last_send, last_recv, own_sem,
+):
+    columns, layers = others("exp", exps), others("shd", shds)
+    group = lax.axis_index("grp")
+    core = lax.rem(group, 2)
+    partner = {"grp": lax.bitwise_xor(group, 1)}
+    seq, width = tok_ref.shape
+    tile = 256
+    greet(
+        [{"shd": layer} for layer in layers[1:]]
+        + [{"exp": column} for column in columns[1:]]
+        + [partner]
+    )
+
+    def total(ref):
+        value = ref[0].astype(f32)
+        for k in range(1, ref.shape[0]):
+            value = value + ref[k].astype(f32)
+        return value
+
+    waits = []
+
+    def begin(copy):
+        copy.start()
+        waits.append(copy)
+        return copy
+
+    def line(part_s, landed_s, kind):
+        return [
+            begin(
+                send(
+                    part_s.at[layers[k]], landed_s.at[k],
+                    line_send.at[kind, k], line_recv.at[kind, k], {"shd": layers[k]},
+                )
+            )
+            for k in range(1, shds)
+        ]
+
+    for z in range(shds):
+        qa_s[z] = sum([la_ref[k, z].astype(f32) for k in range(1, exps)], la_ref[0, z].astype(f32)).astype(bf16)
+        qb_s[z] = sum([lb_ref[k, z].astype(f32) for k in range(1, exps)], lb_ref[0, z].astype(f32)).astype(bf16)
+    line_a, line_b = line(qa_s, za_s, 0), line(qb_s, zb_s, 1)
+
+    for row in range(0, seq, tile):
+        rows = pl.ds(row, tile)
+        x = tok_ref[rows, :].astype(f32)
+        r1 = lax.rsqrt(jnp.mean(x * x, axis=1, keepdims=True) + norm_eps)
+        h1_s[rows, :] = (x * r1 * gains_ref[4:5, :]).astype(bf16)
+    shape = stack_s.shape[2:]
+    stack_s[0, 0] = mm_tn(h1_s[...], dqkv_ref[0]).astype(bf16).reshape(shape)
+    stack_s[0, 1] = mm_tn(h1_s[...], dqkv_ref[1]).astype(bf16).reshape(shape)
+    stack_s[1, 0] = mm_tn(h1_s[...], dqkv_ref[2]).astype(bf16).reshape(shape)
+    stack_s[1, 1] = mm_tn(o_ref[...], midb_ref[...]).astype(bf16).reshape(shape)
+    swap = send(stack_s.at[1 - core], pair_s, pair_send.at[0], pair_recv.at[0], partner)
+    swap.start()
+
+    gain = jnp.zeros((1, width), f32)
+    for row in range(0, seq, tile):
+        rows = pl.ds(row, tile)
+        x = tok_ref[rows, :].astype(f32)
+        r1 = lax.rsqrt(jnp.mean(x * x, axis=1, keepdims=True) + norm_eps)
+        n1 = x * r1
+        grad = mm_nt(dqkv_ref[0, rows, :], w_ref[0])
+        grad = grad + mm_nt(dqkv_ref[1, rows, :], w_ref[1])
+        grad = grad + mm_nt(dqkv_ref[2, rows, :], w_ref[2])
+        gain = gain + jnp.sum(grad * n1, axis=0, keepdims=True)
+        d1 = grad * gains_ref[4:5, :]
+        igrad_ref[rows, :] = midg_ref[rows, :] + r1 * (d1 - n1 * jnp.mean(d1 * n1, axis=1, keepdims=True))
+    spot = lax.broadcasted_iota(jnp.int32, (8, width), 0)
+    small = jnp.where(spot < 4, rgrad_ref[...], jnp.where(spot == 4, gain, gain2_ref[0:1, :]))
+    small = jnp.concatenate([small, jnp.zeros((120, width), f32)], axis=0)
+    tiny_s[...] = small.T.reshape(tiny_s.shape)
+    tswap = send(tiny_s, tpair_s, pair_send.at[1], pair_recv.at[1], partner)
+    tswap.start()
+
+    swap.wait()
+    for i in range(2):
+        for e in range(exps):
+            stack_s[core, i, e] = (stack_s[core, i, e].astype(f32) + pair_s[i, e].astype(f32)).astype(bf16)
+    plane = [
+        begin(
+            send(
+                stack_s.at[core, :, columns[k]], plane_s.at[k],
+                plane_send.at[0, k], plane_recv.at[0, k], {"exp": columns[k]},
+            )
+        )
+        for k in range(1, exps)
+    ]
+    tswap.wait()
+    tpair_s[...] += tiny_s[...]
+    plane += [
+        begin(
+            send(
+                tpair_s.at[columns[k]], tplane_s.at[k],
+                plane_send.at[1, k], plane_recv.at[1, k], {"exp": columns[k]},
+            )
+        )
+        for k in range(1, exps)
+    ]
+
+    def finals(kind, part_s, out_ref, at):
+        return [
+            pltpu.make_async_copy(part_s, out_ref.at[at], own_sem.at[kind]),
+            send(part_s, out_ref.at[at], last_send.at[kind], last_recv.at[kind], partner),
+        ]
+
+    for copy in line_a + line_b:
+        copy.wait_recv()
+    mine = layers[0]
+    fa_s[...] = sum([za_s[k].astype(f32) for k in range(1, shds)], qa_s[mine].astype(f32))
+    fb_s[...] = sum([zb_s[k].astype(f32) for k in range(1, shds)], qb_s[mine].astype(f32))
+    last = finals(0, fa_s, sa_ref, core) + finals(1, fb_s, sb_ref, core)
+    for copy in last:
+        copy.start()
+
+    for copy in plane:
+        copy.wait_recv()
+    own = columns[0]
+    for i in range(2):
+        for z in range(shds):
+            value = stack_s[core, i, own, z].astype(f32)
+            for k in range(1, exps):
+                value = value + plane_s[k, i, z].astype(f32)
+            r_s[z, i] = value.astype(bf16)
+    line_r = line(r_s, zr_s, 2)
+    tr_s[...] = sum([tplane_s[k] for k in range(1, exps)], tpair_s[own])
+    line_r += line(tr_s, tz_s, 3)
+    for copy in line_r:
+        copy.wait_recv()
+    fw_s[...] = sum([zr_s[k].astype(f32) for k in range(1, shds)], r_s[mine].astype(f32))
+    ends = finals(2, fw_s, sw_ref, core)
+    for copy in ends:
+        copy.start()
+    st_ref[...] = sum([tz_s[k] for k in range(1, shds)], tr_s[mine])
+    for copy in waits:
+        copy.wait_send()
+    for copy in last + ends:
+        copy.wait()
+
+
+def finish(dqkv, tokens, midg, o, midb, full, gains, gain2, rgrad, la, lb):
+    exps, shds = la.shape[:2]
+    seq, width = tokens.shape
+    rows = la.shape[2]
+    vmem = pl.BlockSpec(memory_space=pltpu.VMEM)
+    big = lambda *shape: pltpu.VMEM(shape, bf16)
+    wide = lambda *shape: pltpu.VMEM(shape, f32)
+    sems = lambda *n: pltpu.SemaphoreType.DMA(n)
+    a, b = la.shape[2:], lb.shape[2:]
+    tiny = (exps, shds, rows, 128)
+    weights = pl.BlockSpec((3, width, width), lambda i: (0, 0, 0), pipeline_mode=pl.Buffered(1))
+    given = [dqkv, tokens, midg, o, midb, full, gains, gain2, rgrad, la, lb]
+    return pl.pallas_call(
+        functools.partial(finish_kernel, exps, shds),
+        grid=(1,),
+        in_specs=[weights if v is full else once(v.shape) for v in given],
+        out_specs=[once((seq, width)), ANY, ANY, ANY, once((rows, 128))],
+        out_shape=[
+            jax.ShapeDtypeStruct((seq, width), f32),
+            jax.ShapeDtypeStruct((2, 2, rows, width), f32),
+            jax.ShapeDtypeStruct((2,) + a, f32),
+            jax.ShapeDtypeStruct((2,) + b, f32),
+            jax.ShapeDtypeStruct((rows, 128), f32),
+        ],
+        scratch_shapes=[
+            big(seq, width),
+            big(2, 2, exps, shds, rows, width),
+            big(2, exps, shds, rows, width),
+            wide(*tiny),
+            wide(*tiny),
+            big(exps, 2, shds, rows, width),
+            wide(exps, shds, rows, 128),
+            big(shds, *a),
+            big(shds, *b),
+            big(shds, *a),
+            big(shds, *b),
+            big(shds, 2, rows, width),
+            big(shds, 2, rows, width),
+            wide(shds, rows, 128),
+            wide(shds, rows, 128),
+            wide(2, rows, width),
+            wide(*a),
+            wide(*b),
+            sems(2), sems(2), sems(2, exps), sems(2, exps), sems(4, shds), sems(4, shds),
+            sems(3), sems(3), sems(3),
+        ],
+        compiler_params=params(("arbitrary",), collective_id=7, has_side_effects=True),
+        cost_estimate=pl.CostEstimate(
+            flops=60_000_000_000, bytes_accessed=30_000_000, transcendentals=0
+        ),
+        name="finish",
+    )(*given)
 
 
 def adam_update(weight, moment, square, gradient, step_rate, shrink_rate):
@@ -688,23 +1091,6 @@
 
 def pick(array, axis, index):
     return lax.dynamic_index_in_dim(array, index, axis, keepdims=False)
-
-
-def sum_parts(array):
-    return jnp.sum(array.astype(f32), axis=0)
-
-
-def reduce_scatter(stacked, axes, groups, core):
-    own, other = pick(stacked, 0, core), pick(stacked, 0, 1 - core)
-    swap = [(i, i ^ 1) for i in range(groups)]
-    arrived = lax.ppermute(other, "grp", swap)
-    part = (own.astype(f32) + arrived.astype(f32)).astype(bf16)
-    for axis in axes[:-1]:
-        size = lax.axis_size(axis)
-        part = part.reshape((size, part.shape[0] // size) + part.shape[1:])
-        part = lax.all_to_all(part, axis, 0, 0, tiled=True)
-        part = sum_parts(part).astype(bf16)
-    return share(sum_parts(lax.all_to_all(part, axes[-1], 0, 0, tiled=True)), groups, core)
 
 
 def share(part, groups, core):
@@ -727,50 +1113,33 @@
     spread = exps * shds
     core = lax.rem(lax.axis_index("grp"), 2)
     _, seq, width = tokens_in.shape
-    hidden = reducer.shape[1 - 1] * spread
+    hidden = reducer.shape[0] * spread
     experts_all = exps * experts.shape[0]
-    rows = output.shape[0]
-    half = width // 2
+    rows, tall = output.shape[0], reducer.shape[0] // 2
+    deep = width // shds
     tokens, g = tokens_in.reshape(seq, width), cotangent.reshape(seq, width)
 
-    def gather(part, axes, order):
-        names = ("grp",) + axes if order == "first" else axes + ("grp",)
-        if groups == 2:
-            return lax.all_gather(part, names, axis=0, tiled=False).reshape((-1,) + part.shape)
-        wide = lax.all_gather(part, names, axis=0, tiled=False)
-        shape = (groups, -1) if order == "first" else (-1, groups)
-        wide = wide.reshape(shape + part.shape)
-        wide = wide[:2] if order == "first" else wide[:, :2]
-        return wide.reshape((-1,) + part.shape)
-
-    both = ("exp", "shd")
-    small = jnp.concatenate([router.reshape(-1), scales.reshape(-1)])
-    small = jnp.pad(small, (0, half - small.shape[0])).reshape(1, half)
-    small = jnp.pad(small, ((0, 15), (0, 0))).astype(bf16)
-    columns = lambda a, n: pick(a.astype(bf16).reshape(n, 2, half), 1, core)
-    payload = jnp.concatenate(
-        [columns(attend, 3 * rows), columns(output, rows), small], axis=0
-    )
-    first = gather(payload, both, "first").reshape(2, spread, payload.shape[0], half)
-    w_experts = gather(pick(experts.astype(bf16)[0], 0, core), ("shd",), "first").reshape(2, width, hidden)
-    w_narrower = gather(
-        pick(narrower.astype(bf16).reshape(2, -1, width), 0, core), ("shd",), "last"
-    ).reshape(hidden, width)
-    w_widener = gather(pick(widener.astype(bf16), 0, core), both, "first").reshape(2, width, hidden)
-    w_reducer = gather(
-        pick(reducer.astype(bf16).reshape(2, -1, width), 0, core), both, "last"
-    ).reshape(hidden, width)
-
-    wa = first[:, :, : 3 * rows].reshape(2, spread, 3, rows, half)
-    wo = first[:, :, 3 * rows : 4 * rows].reshape(2, width, half)
-    packed = first[0, :, 4 * rows]
-    count = rows * experts_all
-    w_router = packed[:, :count].reshape(width, experts_all)
-    gains = packed[:, count : count + 2 * rows].reshape(spread, 2, rows)
-    gains = gains.transpose(1, 0, 2).reshape(2, width).astype(f32)
-    gains = jnp.pad(gains, ((0, 6), (0, 0)))
-    wr = jnp.pad(w_router, ((0, 0), (0, 128 - experts_all)))
-    wrt = jnp.pad(w_router.T, ((0, 16 - experts_all), (0, 0)))
+    def packed(wide, narrow):
+        wide = pick(wide.astype(bf16), 0, core)
+        narrow = pick(narrow.astype(bf16).reshape(2, -1, width), 0, core)
+        blocks = [
+            a.reshape(a.shape[0], -1, 256).transpose(1, 0, 2).reshape(-1, 256) for a in (wide, narrow)
+        ]
+        return jnp.concatenate(blocks, axis=0)
+
+    def gather(part, axes):
+        wide = lax.all_gather(part, ("grp",) + axes, axis=0, tiled=False)
+        return wide.reshape((groups, -1) + part.shape)[:2]
+
+    mine = jnp.where(
+        core == 0,
+        attend[:2].astype(bf16),
+        jnp.stack([attend[2].astype(bf16), output.astype(bf16)]),
+    )
+    tiny = jnp.concatenate([router, scales.T], axis=1).astype(bf16)
+    tiny = jnp.pad(tiny, ((0, 0), (0, 128 - tiny.shape[1])))
+    expert_weights = gather(packed(experts[0], narrower[0]), ("shd",))
+    shared_weights = gather(packed(widener, reducer), ("exp", "shd"))
 
     ids = expert_ids.reshape(seq, 2)
     every = jnp.arange(128, dtype=jnp.int32)[None, :]
@@ -785,67 +1154,46 @@
     bid_col = jnp.broadcast_to(bid.reshape(seq, 1), (seq, 256))
 
     lanes = -(-CAP // 128) * 128
-    g_slots = place_gradients(g, place_row, experts_all, CAP)
-    qkv, lse, o, mid, h2, probs, probst, g_landed = attention_forward(
-        tokens, bid_row, bid_col, gains, wa, wo, wr, wrt, g_slots
+    full, wr, g_slots = gather_first(mine, tiny, g, place_row, exps, shds, experts_all, CAP)
+    qkv, lse, o, mid, h2, probs, probst, gains, g_landed = attention_forward(
+        tokens, bid_row, bid_col, full, wr, g_slots
     )
     slot_rows, chosen = dispatch(h2, place_row, probst, experts_all, CAP, lanes)
-    eout, ein, sums = routed(slot_rows, chosen, g_landed, w_experts, w_narrower, shds)
-    sout, sin, dsg, dsu, dsn, swapped = ffn(h2, g, w_widener, w_reducer, sums, f32, 256, "shared")
-    part = (pick(sums, 0, core).astype(f32) + swapped.astype(f32)).astype(bf16)
+    eout, ein, own, swapped = routed(slot_rows, chosen, g_landed, expert_weights, hidden)
+    add = lambda a, b: (a.astype(f32) + b.astype(f32)).astype(bf16)
+    part = add(own, swapped)
+    part, h2_later = lax.optimization_barrier((part, h2))
     part = lax.psum_scatter(part, "shd", scatter_dimension=0, tiled=False)
-    block_out, mid_grad, midb, og, gain_two, rgrad = combine(
-        mid, sout, sin, g, h2, probs, place_col, eout, ein, gains, wr, wo
-    )
-    dqkv = attention_backward(qkv, og, lse, bid_row, bid_col)
-
-    x = tokens.astype(f32)
-    r1 = lax.rsqrt(jnp.mean(x * x, axis=1, keepdims=True) + norm_eps)
-    n1 = x * r1
-    h1 = (n1 * gains[0:1]).astype(bf16)
-    attend_grad = jnp.einsum("nd,tnf->tdf", h1, dqkv, preferred_element_type=f32)
-    output_grad = mm_tn(o, midb)
-    w_full = wa.transpose(2, 1, 3, 0, 4).reshape(3, width, width)
-    h1_grad = jnp.einsum("tnf,tdf->nd", dqkv, w_full, preferred_element_type=f32)
-    gain_one = jnp.sum(h1_grad * n1, axis=0)
-    d1 = h1_grad * gains[0:1]
-    input_grad = mid_grad + r1 * (d1 - n1 * jnp.mean(d1 * n1, axis=1, keepdims=True))
-
-    expert_sums = share(part, groups, core)
-    deep = width // shds
+    sout, sin, own_a, swapped_a, own_b, swapped_b = ffn(
+        h2_later, g, shared_weights, hidden, f32, 256, "shared"
+    )
+    part_a = add(own_a, swapped_a).reshape(exps, shds, rows, hidden)
+    part_b = add(own_b, swapped_b).reshape(exps, shds, tall, width)
+    block_out, mid_grad, midb, og, gain_two, rgrad, landed_b = combine(
+        mid, sout, sin, g, h2, probs, place_col, eout, ein, gains, wr, full, part_b
+    )
+    dqkv, landed_a = attention_backward(qkv, og, lse, bid_row, bid_col, part_a)
+    input_grad, sum_w, sum_a, sum_b, sum_t = finish(
+        dqkv, tokens, mid_grad, o, midb, full, gains, gain_two, rgrad, landed_a, landed_b
+    )
+    if groups > 2:
+        sum_w, sum_a, sum_b, sum_t = (
+            0.5 * lax.psum(v, "grp") for v in (sum_w, sum_a, sum_b, sum_t)
+        )
+    expert_sums = share(part, groups, core).astype(f32)
     cut_at = hidden // 256 * deep
     g_experts = expert_sums[:, :cut_at].reshape(2, hidden // 256, deep, 256)
     g_experts = g_experts.transpose(0, 2, 1, 3).reshape(2, deep, hidden)
     g_narrower = expert_sums[:, cut_at:].reshape(2, width // 256, -1, 256)
     g_narrower = g_narrower.transpose(0, 2, 1, 3)
-    small = jnp.concatenate(
-        [rgrad[:experts_all], gain_one[None, :], gain_two[0:1]], axis=0
-    ).reshape(-1, spread, rows).transpose(1, 0, 2).reshape(spread, 1, -1)
-    small = jnp.pad(small, ((0, 0), (0, 15), (0, width - small.shape[2])))
-    dense = jnp.concatenate(
-        [
-            attend_grad.astype(bf16).reshape(3, spread, rows, width).transpose(1, 0, 2, 3).reshape(spread, -1, width),
-            output_grad.astype(bf16).reshape(spread, rows, width),
-            jnp.concatenate([dsg, dsu], axis=0).reshape(2, spread, rows, hidden).transpose(1, 0, 2, 3).reshape(spread, -1, width),
-            dsn.reshape(spread, -1, width),
-            small.astype(bf16),
-        ],
-        axis=1,
-    )
-    total = dense.shape[1]
-    dense = dense.reshape(spread, 2, total // 2, width).transpose(1, 0, 2, 3)
-    dense = reduce_scatter(dense, both, groups, core).reshape(total, width)
-    sizes = (3 * rows, rows, 2 * rows * hidden // width, reducer.shape[0])
-    starts = (0, sizes[0], sizes[0] + sizes[1], sum(sizes[:3]))
-    cut = lambda i, shape: dense[starts[i] : starts[i] + sizes[i]].reshape(shape)
-    tiny = dense[sum(sizes)][: (experts_all + 2) * rows].reshape(experts_all + 2, rows)
+    sum_w = sum_w.reshape(4, rows, width)
     grads = (
-        tiny[experts_all:],
-        cut(0, attend.shape),
-        cut(1, output.shape),
-        tiny[:experts_all].T,
-        cut(2, widener.shape),
-        cut(3, reducer.shape),
+        sum_t[:, 4:6].T,
+        sum_w[:3],
+        sum_w[3],
+        sum_t[:, :experts_all],
+        sum_a,
+        sum_b.reshape(reducer.shape),
         g_experts.reshape(experts.shape),
         g_narrower.reshape(narrower.shape),
     )

time: 708 us -> 547 us (0.77)
  Pallas kernels: 302 us -> 435 us
  waiting for transfers between devices: 106 us -> 0.08 us
  blocking collectives: 88.9 us -> 0 us
  local copies, waits for them, and re-layouts: 109 us -> 45.6 us
  matrix products: 16.2 us -> 0.89 us
  other arithmetic: 56.9 us -> 43.8 us
    pallas_call x2 -> x3, Pallas kernels: 45.4 us -> 164 us  [the longest x1 75 us: finish(): pl.pallas_call(functools.partial(finish_kernel, exps, shds), grid=(1,), i...]
    all_gather x5 -> x2, waiting for transfers between devices: 100 us -> 0.02 us  [gather(): wide = lax.all_gather(part, ('grp',) + axes, axis=0, tiled=False)]
    all_to_all x1 -> x0, blocking collectives: 88.9 us -> none  [reduce_scatter(): part = lax.all_to_all(part, axis, 0, 0, tiled=True)]
    reshape x13 -> x1, local copies, waits for them, and re-layouts: 28.7 us -> 0.04 us  [packed(): a.reshape(a.shape[0], -1, 256).transpose(1, 0, 2).reshape(-1, 256)]
    dot_general x3 -> x0, matrix products: 15.3 us -> none  [the longest x1 8.02 us: on_device(): jnp.einsum('nd,tnf->tdf', h1, dqkv, preferred_element_type=f32)]
    slice x13 -> x1, local copies, waits for them, and re-layouts: 10.4 us -> 0.01 us  [on_device(): attend[2].astype(bf16)]
    pallas_call x1, Pallas kernels: 135 us -> 145 us  [routed(): pl.pallas_call(functools.partial(routed_kernel, exps, shds), in_specs=[AN...]
    unnamed x97 -> x88, local copies, waits for them, and re-layouts: 26.7 us -> 24.8 us
  transfers between devices with their start and end apart: 10 -> 4, of which waited for: 4 -> 0; matrix products, arithmetic and copies ran while one was open for 16% -> 9% of each run, Pallas kernels for 29% -> 80%
where the time goes in v3:
time: 547 us; the launch traced here: 540 us
  Pallas kernels  435 us (80%)
  local copies, waits for them, and re-layouts  45.6 us (8%)
  other arithmetic  43.8 us (8%)
  between operations  14.8 us (3%)
    pallas_call x1, Pallas kernels, routed(): pl.pallas_call(functools.partial(routed_kernel, exps, shds), in_specs=[AN...  145 us
    pallas_call x1, Pallas kernels, finish(): pl.pallas_call(functools.partial(finish_kernel, exps, shds), grid=(1,), i...  75 us
    pallas_call x1, Pallas kernels, gather_first(): pl.pallas_call(functools.partial(gather_kernel, exps, shds), in_specs=[AN...  49.1 us
    pallas_call x1, Pallas kernels, attention_forward(): pl.pallas_call(functools.partial(forward_kernel, exps), grid=(pairs,), in...  47.7 us
    pallas_call x1, Pallas kernels, attention_backward(): pl.pallas_call(backward_kernel, grid=(pairs,), in_specs=[pl.BlockSpec((3,...  40.4 us
    pallas_call x1, Pallas kernels, ffn(): pl.pallas_call(functools.partial(ffn_kernel, tile=tile), grid=(steps,), i...  39.7 us
    pallas_call x1, Pallas kernels, combine(): pl.pallas_call(combine_kernel, grid=(seq // tile,), in_specs=[by_rows, by...  27.4 us
    unnamed x88, local copies, waits for them, and re-layouts  24.8 us
  transfers between devices with their start and end apart: 4, of which 0 were waited for; matrix products, arithmetic and copies ran while one was open for 9% of the time, Pallas kernels for 80%

profile of v3, /device:TPU:0, one launch (start us, length us, event | category | flops | bytes accessed | tf_op | source)
XLA Modules:
  0.0 540.4 jit_solution(5624380399223101220)
XLA Ops:
  7.3 1.5 convert_element_type.64
  9.1 1.5 dynamic-slice_convert_fusion
  11.1 1.1 pad_maximum_fusion
  12.4 1.0 dynamic-slice_convert_fusion.1
  13.5 0.7 pad_maximum_fusion.1
  14.3 0.7 copy.235
  15.1 1.6 copy.242
  16.8 0.7 copy.227
  17.6 0.9 fusion.4.place_ref
  18.5 0.8 copy-done.17
  19.3 0.8 copy.215.place_ref
  20.1 0.7 copy.224
  20.8 0.7 copy.222
  21.5 0.7 copy.231
  22.3 0.7 copy.229
  23.0 1.6 copy.238
  24.6 3.2 copy.240
  29.1 49.1 %gather_first.1 = (bf16[4,768,768]{2,1,0:T(8,128)(2,1)}, bf16[768,128]{1,0:T(8,128)(2,1)}, bf16[4,576,768]{2,1,0:T(8,128)(2,1)}) custom-call(bf16[2,48,768]{2,1,0:T(8,128)(2,1)} %slice_select_fusion.mine_ref, bf16[48,128]{1,0:T(8,128)(2,1)} %pad.4.tiny_ref, bf16[1024,768]{1,0:T(8,128)(2,1)} %bitcast.105, s32[16,1024]{1,0:T(8,128)} %copy.215.place_ref), custom_call_target="tpu_custom_call" | custom-call | flops 40000000000 | bytes 10000000 | tf_op jit(solution)/shard_map/gather_first/pallas_call | solution.py:157
  78.8 1.2 broadcast_in_dim.29.bidc_ref
  80.0 47.7 %attention_forward.1 = (bf16[3,1024,768]{2,1,0:T(8,128)(2,1)}, f32[6,8,1024]{2,1,0:T(8,128)}, bf16[1024,768]{1,0:T(8,128)(2,1)}, f32[1024,768]{1,0:T(8,128)}, bf...) custom-call(bf16[1024,768]{1,0:T(8,128)(2,1)} %bitcast.108, ...), custom_call_target="tpu_custom_call" | custom-call | flops 30000001024 | bytes 20000000 | tf_op jit(solution)/shard_map/attention_forward/pallas_call | solution.py:274
  127.7 10.6 %dispatch.1 = (bf16[4,576,768]{2,1,0:T(8,128)(2,1)}, f32[4,8,640]{2,1,0:T(8,128)}) custom-call(bf16[1024,768]{1,0:T(8,128)(2,1)} %get-tuple-element.77.h2_ref.x_ref, s32[16,1024]{1,0:T(8,128)} %copy.215.place_ref, f32[16,1024]{1,0:T(8,128)} %get-tuple-element.71.probst_ref), custom_call_target="tpu_custom_call" | custom-call | flops 5000000000 | bytes 6000000 | tf_op jit(solution)/shard_map/dispatch/pallas_call | solution.py:345
  138.3 144.7 %routed.1 = (bf16[4,576,768]{2,1,0:T(8,128)(2,1)}, bf16[4,576,768]{2,1,0:T(8,128)(2,1)}, bf16[4,2304,256]{2,1,0:T(8,128)(2,1)}, bf16[4,2304,256]{2,1,0:T(8,128)(2,1)}) custom-call(bf16[4,576,768]{2,1,0:T(8,128)(2,1)} %get-tuple-element.72.rows_ref, f32[4,8,640]{2,1,0:T(8,128)} %get-tuple-element.73.chosen_ref, ...), custom_call_target="tpu_custom_call" | custom-call | flops 65229815808 | bytes 40000000 | tf_op jit(solution)/shard_map/routed/pallas_call | solution.py:517
  283.0 7.1 %add_convert_fusion = bf16[4,2304,256]{2,1,0:T(8,128)(2,1)} fusion(bf16[4,2304,256]{2,1,0:T(8,128)(2,1)} %get-tuple-element.76, bf16[4,2304,256]{2,1,0:T(8,128)(2,1)} %get-tuple-element.75), kind=kLoop, calls=%fused_computation | loop fusion | flops 9437184 | bytes 14155776 | tf_op jit(solution)/shard_map/convert_element_type | solution.py:1163
  290.1 39.7 %shared.1 = (f32[1024,768]{1,0:T(8,128)}, f32[1024,768]{1,0:T(8,128)}, bf16[768,2048]{1,0:T(8,128)(2,1)}, bf16[768,2048]{1,0:T(8,128)(2,1)}, bf16[16,64,768]{2,1,0:T(8,128)(2,1)}, /*index=5*/bf16[16,64,768]{2,1,0:T(8,128)(2,1)}) custom-call(bf16[1024,768]{1,0:T(8,128)(2,1)} %get-tuple-element.77.h2_ref.x_ref, bf16[1024,768]{1,0:T(8,128)(2,1)} %bitcast.106, ...), custom_call_target="tpu_custom_call" | custom-call | flops 28991029248 | bytes 25165824 | tf_op jit(solution)/shard_map/shared/pallas_call | solution.py:637
  329.9 3.5 add_convert_fusion.2
  333.4 27.4 %combine.1 = (bf16[1024,768]{1,0:T(8,128)(2,1)}, f32[1024,768]{1,0:T(8,128)}, bf16[1024,768]{1,0:T(8,128)(2,1)}, bf16[1024,768]{1,0:T(8,128)(2,1)}, f32[8,768]{1...) custom-call(f32[1024,768]{1,0:T(8,128)} %get-tuple-element.69.mid_ref, ...), custom_call_target="tpu_custom_call" | custom-call | flops 11000000512 | bytes 30000000 | tf_op jit(solution)/shard_map/combine/pallas_call | solution.py:768
  360.8 5.1 add_convert_fusion.1
  365.9 40.4 %attention_backward.1 = (bf16[3,1024,768]{2,1,0:T(8,128)(2,1)}, bf16[4,4,48,2048]{3,2,1,0:T(8,128)(2,1)}) custom-call(bf16[3,1024,768]{2,1,0:T(8,128)(2,1)} %get-tuple-element.87.qkv_ref, bf16[1024,768]{1,0:T(8,128)(2,1)} %get-tuple-element.88.og_ref, f32[6,8,1024]{2,1,0:T(8,128)} %get-tuple-element.89.lse_ref, s32[8,1024]{1,0:T(8,128)} %broadcast_in_dim.28.bidr_ref, ...), custom_call_target="tpu_custom_call" | custom-call | flops 35000000512 | bytes 12000000 | tf_op jit(solution)/shard_map/attention_backward/pallas_call | solution.py:859
  406.5 75.0 %finish.1 = (f32[1024,768]{1,0:T(8,128)}, f32[2,2,48,768]{3,2,1,0:T(8,128)}, f32[2,48,2048]{2,1,0:T(8,128)}, f32[2,64,768]{2,1,0:T(8,128)}, f32[48,128]{1,0:T(8,128)}) custom-call(bf16[3,1024,768]{2,1,0:T(8,128)(2,1)} %get-tuple-element.92.dqkv_ref, bf16[1024,768]{1,0:T(8,128)(2,1)} %bitcast.109, f32[1024,768]{1,0:T(8,128)} %get-tuple-element.93.midg_ref, ...), custom_call_target="tpu_custom_call" | custom-call | flops 60000002048 | bytes 30000000 | tf_op jit(solution)/shard_map/finish/pallas_call | solution.py:1043
  481.5 0.9 sqrt_add_fusion.1
  484.6 0.8 sqrt_add_fusion
  487.6 2.8 multiply_subtract_fusion.4
  490.5 2.5 multiply_subtract_fusion.3
  493.4 1.8 multiply_subtract_fusion.5
  495.2 3.0 multiply_subtract_fusion.2
  498.9 1.3 slice.54
  500.1 1.8 copy.237
  502.0 2.3 reshape_reshape.3
  504.2 2.7 copy.239
  506.9 2.4 reshape.227
  509.4 5.2 multiply_subtract_fusion.1
  514.5 1.6 copy.249
  516.1 3.2 copy.250
  519.3 3.0 copy.251
  522.3 6.9 %multiply_subtract_fusion = (f32[1,2,192,2048]{3,2,1,0:T(8,128)}, f32[1,2,192,2048]{3,2,1,0:T(8,128)}, f32[1,2,192,2048]{3,2,1,0:T(8,128)}) fusion(f32[1,2,192,2048]{3,2,1,0:T(8,128)} %param.50, f32[1,2,192,2048]{3,2,1,0:T(8,128)S(1)} %copy-done, f32[1,2,192,2048]{3,2,1,0:T(8,128)} %param.51, f32[1,2,192,2048]{3,2,1,0:T(8,128)} %param.52), kind=kLoop, calls=%fused_computation.6 | loop fusion | flops 11796480 | bytes 22020096 | tf_op jit(solution)/shard_map/sub | solution.py:1089
  529.3 1.1 copy.259
  530.4 1.3 copy-done.3
  531.8 1.7 copy.260
  (126 shorter events, 8.8 us)
Async XLA Ops:
  7.2 131.1 %all-gather.5.cloned.1.call-start = ((), (), s32[]{:S(2)}) async-start(), calls=%async_computation.2 | async-start | bytes 10616832 | tf_op jit(solution)/shard_map/all_gather | solution.py:1131
  10.7 1.6 copy-start.9
  11.0 3.3 copy-start.25
  11.0 4.0 copy-start.1
  12.2 4.5 copy-start.5
  12.2 277.9 %all-gather.7.cloned.1.call-start = ((), (), s32[]{:S(2)}) async-start(), calls=%async_computation.3 | async-start | bytes 9732096 | tf_op jit(solution)/shard_map/all_gather | solution.py:1131
  12.4 4.4 copy-start.29
  12.4 5.2 copy-start.28
  14.3 478.7 %reduce-scatter.2.cloned.1.call-start = ((), (), s32[]{:S(2)}) async-start(), calls=%async_computation.1 | async-start | bytes 5898240 | tf_op jit(solution)/shard_map/reduce_scatter | solution.py:1166
  16.7 3.5 copy-start.33
  16.7 4.2 copy-start.34
  16.7 4.9 copy-start.31
  16.7 5.6 %copy-start.32 = (f32[48,4]{0,1:T(4,128)S(1)}, f32[48,4]{0,1:T(4,128)}, u32[]{:S(2)}) copy-start(f32[48,4]{0,1:T(4,128)} %param.42) | copy-start | bytes 2308
  16.7 6.2 %copy-start.7 = (f32[1,512,768]{2,1,0:T(8,128)S(1)}, f32[1,512,768]{2,1,0:T(8,128)}, u32[]{:S(2)}) copy-start(f32[1,512,768]{2,1,0:T(8,128)} %param.54) | copy-start | bytes 4718596
  18.5 0.8 copy-start.17
  23.0 5.4 copy-start.15
  29.1 49.1 %copy-start.27 = (s32[1,1024]{1,0:T(1,128)S(1)}, s32[1,1024]{1,0:T(1,128)}, u32[]{:S(2)}) copy-start(s32[1,1024]{1,0:T(1,128)} %param.30) | copy-start | bytes 12292
  333.4 27.4 %copy-start.4 = (bf16[768,2048]{1,0:T(8,128)(2,1)S(1)}, bf16[768,2048]{1,0:T(8,128)(2,1)}, u32[]{:S(2)}) copy-start(bf16[768,2048]{1,0:T(8,128)(2,1)} %get-tuple-element.90) | copy-start | bytes 9437188
  406.4 75.1 %copy-start.21 = (f32[2,48]{0,1:T(8,128)S(1)}, f32[2,48]{0,1:T(8,128)}, u32[]{:S(2)}) copy-start(f32[2,48]{0,1:T(8,128)} %copy.224) | copy-start | bytes 1156
  406.4 75.1 %copy-start.22 = (f32[2,48]{0,1:T(8,128)S(1)}, f32[2,48]{0,1:T(8,128)}, u32[]{:S(2)}) copy-start(f32[2,48]{0,1:T(8,128)} %copy.222) | copy-start | bytes 1156
  406.4 76.2 %copy-start.30 = (f32[2,48]{1,0:T(2,128)S(1)}, f32[2,48]{1,0:T(2,128)}, u32[]{:S(2)}) copy-start(f32[2,48]{1,0:T(2,128)} %param.32) | copy-start | bytes 1156
  406.4 76.3 %copy-start.19 = (f32[2,48]{0,1:T(8,128)S(1)}, f32[2,48]{0,1:T(8,128)}, u32[]{:S(2)}) copy-start(f32[2,48]{0,1:T(8,128)} %copy.227) | copy-start | bytes 1156
  406.4 78.2 %copy-start.23 = (f32[48,4]{1,0:T(8,128)S(1)}, f32[48,4]{1,0:T(8,128)}, u32[]{:S(2)}) copy-start(f32[48,4]{1,0:T(8,128)} %copy.231) | copy-start | bytes 2308
  406.5 78.2 %copy-start.24 = (f32[48,4]{1,0:T(8,128)S(1)}, f32[48,4]{1,0:T(8,128)}, u32[]{:S(2)}) copy-start(f32[48,4]{1,0:T(8,128)} %copy.229) | copy-start | bytes 2308
  406.5 79.1 %copy-start.26 = (f32[48,4]{0,1:T(4,128)S(1)}, f32[48,4]{0,1:T(4,128)}, u32[]{:S(2)}) copy-start(f32[48,4]{0,1:T(4,128)} %param.41) | copy-start | bytes 2308
  406.5 79.2 %copy-start.20 = (f32[48,4]{1,0:T(8,128)S(1)}, f32[48,4]{1,0:T(8,128)}, u32[]{:S(2)}) copy-start(f32[48,4]{1,0:T(8,128)} %copy.235) | copy-start | bytes 2308
  406.5 81.1 %copy-start.10 = (f32[128,768]{1,0:T(8,128)S(1)}, f32[128,768]{1,0:T(8,128)}, u32[]{:S(2)}) copy-start(f32[128,768]{1,0:T(8,128)} %param.47) | copy-start | bytes 1179652
  481.5 8.9 %copy-start.6 = (f32[3,48,768]{2,1,0:T(8,128)S(1)}, f32[3,48,768]{2,1,0:T(8,128)}, u32[]{:S(2)}) copy-start(f32[3,48,768]{2,1,0:T(8,128)} %param.35) | copy-start | bytes 1327108
  484.0 9.4 %copy-start.16 = (f32[48,768]{1,0:T(8,128)S(1)}, f32[48,768]{1,0:T(8,128)}, u32[]{:S(2)}) copy-start(f32[48,768]{1,0:T(8,128)} %param.38) | copy-start | bytes 442372
  484.0 9.4 %copy-start.18 = (f32[48,768]{1,0:T(8,128)S(1)}, f32[48,768]{1,0:T(8,128)}, u32[]{:S(2)}) copy-start(f32[48,768]{1,0:T(8,128)} %param.39) | copy-start | bytes 442372
  487.6 7.5 %copy-start.11 = (f32[2,48,2048]{2,1,0:T(8,128)S(1)}, f32[2,48,2048]{2,1,0:T(8,128)}, u32[]{:S(2)}) copy-start(f32[2,48,2048]{2,1,0:T(8,128)} %param.44) | copy-start | bytes 2359300
  487.6 7.6 %copy-start.13 = (f32[2,48,2048]{2,1,0:T(8,128)S(1)}, f32[2,48,2048]{2,1,0:T(8,128)}, u32[]{:S(2)}) copy-start(f32[2,48,2048]{2,1,0:T(8,128)} %param.45) | copy-start | bytes 2359300
  487.6 7.6 %copy-start.14 = (f32[2,48,2048]{2,1,0:T(8,128)S(1)}, f32[2,48,2048]{2,1,0:T(8,128)}, u32[]{:S(2)}) copy-start(f32[2,48,2048]{2,1,0:T(8,128)} %param.46) | copy-start | bytes 2359300
  493.0 5.5 %collective-permute-start = (bf16[2304,256]{1,0:T(8,128)(2,1)}, bf16[2304,256]{1,0:T(8,128)(2,1)S(1)}, u32[]{:S(2)}, u32[]{:S(2)}) collective-permute-start(bf16[2304,256]{1,0:T(8,128)(2,1)} %bitcast.87), channel_id=1, source_target_pairs={{0,16},{16,0},{1,17},{17,1},{2,18},{18,2},{3,19},{19,3},{4,20},{20... | collective-permute-start | bytes 3538952 | tf_op jit(solution)/shard_map/ppermute | solution.py:1102
  495.2 3.2 copy-start.12
  504.2 5.1 copy-start.2
  516.1 6.2 %copy-start = (f32[1,2,192,2048]{3,2,1,0:T(8,128)S(1)}, f32[1,2,192,2048]{3,2,1,0:T(8,128)}, u32[]{:S(2)}) copy-start(f32[1,2,192,2048]{3,2,1,0:T(8,128)} %reshape_reshape.3) | copy-start | bytes 9437188
  522.3 7.0 %copy-start.8 = (bf16[1024,768]{1,0:T(8,128)(2,1)S(1)}, bf16[1024,768]{1,0:T(8,128)(2,1)}, u32[]{:S(2)}) copy-start(bf16[1024,768]{1,0:T(8,128)(2,1)} %get-tuple-element.86) | copy-start | bytes 4718596
  529.3 2.5 copy-start.3
Sparse Core Ops, SparseCore 0:
  12.3 106.9 all-gather.4
  122.7 106.5 all-gather.6
  290.2 86.5 reduce-scatter.1
